TPU v7x, 1024 devices: a whole 4x4x32 slice. The times are simulated.
1024 devices in a mesh: section: 16 (over x, y), expert: 64 (over z, core).
Axes of the slice: x: 4, y: 4, z: 32, core: 2. Of those that a mesh axis runs over, the one named last changes fastest.
Arguments:
- tokens: bfloat16 [16, 2048, 2048], P('section', 'expert'), may hold values from -6 to 6
- norm_gain: float32 [2048], replicated, may hold values from 0.1 to 1.9
- route_ids: int32 [16, 2048, 8], P('section', 'expert'), may hold values from 0 to 63, all different within a row; in each aligned block of 32 rows (0 to 31, 32 to 63, ..., all dimensions but the last counted through in order) at most 6 rows name the same one
- route_weight: float32 [16, 2048, 8], P('section', 'expert'), may hold values from 0.05 to 1
- gate_up: bfloat16 [64, 2048, 1536], P('expert'), may hold values from -0.125 to 0.125
- down: bfloat16 [64, 768, 2048], P('expert'), may hold values from -0.21875 to 0.21875
Outputs:
- next_rows: bfloat16 [16, 2048, 2048], P('section', 'expert')
Inputs may be any that keep to these rules, and one draw needn't show every extreme that they name: `route_ids`: each row names 8 different experts. In each aligned block of 32 rows of a section (the rows of one device), no expert is named by more than 6 entries.
All inputs are finite; a program needn't handle non-finite values.
Results may differ from a plain program's by a relative error of at most 0.0039.
Values may be sent and summed in bfloat16 or wider, within the bound.
No kernel may reach another device: no remote copies, remote signals or barrier semaphores. Data moves between devices by JAX's collectives and lax.ppermute only.
A program may use at most 32 MiB of HBM per device.

v0:
```python
import jax
import jax.numpy as jnp
from jax import lax
from jax.sharding import PartitionSpec as P

EXPERTS = 64
CAP = 6


def from_behind(value, axis, steps):
    count = lax.axis_size(axis)
    pairs = [(source, (source + steps) % count) for source in range(count)]
    return lax.ppermute(value, axis, pairs)


def body(tokens, norm_gain, route_ids, route_weight, gate_up, down):
    hp = lax.Precision.HIGHEST
    rows = tokens[0]
    ids = route_ids[0]
    weights = route_weight[0]
    tok_rows, width = rows.shape
    top_count = ids.shape[1]
    hidden_width = down.shape[1]
    slots = EXPERTS * CAP
    values = rows.astype(jnp.float32)
    scale = lax.rsqrt(jnp.mean(values * values, axis=1, keepdims=True) + 1e-06)
    normed = (values * scale * norm_gain[None, :]).astype(jnp.bfloat16)
    share = weights / jnp.sum(weights, axis=1, keepdims=True)
    flat = ids.reshape(-1)
    onehot = (flat[:, None] == jnp.arange(EXPERTS, dtype=jnp.int32)[None, :]).astype(jnp.int32)
    rank = jnp.sum((jnp.cumsum(onehot, axis=0) - onehot) * onehot, axis=1)
    slot = flat * CAP + rank
    select = (slot[:, None] == jnp.arange(slots, dtype=jnp.int32)[None, :]).astype(jnp.float32)
    select = select.reshape(tok_rows, top_count, slots)
    place = jnp.sum(select, axis=1).astype(jnp.bfloat16)
    weighted = jnp.sum(select * share[:, :, None], axis=1)
    sent = jnp.einsum("ts,td->sd", place, normed, preferred_element_type=jnp.float32)
    sent = sent.astype(jnp.bfloat16).reshape(EXPERTS, CAP, width)
    received = lax.all_to_all(sent, "expert", split_axis=0, concat_axis=0, tiled=True)
    owners = lax.axis_size("expert")
    local = EXPERTS // owners
    blocks = received.reshape(owners, local, received.shape[1], width)
    gated = jnp.einsum("nlcd,ldf->nlcf", blocks, gate_up, preferred_element_type=jnp.float32)
    hidden = (jax.nn.silu(gated[..., :hidden_width]) * gated[..., hidden_width:]).astype(
        jnp.bfloat16
    )
    answer = jnp.einsum("nlcf,lfd->nlcd", hidden, down, preferred_element_type=jnp.float32)
    back = lax.all_to_all(
        answer.astype(jnp.bfloat16).reshape(EXPERTS, received.shape[1], width),
        "expert",
        split_axis=0,
        concat_axis=0,
        tiled=True,
    )
    flat_back = back.reshape(slots, width).astype(jnp.float32)
    branch = jnp.dot(weighted, flat_back, precision=hp)
    result = (values + branch).astype(jnp.bfloat16)
    moved = from_behind(result, "section", 1)
    return moved[None]


def solution(mesh):
    placed = (
        P("section", "expert", None),
        P(),
        P("section", "expert", None),
        P("section", "expert", None),
        P("expert", None, None),
        P("expert", None, None),
    )
    return jax.shard_map(
        body, mesh=mesh, in_specs=placed, out_specs=P("section", "expert", None), check_vma=False
    )
```

profile of v0, /device:TPU:6, one launch (start us, length us, event | category | flops | bytes accessed | tf_op | source)
XLA Modules:
  0.0 472.6 jit_solution(13023439166470854220)
XLA Ops:
  0.0 0.0 copy-start
  0.0 0.9 copy.24
  0.9 0.1 eq.43
  1.0 0.1 eq.39
  1.1 1.0 fusion.15
  2.1 0.7 reduce_sum.49
  2.9 0.7 bitcast_divide_fusion
  3.5 0.1 copy.28
  3.6 0.6 reduce-window.6
  4.3 0.2 slice_reduce_fusion
  4.5 0.1 fusion.24
  4.6 0.1 reduce_sum.48
  4.7 0.3 convert_reduce_fusion
  5.0 2.7 convolution_convert_fusion
  7.7 3.7 reshape.91
  11.4 229.9 %all_to_all.10 = bf16[64,6,2048]{2,1,0:T(8,128)(2,1)S(1)} all-to-all(bf16[64,6,2048]{2,1,0:T(8,128)(2,1)} %reshape.91), channel_id=1, replica_groups=mesh['section'=16,'expert'=64] {'expert'}, dimensions={0} | all-to-all | bytes 3145728 | tf_op jit(solution)/shard_map/all_to_all | solution.py:39
  241.3 8.2 %fusion.4 = f32[64,1,6,1536]{3,0,2,1:T(8,128)S(1)} fusion(bf16[1,2048,1536]{2,1,0:T(8,128)(2,1)} %param.10, bf16[64,6,2048]{2,1,0:T(8,128)(2,1)S(1)} %all_to_all.10), kind=kOutput, calls=%fused_computation.4 | convolution fusion | flops 2415919104 | bytes 10223616 | tf_op jit(solution)/shard_map/nlcd,ldf->nlcf/dot_general | solution.py:43
  249.5 0.0 copy-done
  249.6 1.4 fusion.7
  251.0 0.9 copy.30
  251.9 205.1 %all_to_all.11 = bf16[64,6,2048]{2,1,0:T(8,128)(2,1)} all-to-all(bf16[64,6,2048]{2,1,0:T(8,128)(2,1)S(1)} %copy.30), channel_id=1, replica_groups=mesh['section'=16,'expert'=64] {'expert'}, dimensions={0} | all-to-all | bytes 3145728 | tf_op jit(solution)/shard_map/all_to_all | solution.py:48
  457.0 0.0 copy-start.1
  457.0 3.7 reshape.95
  460.7 0.0 copy-done.1
  460.8 2.3 fusion.10
  463.0 3.5 collective-permute-start
  466.5 5.5 %collective-permute-done = bf16[32,2048]{1,0:T(8,128)(2,1)S(1)} collective-permute-done((bf16[32,2048]{1,0:T(8,128)(2,1)S(1)}, bf16[32,2048]{1,0:T(8,128)(2,1)S(1)}, u32[]{:S(2)}, u32[]{:S(2)}) %collective-permute-start) | collective-permute-done | bytes 131104 | tf_op jit(solution)/shard_map/ppermute | solution.py:13
  472.0 0.7 copy.36
  (5 shorter events, 0.1 us)
Async XLA Ops:
  0.0 249.5 %copy-start = (bf16[1,768,2048]{2,1,0:T(8,128)(2,1)S(1)}, bf16[1,768,2048]{2,1,0:T(8,128)(2,1)}, u32[]{:S(2)}) copy-start(bf16[1,768,2048]{2,1,0:T(8,128)(2,1)} %param.11) | copy-start | bytes 9437188
  457.0 3.7 copy-start.1
  463.0 9.0 %collective-permute-start = (bf16[32,2048]{1,0:T(8,128)(2,1)S(1)}, bf16[32,2048]{1,0:T(8,128)(2,1)S(1)}, u32[]{:S(2)}, u32[]{:S(2)}) collective-permute-start(bf16[32,2048]{1,0:T(8,128)(2,1)S(1)} %fusion.10), channel_id=1, source_target_pairs={{0,64},{64,128},{128,192},{192,256},{256,320},{320,384},{384,448},... | collective-permute-start | bytes 393224 | tf_op jit(solution)/shard_map/ppermute | solution.py:13
where the time goes:
time: 473 us
  blocking collectives  435 us (92%)
  matrix products  14.6 us (3%)
  local copies, waits for them, and re-layouts  10.4 us (2%)
  waiting for transfers between devices  5.47 us (1%)
    all_to_all x1, blocking collectives, body(): lax.all_to_all(sent, 'expert', split_axis=0, concat_axis=0, tiled=True)  230 us
    all_to_all x1, blocking collectives, body(): lax.all_to_all(answer.astype(jnp.bfloat16).reshape(EXPERTS, received.shap...  205 us
  transfers between devices with their start and end apart: 1, of which 1 were waited for; matrix products, arithmetic and copies ran while one was open for 0% of the time, Pallas kernels for 0%

commit v1 on v0

v1 whole, which is shorter than its diff:
```python
import jax
import jax.numpy as jnp
from jax import lax
from jax.experimental import pallas as pl
from jax.experimental.pallas import tpu as pltpu
from jax.sharding import PartitionSpec as P

CAP = 6
ROWS = 32
INFO = 128
FAR = 4
BLOCKS = 8
SEG = BLOCKS * CAP
SLOTS = 8 * SEG
TILES = 3
VMEM = 56 * 2**20


def send(value, up, down, other=False, onward=0):
    count = lax.axis_size("expert")

    def place(i):
        chip, core = i // 2, i % 2
        if other:
            core = 1 - core
        return ((chip + (up if i % 2 == 0 else down)) * 2) % count + core

    if not onward:
        return lax.ppermute(value, "expert", [(i, place(i)) for i in range(count)])
    sections = lax.axis_size("section")
    pairs = [
        (s * count + i, (s + onward) % sections * count + place(i))
        for s in range(sections)
        for i in range(count)
    ]
    return lax.ppermute(value, ("section", "expert"), pairs)


def dispatch_kernel(expert_ref, *refs):
    blocks = refs[:BLOCKS]
    here, up1, down1, up2, down2, hi_ref, lo_ref = refs[BLOCKS:]
    width = here.shape[1]
    rows = BLOCKS * ROWS
    info = jnp.concatenate([b[:, width:] for b in blocks], axis=0).astype(jnp.float32)
    expert = expert_ref[0:1, :]
    member = jnp.zeros((rows, SLOTS), jnp.float32)
    hi = jnp.zeros((rows, SLOTS), jnp.float32)
    lo = jnp.zeros((rows, SLOTS), jnp.float32)
    for k in range(8):
        same = info[:, k : k + 1] == expert
        member = jnp.where(same, 1.0, member)
        hi = jnp.where(same, info[:, 8 + k : 9 + k], hi)
        lo = jnp.where(same, info[:, 16 + k : 17 + k], lo)
    r = lax.broadcasted_iota(jnp.int32, (rows, rows), 0)
    c = lax.broadcasted_iota(jnp.int32, (rows, rows), 1)
    before = jnp.where((c < r) & (c // ROWS == r // ROWS), 1.0, 0.0).astype(jnp.bfloat16)
    rank = jnp.dot(before, member.astype(jnp.bfloat16), preferred_element_type=jnp.float32)
    row_block = lax.broadcasted_iota(jnp.int32, (rows, SLOTS), 0) // ROWS
    q = lax.broadcasted_iota(jnp.int32, (rows, SLOTS), 1) % SEG
    taken = (member > 0.5) & (rank == (q % CAP).astype(jnp.float32)) & (q // CAP == row_block)
    hi_ref[...] = jnp.where(taken, hi, 0.0).astype(jnp.bfloat16)
    lo_ref[...] = jnp.where(taken, lo, 0.0).astype(jnp.bfloat16)
    pick = jnp.where(taken, 1.0, 0.0).astype(jnp.bfloat16)
    step = min(512, width)
    for at in range(0, width, step):
        cols = slice(at, at + step)
        x = jnp.concatenate([b[:, cols] for b in blocks], axis=0)
        y = lax.dot_general(pick, x, (((0,), (0,)), ((), ())), preferred_element_type=jnp.float32)
        y = y.astype(jnp.bfloat16)
        first = 0
        for out in (here, up1, down1, up2, down2):
            out[:, cols] = y[first : first + out.shape[0]]
            first += out.shape[0]


def dispatch(expert, blocks, width):
    rows = BLOCKS * ROWS

    def shape(n, w=width):
        return jax.ShapeDtypeStruct((n, w), jnp.bfloat16)

    return pl.pallas_call(
        dispatch_kernel,
        out_shape=(
            shape(2 * SEG), shape(2 * SEG), shape(2 * SEG), shape(SEG), shape(SEG),
            shape(rows, SLOTS), shape(rows, SLOTS),
        ),
        compiler_params=pltpu.CompilerParams(vmem_limit_bytes=VMEM),
        cost_estimate=pl.CostEstimate(
            flops=2 * rows * SLOTS * (width + rows), bytes_accessed=4 * 2**20, transcendentals=0
        ),
        name="dispatch",
    )(expert, *blocks)


def expert_kernel(core_ref, here, below, above, first2, second2, g0, u0, d0, g1, u1, d1,
                  here_o, below_o, above_o, first2_o, second2_o, x, acc):
    i = pl.program_id(0)
    turn, tile = i // TILES, i % TILES
    which = jnp.where(turn == 0, core_ref[0], 1 - core_ref[0])

    for e in range(2):
        @pl.when((tile == 0) & (which == e))
        def _():
            part = slice(e * SEG, (e + 1) * SEG)
            x[0:SEG] = here[part]
            x[SEG : 2 * SEG] = below[part]
            x[2 * SEG : 3 * SEG] = above[part]
            x[3 * SEG : 4 * SEG] = (first2, second2)[e][...]

    def work(g, u, d):
        gate = jnp.dot(x[...], g[0], preferred_element_type=jnp.float32)
        lift = jnp.dot(x[...], u[0], preferred_element_type=jnp.float32)
        hidden = (gate / (1.0 + jnp.exp(-gate)) * lift).astype(jnp.bfloat16)
        y = jnp.dot(hidden, d[0], preferred_element_type=jnp.float32)

        @pl.when(tile == 0)
        def _():
            acc[...] = y

        @pl.when(tile > 0)
        def _():
            acc[...] += y

    @pl.when(turn == 0)
    def _():
        work(g0, u0, d0)

    @pl.when(turn == 1)
    def _():
        work(g1, u1, d1)

    for e in range(2):
        @pl.when((tile == TILES - 1) & (which == e))
        def _():
            part = slice(e * SEG, (e + 1) * SEG)
            here_o[part] = acc[0:SEG].astype(jnp.bfloat16)
            below_o[part] = acc[SEG : 2 * SEG].astype(jnp.bfloat16)
            above_o[part] = acc[2 * SEG : 3 * SEG].astype(jnp.bfloat16)
            (first2_o, second2_o)[e][...] = acc[3 * SEG : 4 * SEG].astype(jnp.bfloat16)


def experts(core, pieces, own_gu, own_d, other_gu, other_d):
    width, hid = own_gu.shape[1], own_d.shape[1]
    tile = hid // TILES
    whole = [pl.BlockSpec(p.shape, lambda i, c: (0, 0)) for p in pieces]

    def early(i):
        return jnp.minimum(i, TILES - 1)

    def late(i):
        return jnp.maximum(i - TILES, 0)

    def weights(at):
        return [
            pl.BlockSpec((1, width, tile), lambda i, c: (0, 0, at(i))),
            pl.BlockSpec((1, width, tile), lambda i, c: (0, 0, at(i) + TILES)),
            pl.BlockSpec((1, tile, width), lambda i, c: (0, at(i), 0)),
        ]

    return pl.pallas_call(
        expert_kernel,
        grid_spec=pltpu.PrefetchScalarGridSpec(
            num_scalar_prefetch=1,
            grid=(2 * TILES,),
            in_specs=whole + weights(early) + weights(late),
            out_specs=whole,
            scratch_shapes=[
                pltpu.VMEM((4 * SEG, width), jnp.bfloat16),
                pltpu.VMEM((4 * SEG, width), jnp.float32),
            ],
        ),
        out_shape=[jax.ShapeDtypeStruct(p.shape, jnp.bfloat16) for p in pieces],
        compiler_params=pltpu.CompilerParams(vmem_limit_bytes=VMEM),
        cost_estimate=pl.CostEstimate(
            flops=2 * 8 * SEG * 3 * width * hid,
            bytes_accessed=2 * 3 * 2 * width * hid,
            transcendentals=8 * SEG * hid,
        ),
        name="experts",
    )(core, *pieces, own_gu, own_gu, own_d, other_gu, other_gu, other_d)


def combine_kernel(hi, lo, tokens, *refs):
    answers, outs = refs[:5], refs[5:]
    width = tokens.shape[1]
    step = min(512, width)
    for at in range(0, width, step):
        cols = slice(at, at + step)
        a = jnp.concatenate([r[:, cols] for r in answers], axis=0)
        y = jnp.dot(hi[...], a, preferred_element_type=jnp.float32)
        y = y + jnp.dot(lo[...], a, preferred_element_type=jnp.float32)
        outs[0][:, cols] = y[:ROWS] + tokens[:, cols].astype(jnp.float32)
        for b in range(1, BLOCKS):
            outs[b][:, cols] = y[b * ROWS : (b + 1) * ROWS].astype(jnp.bfloat16)


def combine(hi, lo, tokens, answers):
    shapes = [jax.ShapeDtypeStruct(tokens.shape, jnp.float32)]
    shapes += [jax.ShapeDtypeStruct(tokens.shape, jnp.bfloat16)] * (BLOCKS - 1)
    return pl.pallas_call(
        combine_kernel,
        out_shape=shapes,
        compiler_params=pltpu.CompilerParams(vmem_limit_bytes=VMEM),
        cost_estimate=pl.CostEstimate(
            flops=4 * BLOCKS * ROWS * SLOTS * tokens.shape[1], bytes_accessed=4 * 2**20, transcendentals=0
        ),
        name="combine",
    )(hi, lo, tokens, *answers)


def add(a, b):
    return (a.astype(jnp.float32) + b.astype(jnp.float32)).astype(jnp.bfloat16)


def body(tokens, norm_gain, route_ids, route_weight, gate_up, down):
    rows, ids, weights = tokens[0], route_ids[0], route_weight[0]
    width = rows.shape[1]
    count = lax.axis_size("expert")
    place = lax.axis_index("expert")
    chip, core = place // 2, place % 2

    other_gu = send(gate_up, 0, 0, other=True)
    other_d = send(down, 0, 0, other=True)

    values = rows.astype(jnp.float32)
    scale = lax.rsqrt(jnp.mean(values * values, axis=1, keepdims=True) + 1e-06)
    normed = (values * scale * norm_gain[None, :]).astype(jnp.bfloat16)
    share = weights / jnp.sum(weights, axis=1, keepdims=True)
    hi = lax.reduce_precision(share, 8, 7)
    lo = share - hi
    info = jnp.concatenate([ids.astype(jnp.float32), hi, lo], axis=1).astype(jnp.bfloat16)
    info = jnp.pad(info, ((0, 0), (0, INFO - info.shape[1])))
    p = [jnp.concatenate([normed, info], axis=1)]
    p.append(send(p[0], FAR, -FAR))
    q = [send(p[0], -FAR, FAR, other=True)]
    for _ in range(2):
        p.append(send(p[-1], FAR, -FAR))
        q.append(send(q[-1], FAR, -FAR))
    p.append(send(p[-1], FAR, -FAR))

    offsets = jnp.array([0, 1, 2, 3, -2, -1, 4, -3], jnp.int32)
    expert = (2 * chip + offsets) % count
    expert = jnp.broadcast_to(expert.astype(jnp.float32)[None, :, None], (8, 8, SEG)).reshape(8, SLOTS)
    here, up1, down1, up2, down2, hi, lo = dispatch(expert, p + q, width)
    below = send(up1, 1, 1)
    above = send(down1, -1, -1)
    first2 = send(up2, 2, 2)
    second2 = send(down2, -2, -2)
    here, below, above, first2, second2 = experts(
        core.reshape(1), [here, below, above, first2, second2], gate_up, down, other_gu, other_d
    )
    up1 = send(below, -1, -1)
    down1 = send(above, 1, 1)
    up2 = send(first2, -2, -2)
    down2 = send(second2, 2, 2)
    base, p1, p2, p3, p4, q1, q2, q3 = combine(hi, lo, rows, [here, up1, down1, up2, down2])
    base = send(base, 0, 0, onward=1)
    a = add(p3, send(p4, -FAR, FAR))
    b = add(q2, send(q3, -FAR, FAR))
    a = add(p2, send(a, -FAR, FAR))
    b = add(q1, send(b, -FAR, FAR))
    a = add(p1, send(a, -FAR, FAR))
    b = send(b, -FAR, FAR, other=True, onward=1)
    a = send(a, -FAR, FAR, onward=1)
    out = base + a.astype(jnp.float32) + b.astype(jnp.float32)
    return out.astype(jnp.bfloat16)[None]


def solution(mesh):
    placed = (
        P("section", "expert", None),
        P(),
        P("section", "expert", None),
        P("section", "expert", None),
        P("expert", None, None),
        P("expert", None, None),
    )
    return jax.shard_map(
        body, mesh=mesh, in_specs=placed, out_specs=P("section", "expert", None), check_vma=False
    )
```

time: 473 us -> 226 us (0.48)
  blocking collectives: 435 us -> 0 us
  starting transfers between devices: 3.5 us -> 130 us
  waiting for transfers between devices: 5.47 us -> 57.8 us
  Pallas kernels: 0 us -> 21 us
  matrix products: 14.6 us -> 0 us
  other arithmetic: 3.54 us -> 9.71 us
  local copies, waits for them, and re-layouts: 10.4 us -> 4.39 us
    all_to_all x2 -> x0, blocking collectives: 435 us -> none  [the longest x1 230 us: body(): lax.all_to_all(sent, 'expert', split_axis=0, concat_axis=0, tiled=True)]
    ppermute x1 -> x25, starting transfers between devices: 3.5 us -> 130 us  [the longest x22 115 us: send(): return lax.ppermute(value, 'expert', [(i, place(i)) for i in range(count)])]
    ppermute x1 -> x25, waiting for transfers between devices: 5.47 us -> 57.8 us  [the longest x22 48.9 us: send(): return lax.ppermute(value, 'expert', [(i, place(i)) for i in range(count)])]
    pallas_call x0 -> x3, Pallas kernels: none -> 21 us  [the longest x1 13.3 us: experts(): pl.pallas_call(expert_kernel, grid_spec=pltpu.PrefetchScalarGridSpec(num_...]
    dot_general x4 -> x0, matrix products: 14.6 us -> none  [the longest x1 8.21 us: body(): jnp.einsum('nlcd,ldf->nlcf', blocks, gate_up, preferred_element_type=jnp....]
    reshape x2 -> x0, local copies, waits for them, and re-layouts: 7.45 us -> none  [the longest x1 3.74 us: body(): flat_back = back.reshape(slots, width).astype(jnp.float32)]
    convert_element_type x1 -> x8, other arithmetic: 0.01 us -> 7.09 us  [the longest x5 4.7 us: add(): return (a.astype(jnp.float32) + b.astype(jnp.float32)).astype(jnp.bfloat16)]
  transfers between devices with their start and end apart: 1 -> 25, of which waited for: 1 -> 11; matrix products, arithmetic and copies ran while one was open for 0% -> 5% of each run, Pallas kernels for 0% -> 2%
where the time goes in v1:
time: 226 us; the launch traced here: 223 us
  starting transfers between devices  130 us (58%)
  waiting for transfers between devices  57.8 us (26%)
  Pallas kernels  21 us (9%)
  other arithmetic  9.71 us (4%)
  local copies, waits for them, and re-layouts  4.39 us (2%)
    ppermute x22, starting transfers between devices, send(): return lax.ppermute(value, 'expert', [(i, place(i)) for i in range(count)])  115 us
    ppermute x22, waiting for transfers between devices, send(): return lax.ppermute(value, 'expert', [(i, place(i)) for i in range(count)])  48.9 us
    ppermute x3, starting transfers between devices, send(): return lax.ppermute(value, ('section', 'expert'), pairs)  15.6 us
    pallas_call x1, Pallas kernels, experts(): pl.pallas_call(expert_kernel, grid_spec=pltpu.PrefetchScalarGridSpec(num_...  13.3 us
    ppermute x3, waiting for transfers between devices, send(): return lax.ppermute(value, ('section', 'expert'), pairs)  8.9 us
    convert_element_type x5, other arithmetic, add(): return (a.astype(jnp.float32) + b.astype(jnp.float32)).astype(jnp.bfloat16)  4.7 us
  transfers between devices with their start and end apart: 25, of which 11 were waited for; matrix products, arithmetic and copies ran while one was open for 5% of the time, Pallas kernels for 2%

profile of v1, /device:TPU:6, one launch (start us, length us, event | category | flops | bytes accessed | tf_op | source)
XLA Modules:
  0.0 223.5 jit_solution(7073624314303819326)
XLA Ops:
  1.9 2.4 %collective-permute-start.12 = (bf16[1,768,2048]{2,1,0:T(8,128)(2,1)}, bf16[1,768,2048]{2,1,0:T(8,128)(2,1)S(1)}, u32[]{:S(2)}, u32[]{:S(2)}) collective-permute-start(bf16[1,768,2048]{2,1,0:T(8,128)(2,1)} %d0.1), channel_id=1, source_target_pairs={{0,1},{1,0},{2,3},{3,2},{4,5},{5,4},{6,7},{7,6},{8,9},{9,8},{10,11... | collective-permute-start | bytes 9437192 | tf_op jit(solution)/shard_map/ppermute | solution.py:29
  8.9 9.1 %collective-permute-start = (bf16[32,2176]{1,0:T(8,128)(2,1)S(1)}, bf16[32,2176]{1,0:T(8,128)(2,1)S(1)}, u32[]{:S(2)}, u32[]{:S(2)}) collective-permute-start(bf16[32,2176]{1,0:T(8,128)(2,1)S(1)} %pad_maximum_fusion.refs_0_), channel_id=1, source_target_pairs={{0,8},{1,57},{2,10},{3,59},{4,12},{5,61},{6,14},{7,63},{8,16},{9,1... | collective-permute-start | bytes 417800 | tf_op jit(solution)/shard_map/ppermute | solution.py:29
  18.0 15.7 %collective-permute-start.4 = (bf16[32,2176]{1,0:T(8,128)(2,1)S(1)}, bf16[32,2176]{1,0:T(8,128)(2,1)}, u32[]{:S(2)}, u32[]{:S(2)}) collective-permute-start(bf16[32,2176]{1,0:T(8,128)(2,1)S(1)} %pad_maximum_fusion.refs_0_), channel_id=1, source_target_pairs={{0,57},{1,8},{2,59},{3,10},{4,61},{5,12},{6,63},{7,14},{8,1},{9,16... | collective-permute-start | bytes 417800 | tf_op jit(solution)/shard_map/ppermute | solution.py:29
  33.7 4.3 %collective-permute-start.1 = (bf16[32,2176]{1,0:T(8,128)(2,1)S(1)}, bf16[32,2176]{1,0:T(8,128)(2,1)}, u32[]{:S(2)}, u32[]{:S(2)}) collective-permute-start(bf16[32,2176]{1,0:T(8,128)(2,1)S(1)} %collective-permute-done.refs_1_), channel_id=1, source_target_pairs={{0,8},{1,57},{2,10},{3,59},{4,12},{5,61},{6,14},{7,63},{8,16},{9,1... | collective-permute-start | bytes 417800 | tf_op jit(solution)/shard_map/ppermute | solution.py:29
  38.0 5.7 %collective-permute-done.4.refs_5_ = bf16[32,2176]{1,0:T(8,128)(2,1)} collective-permute-done((bf16[32,2176]{1,0:T(8,128)(2,1)S(1)}, bf16[32,2176]{1,0:T(8,128)(2,1)}, u32[]{:S(2)}, u32[]{:S(2)}) %collective-permute-start.4) | collective-permute-done | bytes 139296 | tf_op jit(solution)/shard_map/ppermute | solution.py:29
  43.7 6.6 %collective-permute-start.5 = (bf16[32,2176]{1,0:T(8,128)(2,1)}, bf16[32,2176]{1,0:T(8,128)(2,1)}, u32[]{:S(2)}, u32[]{:S(2)}) collective-permute-start(bf16[32,2176]{1,0:T(8,128)(2,1)} %collective-permute-done.4.refs_5_), channel_id=1, source_target_pairs={{0,8},{1,57},{2,10},{3,59},{4,12},{5,61},{6,14},{7,63},{8,16},{9,1... | collective-permute-start | bytes 417800 | tf_op jit(solution)/shard_map/ppermute | solution.py:29
  52.3 9.6 %collective-permute-done.5.refs_6_ = bf16[32,2176]{1,0:T(8,128)(2,1)} collective-permute-done((bf16[32,2176]{1,0:T(8,128)(2,1)}, bf16[32,2176]{1,0:T(8,128)(2,1)}, u32[]{:S(2)}, u32[]{:S(2)}) %collective-permute-start.5) | collective-permute-done | bytes 139296 | tf_op jit(solution)/shard_map/ppermute | solution.py:29
  61.9 4.0 %collective-permute-start.6 = (bf16[32,2176]{1,0:T(8,128)(2,1)}, bf16[32,2176]{1,0:T(8,128)(2,1)}, u32[]{:S(2)}, u32[]{:S(2)}) collective-permute-start(bf16[32,2176]{1,0:T(8,128)(2,1)} %collective-permute-done.5.refs_6_), channel_id=1, source_target_pairs={{0,8},{1,57},{2,10},{3,59},{4,12},{5,61},{6,14},{7,63},{8,16},{9,1... | collective-permute-start | bytes 417800 | tf_op jit(solution)/shard_map/ppermute | solution.py:29
  68.7 8.4 %collective-permute-done.6.refs_7_ = bf16[32,2176]{1,0:T(8,128)(2,1)} collective-permute-done((bf16[32,2176]{1,0:T(8,128)(2,1)}, bf16[32,2176]{1,0:T(8,128)(2,1)}, u32[]{:S(2)}, u32[]{:S(2)}) %collective-permute-start.6) | collective-permute-done | bytes 139296 | tf_op jit(solution)/shard_map/ppermute | solution.py:29
  79.2 4.0 %dispatch.1 = (bf16[96,2048]{1,0:T(8,128)(2,1)}, bf16[96,2048]{1,0:T(8,128)(2,1)}, bf16[96,2048]{1,0:T(8,128)(2,1)}, bf16[48,2048]{1,0:T(8,128)(2,1)}, bf16[48,2...) custom-call(f32[8,384]{1,0:T(8,128)} %broadcast_in_dim.18.expert_ref, ...), custom_call_target="tpu_custom_call" | custom-call | flops 452984832 | bytes 4194304 | tf_op jit(solution)/shard_map/dispatch/pallas_call | solution.py:82
  83.2 7.6 %collective-permute-start.9 = (bf16[48,2048]{1,0:T(8,128)(2,1)}, bf16[48,2048]{1,0:T(8,128)(2,1)}, u32[]{:S(2)}, u32[]{:S(2)}) collective-permute-start(bf16[48,2048]{1,0:T(8,128)(2,1)} %get-tuple-element.30), channel_id=1, source_target_pairs={{0,4},{1,5},{2,6},{3,7},{4,8},{5,9},{6,10},{7,11},{8,12},{9,13},{1... | collective-permute-start | bytes 589832 | tf_op jit(solution)/shard_map/ppermute | solution.py:29
  90.8 4.8 %collective-permute-start.7 = (bf16[96,2048]{1,0:T(8,128)(2,1)}, bf16[96,2048]{1,0:T(8,128)(2,1)S(1)}, u32[]{:S(2)}, u32[]{:S(2)}) collective-permute-start(bf16[96,2048]{1,0:T(8,128)(2,1)} %get-tuple-element.28), channel_id=1, source_target_pairs={{0,2},{1,3},{2,4},{3,5},{4,6},{5,7},{6,8},{7,9},{8,10},{9,11},{10,... | collective-permute-start | bytes 1179656 | tf_op jit(solution)/shard_map/ppermute | solution.py:29
  95.6 2.2 %collective-permute-start.8 = (bf16[96,2048]{1,0:T(8,128)(2,1)}, bf16[96,2048]{1,0:T(8,128)(2,1)}, u32[]{:S(2)}, u32[]{:S(2)}) collective-permute-start(bf16[96,2048]{1,0:T(8,128)(2,1)} %get-tuple-element.29), channel_id=1, source_target_pairs={{0,62},{1,63},{2,0},{3,1},{4,2},{5,3},{6,4},{7,5},{8,6},{9,7},{10,... | collective-permute-start | bytes 1179656 | tf_op jit(solution)/shard_map/ppermute | solution.py:29
  97.9 3.0 %collective-permute-done.9.first2 = bf16[48,2048]{1,0:T(8,128)(2,1)} collective-permute-done((bf16[48,2048]{1,0:T(8,128)(2,1)}, bf16[48,2048]{1,0:T(8,128)(2,1)}, u32[]{:S(2)}, u32[]{:S(2)}) %collective-permute-start.9) | collective-permute-done | bytes 196640 | tf_op jit(solution)/shard_map/ppermute | solution.py:29
  100.9 5.8 %collective-permute-start.10 = (bf16[48,2048]{1,0:T(8,128)(2,1)}, bf16[48,2048]{1,0:T(8,128)(2,1)}, u32[]{:S(2)}, u32[]{:S(2)}) collective-permute-start(bf16[48,2048]{1,0:T(8,128)(2,1)} %get-tuple-element.31), channel_id=1, source_target_pairs={{0,60},{1,61},{2,62},{3,63},{4,0},{5,1},{6,2},{7,3},{8,4},{9,5},{1... | collective-permute-start | bytes 589832 | tf_op jit(solution)/shard_map/ppermute | solution.py:29
  106.7 7.4 %collective-permute-done.10.second2 = bf16[48,2048]{1,0:T(8,128)(2,1)} collective-permute-done((bf16[48,2048]{1,0:T(8,128)(2,1)}, bf16[48,2048]{1,0:T(8,128)(2,1)}, u32[]{:S(2)}, u32[]{:S(2)}) %collective-permute-start.10) | collective-permute-done | bytes 196640 | tf_op jit(solution)/shard_map/ppermute | solution.py:29
  115.9 13.3 %experts.1 = (bf16[96,2048]{1,0:T(8,128)(2,1)}, bf16[96,2048]{1,0:T(8,128)(2,1)}, bf16[96,2048]{1,0:T(8,128)(2,1)}, bf16[48,2048]{1,0:T(8,128)(2,1)}, bf16[48,2048]{1,0:T(8,128)(2,1)}) custom-call(s32[1]{0:T(128)} %bitcast.3.core_ref, bf16[96,2048]{1,0:T(8,128)(2,1)} %get-tuple-element.27.here, bf16[96,2048]{1,0:T(8,128)(2,1)} %copy-done.1, ...), custom_call_target="tpu_custom_call" | custom-call | flops 3623878656 | bytes 18874368 | tf_op jit(solution)/shard_map/experts/pallas_call | solution.py:161
  131.1 3.9 %collective-permute-start.14 = (bf16[96,2048]{1,0:T(8,128)(2,1)}, bf16[96,2048]{1,0:T(8,128)(2,1)S(1)}, u32[]{:S(2)}, u32[]{:S(2)}) collective-permute-start(bf16[96,2048]{1,0:T(8,128)(2,1)} %get-tuple-element.34), channel_id=1, source_target_pairs={{0,2},{1,3},{2,4},{3,5},{4,6},{5,7},{6,8},{7,9},{8,10},{9,11},{10,... | collective-permute-start | bytes 1179656 | tf_op jit(solution)/shard_map/ppermute | solution.py:29
  135.0 4.3 %collective-permute-start.15 = (bf16[48,2048]{1,0:T(8,128)(2,1)}, bf16[48,2048]{1,0:T(8,128)(2,1)S(1)}, u32[]{:S(2)}, u32[]{:S(2)}) collective-permute-start(bf16[48,2048]{1,0:T(8,128)(2,1)} %get-tuple-element.35), channel_id=1, source_target_pairs={{0,60},{1,61},{2,62},{3,63},{4,0},{5,1},{6,2},{7,3},{8,4},{9,5},{1... | collective-permute-start | bytes 589832 | tf_op jit(solution)/shard_map/ppermute | solution.py:29
  139.3 2.4 %collective-permute-start.16 = (bf16[48,2048]{1,0:T(8,128)(2,1)}, bf16[48,2048]{1,0:T(8,128)(2,1)S(1)}, u32[]{:S(2)}, u32[]{:S(2)}) collective-permute-start(bf16[48,2048]{1,0:T(8,128)(2,1)} %get-tuple-element.36), channel_id=1, source_target_pairs={{0,4},{1,5},{2,6},{3,7},{4,8},{5,9},{6,10},{7,11},{8,12},{9,13},{1... | collective-permute-start | bytes 589832 | tf_op jit(solution)/shard_map/ppermute | solution.py:29
  141.8 5.6 %collective-permute-done.15.refs_3_ = bf16[48,2048]{1,0:T(8,128)(2,1)S(1)} collective-permute-done((bf16[48,2048]{1,0:T(8,128)(2,1)}, bf16[48,2048]{1,0:T(8,128)(2,1)S(1)}, u32[]{:S(2)}, u32[]{:S(2)}) %collective-permute-start.15) | collective-permute-done | bytes 196640 | tf_op jit(solution)/shard_map/ppermute | solution.py:29
  147.4 5.1 %collective-permute-done.16.refs_4_ = bf16[48,2048]{1,0:T(8,128)(2,1)S(1)} collective-permute-done((bf16[48,2048]{1,0:T(8,128)(2,1)}, bf16[48,2048]{1,0:T(8,128)(2,1)S(1)}, u32[]{:S(2)}, u32[]{:S(2)}) %collective-permute-start.16) | collective-permute-done | bytes 196640 | tf_op jit(solution)/shard_map/ppermute | solution.py:29
  153.4 3.7 %combine.1 = (f32[32,2048]{1,0:T(8,128)}, bf16[32,2048]{1,0:T(8,128)(2,1)}, bf16[32,2048]{1,0:T(8,128)(2,1)}, bf16[32,2048]{1,0:T(8,128)(2,1)}, bf16[32,2048]{1,...) custom-call(bf16[256,384]{1,0:T(8,128)(2,1)} %get-tuple-element.25.hi, ...), custom_call_target="tpu_custom_call" | custom-call | flops 805306368 | bytes 4194304 | tf_op jit(solution)/shard_map/combine/pallas_call | solution.py:201
  157.2 5.7 %collective-permute-start.18 = (bf16[32,2048]{1,0:T(8,128)(2,1)}, bf16[32,2048]{1,0:T(8,128)(2,1)S(1)}, u32[]{:S(2)}, u32[]{:S(2)}) collective-permute-start(bf16[32,2048]{1,0:T(8,128)(2,1)} %get-tuple-element.41), channel_id=1, source_target_pairs={{0,56},{1,9},{2,58},{3,11},{4,60},{5,13},{6,62},{7,15},{8,0},{9,17... | collective-permute-start | bytes 393224 | tf_op jit(solution)/shard_map/ppermute | solution.py:29
  162.9 10.1 %collective-permute-start.22 = (bf16[32,2048]{1,0:T(8,128)(2,1)}, bf16[32,2048]{1,0:T(8,128)(2,1)S(1)}, u32[]{:S(2)}, u32[]{:S(2)}) collective-permute-start(bf16[32,2048]{1,0:T(8,128)(2,1)} %get-tuple-element.44), channel_id=1, source_target_pairs={{0,56},{1,9},{2,58},{3,11},{4,60},{5,13},{6,62},{7,15},{8,0},{9,17... | collective-permute-start | bytes 393224 | tf_op jit(solution)/shard_map/ppermute | solution.py:29
  173.0 3.5 %collective-permute-start.17 = (f32[32,2048]{1,0:T(8,128)}, f32[32,2048]{1,0:T(8,128)S(1)}, u32[]{:S(2)}, u32[]{:S(2)}) collective-permute-start(f32[32,2048]{1,0:T(8,128)} %get-tuple-element.37), channel_id=1, source_target_pairs={{0,64},{1,65},{2,66},{3,67},{4,68},{5,69},{6,70},{7,71},{8,72},{9,... | collective-permute-start | bytes 786440 | tf_op jit(solution)/shard_map/ppermute | solution.py:36
  177.5 6.1 %collective-permute-start.19 = (bf16[32,2048]{1,0:T(8,128)(2,1)S(1)}, bf16[32,2048]{1,0:T(8,128)(2,1)S(1)}, u32[]{:S(2)}, u32[]{:S(2)}) collective-permute-start(bf16[32,2048]{1,0:T(8,128)(2,1)S(1)} %add_convert_fusion.5), channel_id=1, source_target_pairs={{0,56},{1,9},{2,58},{3,11},{4,60},{5,13},{6,62},{7,15},{8,0},{9,17... | collective-permute-start | bytes 393224 | tf_op jit(solution)/shard_map/ppermute | solution.py:29
  184.6 8.2 %collective-permute-start.23 = (bf16[32,2048]{1,0:T(8,128)(2,1)S(1)}, bf16[32,2048]{1,0:T(8,128)(2,1)S(1)}, u32[]{:S(2)}, u32[]{:S(2)}) collective-permute-start(bf16[32,2048]{1,0:T(8,128)(2,1)S(1)} %add_convert_fusion.2), channel_id=1, source_target_pairs={{0,56},{1,9},{2,58},{3,11},{4,60},{5,13},{6,62},{7,15},{8,0},{9,17... | collective-permute-start | bytes 393224 | tf_op jit(solution)/shard_map/ppermute | solution.py:29
  194.2 3.5 %collective-permute-start.20 = (bf16[32,2048]{1,0:T(8,128)(2,1)S(1)}, bf16[32,2048]{1,0:T(8,128)(2,1)S(1)}, u32[]{:S(2)}, u32[]{:S(2)}) collective-permute-start(bf16[32,2048]{1,0:T(8,128)(2,1)S(1)} %add_convert_fusion.4), channel_id=1, source_target_pairs={{0,56},{1,9},{2,58},{3,11},{4,60},{5,13},{6,62},{7,15},{8,0},{9,17... | collective-permute-start | bytes 393224 | tf_op jit(solution)/shard_map/ppermute | solution.py:29
  198.6 6.3 %collective-permute-start.24 = (bf16[32,2048]{1,0:T(8,128)(2,1)S(1)}, bf16[32,2048]{1,0:T(8,128)(2,1)S(1)}, u32[]{:S(2)}, u32[]{:S(2)}) collective-permute-start(bf16[32,2048]{1,0:T(8,128)(2,1)S(1)} %add_convert_fusion.1), channel_id=1, source_target_pairs={{0,121},{1,72},{2,123},{3,74},{4,125},{5,76},{6,127},{7,78},{8,65}... | collective-permute-start | bytes 393224 | tf_op jit(solution)/shard_map/ppermute | solution.py:36
  208.0 5.9 %collective-permute-start.21 = (bf16[32,2048]{1,0:T(8,128)(2,1)S(1)}, bf16[32,2048]{1,0:T(8,128)(2,1)S(1)}, u32[]{:S(2)}, u32[]{:S(2)}) collective-permute-start(bf16[32,2048]{1,0:T(8,128)(2,1)S(1)} %add_convert_fusion.3), channel_id=1, source_target_pairs={{0,120},{1,73},{2,122},{3,75},{4,124},{5,77},{6,126},{7,79},{8,64}... | collective-permute-start | bytes 393224 | tf_op jit(solution)/shard_map/ppermute | solution.py:36
  213.9 8.9 %collective-permute-done.21 = bf16[32,2048]{1,0:T(8,128)(2,1)S(1)} collective-permute-done((bf16[32,2048]{1,0:T(8,128)(2,1)S(1)}, bf16[32,2048]{1,0:T(8,128)(2,1)S(1)}, u32[]{:S(2)}, u32[]{:S(2)}) %collective-permute-start.21) | collective-permute-done | bytes 131104 | tf_op jit(solution)/shard_map/ppermute | solution.py:36
  (57 shorter events, 25.9 us)
Async XLA Ops:
  0.0 114.1 %collective-permute-start.11 = (bf16[1,2048,1536]{2,1,0:T(8,128)(2,1)}, bf16[1,2048,1536]{2,1,0:T(8,128)(2,1)}, u32[]{:S(2)}, u32[]{:S(2)}) collective-permute-start(bf16[1,2048,1536]{2,1,0:T(8,128)(2,1)} %u0.1), channel_id=1, source_target_pairs={{0,1},{1,0},{2,3},{3,2},{4,5},{5,4},{6,7},{7,6},{8,9},{9,8},{10,11... | collective-permute-start | bytes 18874376 | tf_op jit(solution)/shard_map/ppermute | solution.py:29
  1.9 112.1 %collective-permute-start.12 = (bf16[1,768,2048]{2,1,0:T(8,128)(2,1)}, bf16[1,768,2048]{2,1,0:T(8,128)(2,1)S(1)}, u32[]{:S(2)}, u32[]{:S(2)}) collective-permute-start(bf16[1,768,2048]{2,1,0:T(8,128)(2,1)} %d0.1), channel_id=1, source_target_pairs={{0,1},{1,0},{2,3},{3,2},{4,5},{5,4},{6,7},{7,6},{8,9},{9,8},{10,11... | collective-permute-start | bytes 9437192 | tf_op jit(solution)/shard_map/ppermute | solution.py:29
  8.9 70.3 %copy-start.2 = (bf16[32,2176]{1,0:T(8,128)(2,1)}, bf16[32,2176]{1,0:T(8,128)(2,1)S(1)}, u32[]{:S(2)}) copy-start(bf16[32,2176]{1,0:T(8,128)(2,1)S(1)} %pad_maximum_fusion.refs_0_) | copy-start | bytes 417796
  8.9 24.8 %collective-permute-start = (bf16[32,2176]{1,0:T(8,128)(2,1)S(1)}, bf16[32,2176]{1,0:T(8,128)(2,1)S(1)}, u32[]{:S(2)}, u32[]{:S(2)}) collective-permute-start(bf16[32,2176]{1,0:T(8,128)(2,1)S(1)} %pad_maximum_fusion.refs_0_), channel_id=1, source_target_pairs={{0,8},{1,57},{2,10},{3,59},{4,12},{5,61},{6,14},{7,63},{8,16},{9,1... | collective-permute-start | bytes 417800 | tf_op jit(solution)/shard_map/ppermute | solution.py:29
  18.0 25.8 %collective-permute-start.4 = (bf16[32,2176]{1,0:T(8,128)(2,1)S(1)}, bf16[32,2176]{1,0:T(8,128)(2,1)}, u32[]{:S(2)}, u32[]{:S(2)}) collective-permute-start(bf16[32,2176]{1,0:T(8,128)(2,1)S(1)} %pad_maximum_fusion.refs_0_), channel_id=1, source_target_pairs={{0,57},{1,8},{2,59},{3,10},{4,61},{5,12},{6,63},{7,14},{8,1},{9,16... | collective-permute-start | bytes 417800 | tf_op jit(solution)/shard_map/ppermute | solution.py:29
  33.7 45.5 %copy-start.7 = (bf16[32,2176]{1,0:T(8,128)(2,1)}, bf16[32,2176]{1,0:T(8,128)(2,1)S(1)}, u32[]{:S(2)}) copy-start(bf16[32,2176]{1,0:T(8,128)(2,1)S(1)} %collective-permute-done.refs_1_) | copy-start | bytes 417796
  33.7 16.6 %collective-permute-start.1 = (bf16[32,2176]{1,0:T(8,128)(2,1)S(1)}, bf16[32,2176]{1,0:T(8,128)(2,1)}, u32[]{:S(2)}, u32[]{:S(2)}) collective-permute-start(bf16[32,2176]{1,0:T(8,128)(2,1)S(1)} %collective-permute-done.refs_1_), channel_id=1, source_target_pairs={{0,8},{1,57},{2,10},{3,59},{4,12},{5,61},{6,14},{7,63},{8,16},{9,1... | collective-permute-start | bytes 417800 | tf_op jit(solution)/shard_map/ppermute | solution.py:29
  43.7 18.1 %collective-permute-start.5 = (bf16[32,2176]{1,0:T(8,128)(2,1)}, bf16[32,2176]{1,0:T(8,128)(2,1)}, u32[]{:S(2)}, u32[]{:S(2)}) collective-permute-start(bf16[32,2176]{1,0:T(8,128)(2,1)} %collective-permute-done.4.refs_5_), channel_id=1, source_target_pairs={{0,8},{1,57},{2,10},{3,59},{4,12},{5,61},{6,14},{7,63},{8,16},{9,1... | collective-permute-start | bytes 417800 | tf_op jit(solution)/shard_map/ppermute | solution.py:29
  50.3 15.6 %collective-permute-start.2 = (bf16[32,2176]{1,0:T(8,128)(2,1)}, bf16[32,2176]{1,0:T(8,128)(2,1)}, u32[]{:S(2)}, u32[]{:S(2)}) collective-permute-start(bf16[32,2176]{1,0:T(8,128)(2,1)} %collective-permute-done.1.refs_2_), channel_id=1, source_target_pairs={{0,8},{1,57},{2,10},{3,59},{4,12},{5,61},{6,14},{7,63},{8,16},{9,1... | collective-permute-start | bytes 417800 | tf_op jit(solution)/shard_map/ppermute | solution.py:29
  61.9 15.2 %collective-permute-start.6 = (bf16[32,2176]{1,0:T(8,128)(2,1)}, bf16[32,2176]{1,0:T(8,128)(2,1)}, u32[]{:S(2)}, u32[]{:S(2)}) collective-permute-start(bf16[32,2176]{1,0:T(8,128)(2,1)} %collective-permute-done.5.refs_6_), channel_id=1, source_target_pairs={{0,8},{1,57},{2,10},{3,59},{4,12},{5,61},{6,14},{7,63},{8,16},{9,1... | collective-permute-start | bytes 417800 | tf_op jit(solution)/shard_map/ppermute | solution.py:29
  65.9 12.7 %collective-permute-start.3 = (bf16[32,2176]{1,0:T(8,128)(2,1)}, bf16[32,2176]{1,0:T(8,128)(2,1)}, u32[]{:S(2)}, u32[]{:S(2)}) collective-permute-start(bf16[32,2176]{1,0:T(8,128)(2,1)} %collective-permute-done.2.refs_3_), channel_id=1, source_target_pairs={{0,8},{1,57},{2,10},{3,59},{4,12},{5,61},{6,14},{7,63},{8,16},{9,1... | collective-permute-start | bytes 417800 | tf_op jit(solution)/shard_map/ppermute | solution.py:29
  83.2 17.7 %collective-permute-start.9 = (bf16[48,2048]{1,0:T(8,128)(2,1)}, bf16[48,2048]{1,0:T(8,128)(2,1)}, u32[]{:S(2)}, u32[]{:S(2)}) collective-permute-start(bf16[48,2048]{1,0:T(8,128)(2,1)} %get-tuple-element.30), channel_id=1, source_target_pairs={{0,4},{1,5},{2,6},{3,7},{4,8},{5,9},{6,10},{7,11},{8,12},{9,13},{1... | collective-permute-start | bytes 589832 | tf_op jit(solution)/shard_map/ppermute | solution.py:29
  90.8 23.2 %collective-permute-start.7 = (bf16[96,2048]{1,0:T(8,128)(2,1)}, bf16[96,2048]{1,0:T(8,128)(2,1)S(1)}, u32[]{:S(2)}, u32[]{:S(2)}) collective-permute-start(bf16[96,2048]{1,0:T(8,128)(2,1)} %get-tuple-element.28), channel_id=1, source_target_pairs={{0,2},{1,3},{2,4},{3,5},{4,6},{5,7},{6,8},{7,9},{8,10},{9,11},{10,... | collective-permute-start | bytes 1179656 | tf_op jit(solution)/shard_map/ppermute | solution.py:29
  95.6 18.4 %collective-permute-start.8 = (bf16[96,2048]{1,0:T(8,128)(2,1)}, bf16[96,2048]{1,0:T(8,128)(2,1)}, u32[]{:S(2)}, u32[]{:S(2)}) collective-permute-start(bf16[96,2048]{1,0:T(8,128)(2,1)} %get-tuple-element.29), channel_id=1, source_target_pairs={{0,62},{1,63},{2,0},{3,1},{4,2},{5,3},{6,4},{7,5},{8,6},{9,7},{10,... | collective-permute-start | bytes 1179656 | tf_op jit(solution)/shard_map/ppermute | solution.py:29
  100.9 13.2 %collective-permute-start.10 = (bf16[48,2048]{1,0:T(8,128)(2,1)}, bf16[48,2048]{1,0:T(8,128)(2,1)}, u32[]{:S(2)}, u32[]{:S(2)}) collective-permute-start(bf16[48,2048]{1,0:T(8,128)(2,1)} %get-tuple-element.31), channel_id=1, source_target_pairs={{0,60},{1,61},{2,62},{3,63},{4,0},{5,1},{6,2},{7,3},{8,4},{9,5},{1... | collective-permute-start | bytes 589832 | tf_op jit(solution)/shard_map/ppermute | solution.py:29
  114.0 0.8 copy-start.1
  114.1 1.8 copy-start
  129.2 23.3 %collective-permute-start.13 = (bf16[96,2048]{1,0:T(8,128)(2,1)}, bf16[96,2048]{1,0:T(8,128)(2,1)S(1)}, u32[]{:S(2)}, u32[]{:S(2)}) collective-permute-start(bf16[96,2048]{1,0:T(8,128)(2,1)} %get-tuple-element.33), channel_id=1, source_target_pairs={{0,62},{1,63},{2,0},{3,1},{4,2},{5,3},{6,4},{7,5},{8,6},{9,7},{10,... | collective-permute-start | bytes 1179656 | tf_op jit(solution)/shard_map/ppermute | solution.py:29
  131.1 21.4 %collective-permute-start.14 = (bf16[96,2048]{1,0:T(8,128)(2,1)}, bf16[96,2048]{1,0:T(8,128)(2,1)S(1)}, u32[]{:S(2)}, u32[]{:S(2)}) collective-permute-start(bf16[96,2048]{1,0:T(8,128)(2,1)} %get-tuple-element.34), channel_id=1, source_target_pairs={{0,2},{1,3},{2,4},{3,5},{4,6},{5,7},{6,8},{7,9},{8,10},{9,11},{10,... | collective-permute-start | bytes 1179656 | tf_op jit(solution)/shard_map/ppermute | solution.py:29
  135.0 12.3 %collective-permute-start.15 = (bf16[48,2048]{1,0:T(8,128)(2,1)}, bf16[48,2048]{1,0:T(8,128)(2,1)S(1)}, u32[]{:S(2)}, u32[]{:S(2)}) collective-permute-start(bf16[48,2048]{1,0:T(8,128)(2,1)} %get-tuple-element.35), channel_id=1, source_target_pairs={{0,60},{1,61},{2,62},{3,63},{4,0},{5,1},{6,2},{7,3},{8,4},{9,5},{1... | collective-permute-start | bytes 589832 | tf_op jit(solution)/shard_map/ppermute | solution.py:29
  139.3 13.1 %collective-permute-start.16 = (bf16[48,2048]{1,0:T(8,128)(2,1)}, bf16[48,2048]{1,0:T(8,128)(2,1)S(1)}, u32[]{:S(2)}, u32[]{:S(2)}) collective-permute-start(bf16[48,2048]{1,0:T(8,128)(2,1)} %get-tuple-element.36), channel_id=1, source_target_pairs={{0,4},{1,5},{2,6},{3,7},{4,8},{5,9},{6,10},{7,11},{8,12},{9,13},{1... | collective-permute-start | bytes 589832 | tf_op jit(solution)/shard_map/ppermute | solution.py:29
  147.4 5.1 %copy-start.5 = (bf16[48,2048]{1,0:T(8,128)(2,1)}, bf16[48,2048]{1,0:T(8,128)(2,1)S(1)}, u32[]{:S(2)}) copy-start(bf16[48,2048]{1,0:T(8,128)(2,1)S(1)} %collective-permute-done.15.refs_3_) | copy-start | bytes 589828
  152.4 0.8 copy-start.3
  152.4 1.0 copy-start.4
  157.2 19.4 %collective-permute-start.18 = (bf16[32,2048]{1,0:T(8,128)(2,1)}, bf16[32,2048]{1,0:T(8,128)(2,1)S(1)}, u32[]{:S(2)}, u32[]{:S(2)}) collective-permute-start(bf16[32,2048]{1,0:T(8,128)(2,1)} %get-tuple-element.41), channel_id=1, source_target_pairs={{0,56},{1,9},{2,58},{3,11},{4,60},{5,13},{6,62},{7,15},{8,0},{9,17... | collective-permute-start | bytes 393224 | tf_op jit(solution)/shard_map/ppermute | solution.py:29
  162.9 20.7 %collective-permute-start.22 = (bf16[32,2048]{1,0:T(8,128)(2,1)}, bf16[32,2048]{1,0:T(8,128)(2,1)S(1)}, u32[]{:S(2)}, u32[]{:S(2)}) collective-permute-start(bf16[32,2048]{1,0:T(8,128)(2,1)} %get-tuple-element.44), channel_id=1, source_target_pairs={{0,56},{1,9},{2,58},{3,11},{4,60},{5,13},{6,62},{7,15},{8,0},{9,17... | collective-permute-start | bytes 393224 | tf_op jit(solution)/shard_map/ppermute | solution.py:29
  173.0 40.8 %collective-permute-start.17 = (f32[32,2048]{1,0:T(8,128)}, f32[32,2048]{1,0:T(8,128)S(1)}, u32[]{:S(2)}, u32[]{:S(2)}) collective-permute-start(f32[32,2048]{1,0:T(8,128)} %get-tuple-element.37), channel_id=1, source_target_pairs={{0,64},{1,65},{2,66},{3,67},{4,68},{5,69},{6,70},{7,71},{8,72},{9,... | collective-permute-start | bytes 786440 | tf_op jit(solution)/shard_map/ppermute | solution.py:36
  177.5 15.7 %collective-permute-start.19 = (bf16[32,2048]{1,0:T(8,128)(2,1)S(1)}, bf16[32,2048]{1,0:T(8,128)(2,1)S(1)}, u32[]{:S(2)}, u32[]{:S(2)}) collective-permute-start(bf16[32,2048]{1,0:T(8,128)(2,1)S(1)} %add_convert_fusion.5), channel_id=1, source_target_pairs={{0,56},{1,9},{2,58},{3,11},{4,60},{5,13},{6,62},{7,15},{8,0},{9,17... | collective-permute-start | bytes 393224 | tf_op jit(solution)/shard_map/ppermute | solution.py:29
  184.6 13.1 %collective-permute-start.23 = (bf16[32,2048]{1,0:T(8,128)(2,1)S(1)}, bf16[32,2048]{1,0:T(8,128)(2,1)S(1)}, u32[]{:S(2)}, u32[]{:S(2)}) collective-permute-start(bf16[32,2048]{1,0:T(8,128)(2,1)S(1)} %add_convert_fusion.2), channel_id=1, source_target_pairs={{0,56},{1,9},{2,58},{3,11},{4,60},{5,13},{6,62},{7,15},{8,0},{9,17... | collective-permute-start | bytes 393224 | tf_op jit(solution)/shard_map/ppermute | solution.py:29
  194.2 12.9 %collective-permute-start.20 = (bf16[32,2048]{1,0:T(8,128)(2,1)S(1)}, bf16[32,2048]{1,0:T(8,128)(2,1)S(1)}, u32[]{:S(2)}, u32[]{:S(2)}) collective-permute-start(bf16[32,2048]{1,0:T(8,128)(2,1)S(1)} %add_convert_fusion.4), channel_id=1, source_target_pairs={{0,56},{1,9},{2,58},{3,11},{4,60},{5,13},{6,62},{7,15},{8,0},{9,17... | collective-permute-start | bytes 393224 | tf_op jit(solution)/shard_map/ppermute | solution.py:29
  198.6 15.3 %collective-permute-start.24 = (bf16[32,2048]{1,0:T(8,128)(2,1)S(1)}, bf16[32,2048]{1,0:T(8,128)(2,1)S(1)}, u32[]{:S(2)}, u32[]{:S(2)}) collective-permute-start(bf16[32,2048]{1,0:T(8,128)(2,1)S(1)} %add_convert_fusion.1), channel_id=1, source_target_pairs={{0,121},{1,72},{2,123},{3,74},{4,125},{5,76},{6,127},{7,78},{8,65}... | collective-permute-start | bytes 393224 | tf_op jit(solution)/shard_map/ppermute | solution.py:36
  208.0 14.8 %collective-permute-start.21 = (bf16[32,2048]{1,0:T(8,128)(2,1)S(1)}, bf16[32,2048]{1,0:T(8,128)(2,1)S(1)}, u32[]{:S(2)}, u32[]{:S(2)}) collective-permute-start(bf16[32,2048]{1,0:T(8,128)(2,1)S(1)} %add_convert_fusion.3), channel_id=1, source_target_pairs={{0,120},{1,73},{2,122},{3,75},{4,124},{5,77},{6,126},{7,79},{8,64}... | collective-permute-start | bytes 393224 | tf_op jit(solution)/shard_map/ppermute | solution.py:36
  (1 other events, 0.7 us)

commit v2 on v1

v2 whole, which is shorter than its diff:
```python
import functools

import jax
import jax.numpy as jnp
from jax import lax
from jax.experimental import pallas as pl
from jax.experimental.pallas import tpu as pltpu
from jax.sharding import PartitionSpec as P

CAP = 6
ROWS = 32
INFO = 128
FAR = 4
NEAR = FAR // 2
BLOCKS = 8
SEG = BLOCKS * CAP
SLOTS = 8 * SEG
TILES = 3


def send(value, up, down, other=False, onward=0):
    count, sections = lax.axis_size("expert"), lax.axis_size("section")

    def place(i):
        core = 1 - i % 2 if other else i % 2
        return ((i // 2 + (down if i % 2 else up)) * 2) % count + core

    if not onward:
        return lax.ppermute(value, "expert", [(i, place(i)) for i in range(count)])
    pairs = [
        (s * count + i, (s + onward) % sections * count + place(i))
        for s in range(sections)
        for i in range(count)
    ]
    return lax.ppermute(value, ("section", "expert"), pairs)


def prepare_kernel(tokens, gain, ids, weights, raw, ready):
    width = tokens.shape[2]
    values = tokens[0].astype(jnp.float32)
    scale = lax.rsqrt(jnp.mean(values * values, axis=1, keepdims=True) + 1e-06)
    share = weights[0] / jnp.sum(weights[0], axis=1, keepdims=True)
    hi = share.astype(jnp.bfloat16).astype(jnp.float32)
    lo = share - hi
    named = ids[0].astype(jnp.float32)
    lane = lax.broadcasted_iota(jnp.int32, (ROWS, INFO), 1)
    info = jnp.zeros((ROWS, INFO), jnp.float32)
    for k in range(8):
        info = jnp.where(lane == k, named[:, k : k + 1], info)
        info = jnp.where(lane == 8 + k, hi[:, k : k + 1], info)
        info = jnp.where(lane == 16 + k, lo[:, k : k + 1], info)
    info = info.astype(jnp.bfloat16)
    raw[:, :width] = tokens[0]
    raw[:, width:] = info
    ready[:, :width] = (values * scale * gain[...]).astype(jnp.bfloat16)
    ready[:, width:] = info


def prepare(tokens, gain, ids, weights):
    shape = jax.ShapeDtypeStruct((ROWS, tokens.shape[2] + INFO), jnp.bfloat16)
    return pl.pallas_call(
        prepare_kernel,
        out_shape=(shape, shape),
        compiler_params=pltpu.CompilerParams(vmem_limit_bytes=8 * 2**20),
        name="prepare",
    )(tokens, gain.reshape(1, -1), ids, weights)


def dispatch_kernel(count, place, raw, gain, *refs):
    blocks = refs[: BLOCKS - 1]
    *outs, hi_ref, lo_ref = refs[BLOCKS - 1 :]
    width = outs[0].shape[1]
    rows = BLOCKS * ROWS
    chip, core = place[0] >> 1, place[0] & 1
    info = jnp.concatenate([b[:, width:] for b in (raw, *blocks)], axis=0).astype(jnp.float32)
    group = lax.broadcasted_iota(jnp.int32, (1, SLOTS), 1) // SEG
    far = jnp.where(core == 0, 2 * NEAR, -2 * NEAR)
    offset = jnp.where(group < 4, group, jnp.where(group < 6, group - 6, group - 6 + far))
    expert = 2 * chip + offset
    expert = jnp.where(expert < 0, expert + count, expert)
    expert = jnp.where(expert >= count, expert - count, expert).astype(jnp.float32)
    member = jnp.zeros((rows, SLOTS), jnp.float32)
    hi = jnp.zeros((rows, SLOTS), jnp.float32)
    lo = jnp.zeros((rows, SLOTS), jnp.float32)
    for k in range(8):
        same = info[:, k : k + 1] == expert
        member = jnp.where(same, 1.0, member)
        hi = jnp.where(same, info[:, 8 + k : 9 + k], hi)
        lo = jnp.where(same, info[:, 16 + k : 17 + k], lo)
    r = lax.broadcasted_iota(jnp.int32, (rows, rows), 0)
    c = lax.broadcasted_iota(jnp.int32, (rows, rows), 1)
    before = jnp.where((c < r) & (c // ROWS == r // ROWS), 1.0, 0.0).astype(jnp.bfloat16)
    rank = jnp.dot(before, member.astype(jnp.bfloat16), preferred_element_type=jnp.float32)
    row_block = lax.broadcasted_iota(jnp.int32, (rows, SLOTS), 0) // ROWS
    q = lax.broadcasted_iota(jnp.int32, (1, SLOTS), 1) % SEG
    taken = (member > 0.5) & (rank == (q % CAP).astype(jnp.float32)) & (q // CAP == row_block)
    hi_ref[...] = jnp.where(taken, hi, 0.0).astype(jnp.bfloat16)
    lo_ref[...] = jnp.where(taken, lo, 0.0).astype(jnp.bfloat16)
    pick = jnp.where(taken, 1.0, 0.0).astype(jnp.bfloat16)
    values = raw[:, :width].astype(jnp.float32)
    scale = lax.rsqrt(jnp.mean(values * values, axis=1, keepdims=True) + 1e-06)
    step = min(512, width)
    for at in range(0, width, step):
        cols = slice(at, at + step)
        own = raw[:, cols].astype(jnp.float32) * scale * gain[:, cols]
        x = jnp.concatenate([own.astype(jnp.bfloat16)] + [b[:, cols] for b in blocks], axis=0)
        y = lax.dot_general(pick, x, (((0,), (0,)), ((), ())), preferred_element_type=jnp.float32)
        y = y.astype(jnp.bfloat16)
        for i, out in enumerate(outs):
            out[:, cols] = y[i * 2 * SEG : (i + 1) * 2 * SEG]


def dispatch(count, place, raw, gain, blocks):
    rows, width = BLOCKS * ROWS, raw.shape[1] - INFO
    vmem = pl.BlockSpec(memory_space=pltpu.VMEM)
    return pl.pallas_call(
        functools.partial(dispatch_kernel, count),
        in_specs=[pl.BlockSpec(memory_space=pltpu.SMEM)] + [vmem] * (BLOCKS + 1),
        out_shape=[jax.ShapeDtypeStruct((2 * SEG, width), jnp.bfloat16)] * 4
        + [jax.ShapeDtypeStruct((rows, SLOTS), jnp.bfloat16)] * 2,
        compiler_params=pltpu.CompilerParams(vmem_limit_bytes=24 * 2**20),
        cost_estimate=pl.CostEstimate(
            flops=2 * rows * SLOTS * (width + rows), bytes_accessed=4 * 2**20, transcendentals=0
        ),
        name="dispatch",
    )(place, raw, gain.reshape(1, -1), *blocks)


def expert_kernel(place, *refs):
    ins, (g0, u0, d0, g1, u1, d1), outs, (x, acc) = refs[:4], refs[4:10], refs[10:14], refs[14:]
    i = pl.program_id(0)
    turn, tile = i // TILES, i % TILES
    core = place[0] & 1
    which = jnp.where(turn == 0, core, 1 - core)

    for e in range(2):
        @pl.when((tile == 0) & (which == e))
        def _():
            for n, piece in enumerate(ins):
                x[n * SEG : (n + 1) * SEG] = piece[e * SEG : (e + 1) * SEG]

    def work(g, u, d):
        gate = jnp.dot(x[...], g[0], preferred_element_type=jnp.float32)
        lift = jnp.dot(x[...], u[0], preferred_element_type=jnp.float32)
        hidden = (gate / (1.0 + jnp.exp(-gate)) * lift).astype(jnp.bfloat16)
        y = jnp.dot(hidden, d[0], preferred_element_type=jnp.float32)

        @pl.when(tile == 0)
        def _():
            acc[...] = y

        @pl.when(tile > 0)
        def _():
            acc[...] += y

    @pl.when(turn == 0)
    def _():
        work(g0, u0, d0)

    @pl.when(turn == 1)
    def _():
        work(g1, u1, d1)

    for e in range(2):
        @pl.when((tile == TILES - 1) & (which == e))
        def _():
            for n, piece in enumerate(outs):
                piece[e * SEG : (e + 1) * SEG] = acc[n * SEG : (n + 1) * SEG].astype(jnp.bfloat16)


def experts(place, pieces, own_gu, own_d, other_gu, other_d):
    width, hid = own_gu.shape[1], own_d.shape[1]
    tile = hid // TILES
    whole = [pl.BlockSpec(p.shape, lambda i, c: (0, 0)) for p in pieces]

    def early(i):
        return jnp.minimum(i, TILES - 1)

    def late(i):
        return jnp.maximum(i - TILES, 0)

    def weights(at):
        return [
            pl.BlockSpec((1, width, tile), lambda i, c: (0, 0, at(i))),
            pl.BlockSpec((1, width, tile), lambda i, c: (0, 0, at(i) + TILES)),
            pl.BlockSpec((1, tile, width), lambda i, c: (0, at(i), 0)),
        ]

    return pl.pallas_call(
        expert_kernel,
        grid_spec=pltpu.PrefetchScalarGridSpec(
            num_scalar_prefetch=1,
            grid=(2 * TILES,),
            in_specs=whole + weights(early) + weights(late),
            out_specs=whole,
            scratch_shapes=[
                pltpu.VMEM((4 * SEG, width), jnp.bfloat16),
                pltpu.VMEM((4 * SEG, width), jnp.float32),
            ],
        ),
        out_shape=[jax.ShapeDtypeStruct(p.shape, jnp.bfloat16) for p in pieces],
        compiler_params=pltpu.CompilerParams(vmem_limit_bytes=32 * 2**20),
        cost_estimate=pl.CostEstimate(
            flops=2 * 8 * SEG * 3 * width * hid,
            bytes_accessed=2 * 3 * 2 * width * hid,
            transcendentals=8 * SEG * hid,
        ),
        name="experts",
    )(place, *pieces, own_gu, own_gu, own_d, other_gu, other_gu, other_d)


def combine_kernel(hi, lo, raw, *refs):
    answers, outs = refs[:4], refs[4:]
    width = outs[0].shape[1]
    step = min(512, width)
    for at in range(0, width, step):
        cols = slice(at, at + step)
        a = jnp.concatenate([r[:, cols] for r in answers], axis=0)
        y = jnp.dot(hi[...], a, preferred_element_type=jnp.float32)
        y = y + jnp.dot(lo[...], a, preferred_element_type=jnp.float32)
        outs[0][:, cols] = y[:ROWS] + raw[:, cols].astype(jnp.float32)
        for b in range(1, BLOCKS):
            outs[b][:, cols] = y[b * ROWS : (b + 1) * ROWS].astype(jnp.bfloat16)


def combine(hi, lo, raw, answers):
    width = raw.shape[1] - INFO
    shapes = [jax.ShapeDtypeStruct((ROWS, width), jnp.float32)]
    shapes += [jax.ShapeDtypeStruct((ROWS, width), jnp.bfloat16)] * (BLOCKS - 1)
    return pl.pallas_call(
        combine_kernel,
        out_shape=shapes,
        compiler_params=pltpu.CompilerParams(vmem_limit_bytes=24 * 2**20),
        cost_estimate=pl.CostEstimate(
            flops=4 * BLOCKS * ROWS * SLOTS * width, bytes_accessed=4 * 2**20, transcendentals=0
        ),
        name="combine",
    )(hi, lo, raw, *answers)


def add(a, b):
    return (a.astype(jnp.float32) + b.astype(jnp.float32)).astype(jnp.bfloat16)


def body(tokens, norm_gain, route_ids, route_weight, gate_up, down):
    count = lax.axis_size("expert")
    place = lax.axis_index("expert").reshape(1)
    raw, ready = prepare(tokens, norm_gain, route_ids, route_weight)

    a = [send(ready, FAR, FAR, onward=1)]
    b = [send(ready, -FAR, -FAR, onward=1)]
    raw = send(raw, 0, 0, onward=1)
    gate_up, down, a[0], b[0] = lax.optimization_barrier((gate_up, down, a[0], b[0]))
    other_gu = send(gate_up, 0, 0, other=True)
    other_d = send(down, 0, 0, other=True)
    for _ in range(2):
        a.append(send(a[-1], FAR, FAR))
        b.append(send(b[-1], -FAR, -FAR))
    a.append(send(a[-1], FAR, FAR))

    here, up, low, far, hi, lo = dispatch(count, place, raw, norm_gain, a + b)
    far = send(far, NEAR, -NEAR)
    up = send(up, 1, 1)
    low = send(low, -1, -1)
    here, up, low, far = experts(place, [here, up, low, far], gate_up, down, other_gu, other_d)
    far = send(far, -NEAR, NEAR)
    up = send(up, -1, -1)
    low = send(low, 1, 1)
    base, a1, a2, a3, a4, b1, b2, b3 = combine(hi, lo, raw, [here, up, low, far])
    x = add(a3, send(a4, -FAR, -FAR))
    y = add(b2, send(b3, FAR, FAR))
    x = add(a2, send(x, -FAR, -FAR))
    y = add(b1, send(y, FAR, FAR))
    x = add(a1, send(x, -FAR, -FAR))
    y = send(y, FAR, FAR)
    x = send(x, -FAR, -FAR)
    out = base + x.astype(jnp.float32) + y.astype(jnp.float32)
    return out.astype(jnp.bfloat16)[None]


def solution(mesh):
    placed = (
        P("section", "expert", None),
        P(),
        P("section", "expert", None),
        P("section", "expert", None),
        P("expert", None, None),
        P("expert", None, None),
    )
    return jax.shard_map(
        body, mesh=mesh, in_specs=placed, out_specs=P("section", "expert", None), check_vma=False
    )
```

time: 226 us -> 233 us (1.031)
  waiting for transfers between devices: 57.8 us -> 92.5 us
  starting transfers between devices: 130 us -> 112 us
  other arithmetic: 9.71 us -> 0.87 us
  local copies, waits for them, and re-layouts: 4.39 us -> 11.6 us
  Pallas kernels: 21 us -> 14.1 us
    ppermute x22 -> x20, waiting for transfers between devices: 48.9 us -> 78.6 us  [send(): return lax.ppermute(value, 'expert', [(i, place(i)) for i in range(count)])]
    ppermute x22 -> x20, starting transfers between devices: 115 us -> 87.2 us  [send(): return lax.ppermute(value, 'expert', [(i, place(i)) for i in range(count)])]
    ppermute x3, starting transfers between devices: 15.6 us -> 24.8 us  [send(): return lax.ppermute(value, ('section', 'expert'), pairs)]
    unnamed x17 -> x20, local copies, waits for them, and re-layouts: 3.55 us -> 11.6 us
    ppermute x3, waiting for transfers between devices: 8.9 us -> 14 us  [send(): return lax.ppermute(value, ('section', 'expert'), pairs)]
    convert_element_type x5, other arithmetic: 4.7 us -> 0.17 us  [add(): return (a.astype(jnp.float32) + b.astype(jnp.float32)).astype(jnp.bfloat16)]
    pallas_call x1, Pallas kernels: 13.3 us -> 9.24 us  [experts(): pl.pallas_call(expert_kernel, grid_spec=pltpu.PrefetchScalarGridSpec(num_...]
    pallas_call x1, Pallas kernels: 3.72 us -> 1.24 us  [combine(): pl.pallas_call(combine_kernel, out_shape=shapes, compiler_params=pltpu.Co...]
  transfers between devices with their start and end apart: 25 -> 23, of which waited for: 11 -> 17; matrix products, arithmetic and copies ran while one was open for 5% -> 0% of each run, Pallas kernels for 2% -> 1%
where the time goes in v2:
time: 233 us; the launch traced here: 231 us
  starting transfers between devices  112 us (48%)
  waiting for transfers between devices  92.5 us (40%)
  Pallas kernels  14.1 us (6%)
  local copies, waits for them, and re-layouts  11.6 us (5%)
    ppermute x20, starting transfers between devices, send(): return lax.ppermute(value, 'expert', [(i, place(i)) for i in range(count)])  87.2 us
    ppermute x20, waiting for transfers between devices, send(): return lax.ppermute(value, 'expert', [(i, place(i)) for i in range(count)])  78.6 us
    ppermute x3, starting transfers between devices, send(): return lax.ppermute(value, ('section', 'expert'), pairs)  24.8 us
    ppermute x3, waiting for transfers between devices, send(): return lax.ppermute(value, ('section', 'expert'), pairs)  14 us
    unnamed x20, local copies, waits for them, and re-layouts  11.6 us
    pallas_call x1, Pallas kernels, experts(): pl.pallas_call(expert_kernel, grid_spec=pltpu.PrefetchScalarGridSpec(num_...  9.24 us
  transfers between devices with their start and end apart: 23, of which 17 were waited for; matrix products, arithmetic and copies ran while one was open for 0% of the time, Pallas kernels for 1%

profile of v2, /device:TPU:6, one launch (start us, length us, event | category | flops | bytes accessed | tf_op | source)
XLA Modules:
  0.0 231.5 jit_solution(6319383502711254141)
XLA Ops:
  4.0 21.0 %collective-permute-start.2 = (bf16[32,2176]{1,0:T(8,128)(2,1)S(1)}, bf16[32,2176]{1,0:T(8,128)(2,1)S(1)}, u32[]{:S(2)}, u32[]{:S(2)}) collective-permute-start(bf16[32,2176]{1,0:T(8,128)(2,1)S(1)} %get-tuple-element.30), channel_id=1, source_target_pairs={{0,120},{1,121},{2,122},{3,123},{4,124},{5,125},{6,126},{7,127},{8... | collective-permute-start | bytes 417800 | tf_op jit(solution)/shard_map/ppermute | solution.py:35
  27.0 10.2 %collective-permute-done.2.refs_4_ = bf16[32,2176]{1,0:T(8,128)(2,1)S(1)} collective-permute-done((bf16[32,2176]{1,0:T(8,128)(2,1)S(1)}, bf16[32,2176]{1,0:T(8,128)(2,1)S(1)}, u32[]{:S(2)}, u32[]{:S(2)}) %collective-permute-start.2) | collective-permute-done | bytes 139296 | tf_op jit(solution)/shard_map/ppermute | solution.py:35
  37.2 3.7 %collective-permute-done.1.refs_0_ = bf16[32,2176]{1,0:T(8,128)(2,1)S(1)} collective-permute-done((bf16[32,2176]{1,0:T(8,128)(2,1)S(1)}, bf16[32,2176]{1,0:T(8,128)(2,1)S(1)}, u32[]{:S(2)}, u32[]{:S(2)}) %collective-permute-start.1) | collective-permute-done | bytes 139296 | tf_op jit(solution)/shard_map/ppermute | solution.py:35
  42.9 2.4 %collective-permute-start.12 = (bf16[1,768,2048]{2,1,0:T(8,128)(2,1)}, bf16[1,768,2048]{2,1,0:T(8,128)(2,1)S(1)}, u32[]{:S(2)}, u32[]{:S(2)}) collective-permute-start(bf16[1,768,2048]{2,1,0:T(8,128)(2,1)} %refs_6_), channel_id=1, source_target_pairs={{0,1},{1,0},{2,3},{3,2},{4,5},{5,4},{6,7},{7,6},{8,9},{9,8},{10,11... | collective-permute-start | bytes 9437192 | tf_op jit(solution)/shard_map/ppermute | solution.py:29
  47.9 7.9 %collective-permute-start.6 = (bf16[32,2176]{1,0:T(8,128)(2,1)S(1)}, bf16[32,2176]{1,0:T(8,128)(2,1)}, u32[]{:S(2)}, u32[]{:S(2)}) collective-permute-start(bf16[32,2176]{1,0:T(8,128)(2,1)S(1)} %collective-permute-done.2.refs_4_), channel_id=1, source_target_pairs={{0,56},{1,57},{2,58},{3,59},{4,60},{5,61},{6,62},{7,63},{8,0},{9,1... | collective-permute-start | bytes 417800 | tf_op jit(solution)/shard_map/ppermute | solution.py:29
  61.5 15.9 %collective-permute-start.7 = (bf16[32,2176]{1,0:T(8,128)(2,1)}, bf16[32,2176]{1,0:T(8,128)(2,1)}, u32[]{:S(2)}, u32[]{:S(2)}) collective-permute-start(bf16[32,2176]{1,0:T(8,128)(2,1)} %collective-permute-done.6.refs_5_), channel_id=1, source_target_pairs={{0,56},{1,57},{2,58},{3,59},{4,60},{5,61},{6,62},{7,63},{8,0},{9,1... | collective-permute-start | bytes 417800 | tf_op jit(solution)/shard_map/ppermute | solution.py:29
  77.5 5.0 %collective-permute-done.4.refs_2_ = bf16[32,2176]{1,0:T(8,128)(2,1)} collective-permute-done((bf16[32,2176]{1,0:T(8,128)(2,1)S(1)}, bf16[32,2176]{1,0:T(8,128)(2,1)}, u32[]{:S(2)}, u32[]{:S(2)}) %collective-permute-start.4) | collective-permute-done | bytes 139296 | tf_op jit(solution)/shard_map/ppermute | solution.py:29
  82.4 2.3 collective-permute-start.5
  84.7 4.5 %collective-permute-done.7.refs_6_ = bf16[32,2176]{1,0:T(8,128)(2,1)} collective-permute-done((bf16[32,2176]{1,0:T(8,128)(2,1)}, bf16[32,2176]{1,0:T(8,128)(2,1)}, u32[]{:S(2)}, u32[]{:S(2)}) %collective-permute-start.7) | collective-permute-done | bytes 139296 | tf_op jit(solution)/shard_map/ppermute | solution.py:29
  89.2 7.7 %collective-permute-done.5.refs_3_ = bf16[32,2176]{1,0:T(8,128)(2,1)} collective-permute-done((bf16[32,2176]{1,0:T(8,128)(2,1)}, bf16[32,2176]{1,0:T(8,128)(2,1)}, u32[]{:S(2)}, u32[]{:S(2)}) %collective-permute-start.5) | collective-permute-done | bytes 139296 | tf_op jit(solution)/shard_map/ppermute | solution.py:29
  99.4 2.7 %dispatch.1 = (bf16[96,2048]{1,0:T(8,128)(2,1)S(1)}, bf16[96,2048]{1,0:T(8,128)(2,1)S(1)}, bf16[96,2048]{1,0:T(8,128)(2,1)S(1)}, bf16[96,2048]{1,0:T(8,128)(2,1)...) custom-call(s32[1]{0:T(128)} %bitcast.place, bf16[32,2176]{1,0:T(8,128)(2,1)S(1)} %collective-permute-done.raw, ...), custom_call_target="tpu_custom_call" | custom-call | flops 452984832 | bytes 4194304 | tf_op jit(solution)/shard_map/dispatch/pallas_call | solution.py:116
  102.1 6.3 %collective-permute-start.8 = (bf16[96,2048]{1,0:T(8,128)(2,1)S(1)}, bf16[96,2048]{1,0:T(8,128)(2,1)S(1)}, u32[]{:S(2)}, u32[]{:S(2)}) collective-permute-start(bf16[96,2048]{1,0:T(8,128)(2,1)S(1)} %get-tuple-element.36), channel_id=1, source_target_pairs={{0,2},{1,3},{2,4},{3,5},{4,6},{5,7},{6,8},{7,9},{8,10},{9,11},{10,... | collective-permute-start | bytes 1179656 | tf_op jit(solution)/shard_map/ppermute | solution.py:29
  110.3 3.4 %collective-permute-start.10 = (bf16[96,2048]{1,0:T(8,128)(2,1)S(1)}, bf16[96,2048]{1,0:T(8,128)(2,1)S(1)}, u32[]{:S(2)}, u32[]{:S(2)}) collective-permute-start(bf16[96,2048]{1,0:T(8,128)(2,1)S(1)} %get-tuple-element.38), channel_id=1, source_target_pairs={{0,4},{1,61},{2,6},{3,63},{4,8},{5,1},{6,10},{7,3},{8,12},{9,5},{1... | collective-permute-start | bytes 1179656 | tf_op jit(solution)/shard_map/ppermute | solution.py:29
  113.7 3.2 %collective-permute-done.8.refs_1_ = bf16[96,2048]{1,0:T(8,128)(2,1)S(1)} collective-permute-done((bf16[96,2048]{1,0:T(8,128)(2,1)S(1)}, bf16[96,2048]{1,0:T(8,128)(2,1)S(1)}, u32[]{:S(2)}, u32[]{:S(2)}) %collective-permute-start.8) | collective-permute-done | bytes 393248 | tf_op jit(solution)/shard_map/ppermute | solution.py:29
  116.9 5.4 %collective-permute-done.9.refs_2_ = bf16[96,2048]{1,0:T(8,128)(2,1)S(1)} collective-permute-done((bf16[96,2048]{1,0:T(8,128)(2,1)S(1)}, bf16[96,2048]{1,0:T(8,128)(2,1)S(1)}, u32[]{:S(2)}, u32[]{:S(2)}) %collective-permute-start.9) | collective-permute-done | bytes 393248 | tf_op jit(solution)/shard_map/ppermute | solution.py:29
  122.3 2.4 %collective-permute-done.10.refs_3_ = bf16[96,2048]{1,0:T(8,128)(2,1)S(1)} collective-permute-done((bf16[96,2048]{1,0:T(8,128)(2,1)S(1)}, bf16[96,2048]{1,0:T(8,128)(2,1)S(1)}, u32[]{:S(2)}, u32[]{:S(2)}) %collective-permute-start.10) | collective-permute-done | bytes 393248 | tf_op jit(solution)/shard_map/ppermute | solution.py:29
  124.8 2.8 %copy-done = bf16[1,2048,1536]{2,1,0:T(8,128)(2,1)S(1)} copy-done((bf16[1,2048,1536]{2,1,0:T(8,128)(2,1)S(1)}, bf16[1,2048,1536]{2,1,0:T(8,128)(2,1)}, u32[]{:S(2)}) %copy-start) | copy-done | bytes 6291480
  129.4 9.2 %experts.1 = (bf16[96,2048]{1,0:T(8,128)(2,1)S(1)}, bf16[96,2048]{1,0:T(8,128)(2,1)S(1)}, bf16[96,2048]{1,0:T(8,128)(2,1)S(1)}, bf16[96,2048]{1,0:T(8,128)(2,1)S(1)}) custom-call(s32[1]{0:T(128)} %bitcast.place, bf16[96,2048]{1,0:T(8,128)(2,1)S(1)} %get-tuple-element.35.refs_0_, bf16[96,2048]{1,0:T(8,128)(2,1)S(1)} %collective-permute-done.8.refs_1_, ...), custom_call_target="tpu_custom_call" | custom-call | flops 3623878656 | bytes 18874368 | tf_op jit(solution)/shard_map/experts/pallas_call | solution.py:189
  138.7 5.4 %collective-permute-start.13 = (bf16[96,2048]{1,0:T(8,128)(2,1)S(1)}, bf16[96,2048]{1,0:T(8,128)(2,1)S(1)}, u32[]{:S(2)}, u32[]{:S(2)}) collective-permute-start(bf16[96,2048]{1,0:T(8,128)(2,1)S(1)} %get-tuple-element.42), channel_id=1, source_target_pairs={{0,62},{1,63},{2,0},{3,1},{4,2},{5,3},{6,4},{7,5},{8,6},{9,7},{10,... | collective-permute-start | bytes 1179656 | tf_op jit(solution)/shard_map/ppermute | solution.py:29
  146.0 4.3 %collective-permute-start.15 = (bf16[96,2048]{1,0:T(8,128)(2,1)S(1)}, bf16[96,2048]{1,0:T(8,128)(2,1)S(1)}, u32[]{:S(2)}, u32[]{:S(2)}) collective-permute-start(bf16[96,2048]{1,0:T(8,128)(2,1)S(1)} %get-tuple-element.44), channel_id=1, source_target_pairs={{0,60},{1,5},{2,62},{3,7},{4,0},{5,9},{6,2},{7,11},{8,4},{9,13},{1... | collective-permute-start | bytes 1179656 | tf_op jit(solution)/shard_map/ppermute | solution.py:29
  151.1 5.5 %collective-permute-done.14.refs_2_ = bf16[96,2048]{1,0:T(8,128)(2,1)S(1)} collective-permute-done((bf16[96,2048]{1,0:T(8,128)(2,1)S(1)}, bf16[96,2048]{1,0:T(8,128)(2,1)S(1)}, u32[]{:S(2)}, u32[]{:S(2)}) %collective-permute-start.14) | collective-permute-done | bytes 393248 | tf_op jit(solution)/shard_map/ppermute | solution.py:29
  156.6 6.9 %collective-permute-done.15.refs_3_ = bf16[96,2048]{1,0:T(8,128)(2,1)S(1)} collective-permute-done((bf16[96,2048]{1,0:T(8,128)(2,1)S(1)}, bf16[96,2048]{1,0:T(8,128)(2,1)S(1)}, u32[]{:S(2)}, u32[]{:S(2)}) %collective-permute-start.15) | collective-permute-done | bytes 393248 | tf_op jit(solution)/shard_map/ppermute | solution.py:29
  164.7 5.6 %collective-permute-start.16 = (bf16[32,2048]{1,0:T(8,128)(2,1)S(1)}, bf16[32,2048]{1,0:T(8,128)(2,1)S(1)}, u32[]{:S(2)}, u32[]{:S(2)}) collective-permute-start(bf16[32,2048]{1,0:T(8,128)(2,1)S(1)} %get-tuple-element.49), channel_id=1, source_target_pairs={{0,56},{1,57},{2,58},{3,59},{4,60},{5,61},{6,62},{7,63},{8,0},{9,1... | collective-permute-start | bytes 393224 | tf_op jit(solution)/shard_map/ppermute | solution.py:29
  170.4 4.1 %collective-permute-start.20 = (bf16[32,2048]{1,0:T(8,128)(2,1)S(1)}, bf16[32,2048]{1,0:T(8,128)(2,1)S(1)}, u32[]{:S(2)}, u32[]{:S(2)}) collective-permute-start(bf16[32,2048]{1,0:T(8,128)(2,1)S(1)} %get-tuple-element.52), channel_id=1, source_target_pairs={{0,8},{1,9},{2,10},{3,11},{4,12},{5,13},{6,14},{7,15},{8,16},{9,17... | collective-permute-start | bytes 393224 | tf_op jit(solution)/shard_map/ppermute | solution.py:29
  174.5 7.2 %collective-permute-done.16 = bf16[32,2048]{1,0:T(8,128)(2,1)S(1)} collective-permute-done((bf16[32,2048]{1,0:T(8,128)(2,1)S(1)}, bf16[32,2048]{1,0:T(8,128)(2,1)S(1)}, u32[]{:S(2)}, u32[]{:S(2)}) %collective-permute-start.16) | collective-permute-done | bytes 131104 | tf_op jit(solution)/shard_map/ppermute | solution.py:29
  181.8 3.7 %collective-permute-start.17 = (bf16[32,2048]{1,0:T(8,128)(2,1)S(1)}, bf16[32,2048]{1,0:T(8,128)(2,1)S(1)}, u32[]{:S(2)}, u32[]{:S(2)}) collective-permute-start(bf16[32,2048]{1,0:T(8,128)(2,1)S(1)} %add_convert_fusion.5), channel_id=1, source_target_pairs={{0,56},{1,57},{2,58},{3,59},{4,60},{5,61},{6,62},{7,63},{8,0},{9,1... | collective-permute-start | bytes 393224 | tf_op jit(solution)/shard_map/ppermute | solution.py:29
  185.4 2.2 collective-permute-done.20
  187.7 4.8 %collective-permute-start.21 = (bf16[32,2048]{1,0:T(8,128)(2,1)S(1)}, bf16[32,2048]{1,0:T(8,128)(2,1)S(1)}, u32[]{:S(2)}, u32[]{:S(2)}) collective-permute-start(bf16[32,2048]{1,0:T(8,128)(2,1)S(1)} %add_convert_fusion.2), channel_id=1, source_target_pairs={{0,8},{1,9},{2,10},{3,11},{4,12},{5,13},{6,14},{7,15},{8,16},{9,17... | collective-permute-start | bytes 393224 | tf_op jit(solution)/shard_map/ppermute | solution.py:29
  192.5 9.0 %collective-permute-done.17 = bf16[32,2048]{1,0:T(8,128)(2,1)S(1)} collective-permute-done((bf16[32,2048]{1,0:T(8,128)(2,1)S(1)}, bf16[32,2048]{1,0:T(8,128)(2,1)S(1)}, u32[]{:S(2)}, u32[]{:S(2)}) %collective-permute-start.17) | collective-permute-done | bytes 131104 | tf_op jit(solution)/shard_map/ppermute | solution.py:29
  203.6 7.8 %collective-permute-start.22 = (bf16[32,2048]{1,0:T(8,128)(2,1)S(1)}, bf16[32,2048]{1,0:T(8,128)(2,1)S(1)}, u32[]{:S(2)}, u32[]{:S(2)}) collective-permute-start(bf16[32,2048]{1,0:T(8,128)(2,1)S(1)} %add_convert_fusion.1), channel_id=1, source_target_pairs={{0,8},{1,9},{2,10},{3,11},{4,12},{5,13},{6,14},{7,15},{8,16},{9,17... | collective-permute-start | bytes 393224 | tf_op jit(solution)/shard_map/ppermute | solution.py:29
  211.4 8.6 %collective-permute-done.18 = bf16[32,2048]{1,0:T(8,128)(2,1)S(1)} collective-permute-done((bf16[32,2048]{1,0:T(8,128)(2,1)S(1)}, bf16[32,2048]{1,0:T(8,128)(2,1)S(1)}, u32[]{:S(2)}, u32[]{:S(2)}) %collective-permute-start.18) | collective-permute-done | bytes 131104 | tf_op jit(solution)/shard_map/ppermute | solution.py:29
  222.0 8.8 %collective-permute-done.19 = bf16[32,2048]{1,0:T(8,128)(2,1)S(1)} collective-permute-done((bf16[32,2048]{1,0:T(8,128)(2,1)S(1)}, bf16[32,2048]{1,0:T(8,128)(2,1)S(1)}, u32[]{:S(2)}, u32[]{:S(2)}) %collective-permute-start.19) | collective-permute-done | bytes 131104 | tf_op jit(solution)/shard_map/ppermute | solution.py:29
  (44 shorter events, 31.2 us)
Async XLA Ops:
  1.5 0.9 copy-start.2
  2.4 0.7 copy-start.3
  4.0 33.2 %collective-permute-start.2 = (bf16[32,2176]{1,0:T(8,128)(2,1)S(1)}, bf16[32,2176]{1,0:T(8,128)(2,1)S(1)}, u32[]{:S(2)}, u32[]{:S(2)}) collective-permute-start(bf16[32,2176]{1,0:T(8,128)(2,1)S(1)} %get-tuple-element.30), channel_id=1, source_target_pairs={{0,120},{1,121},{2,122},{3,123},{4,124},{5,125},{6,126},{7,127},{8... | collective-permute-start | bytes 417800 | tf_op jit(solution)/shard_map/ppermute | solution.py:35
  25.0 15.9 %collective-permute-start.1 = (bf16[32,2176]{1,0:T(8,128)(2,1)S(1)}, bf16[32,2176]{1,0:T(8,128)(2,1)S(1)}, u32[]{:S(2)}, u32[]{:S(2)}) collective-permute-start(bf16[32,2176]{1,0:T(8,128)(2,1)S(1)} %get-tuple-element.30), channel_id=1, source_target_pairs={{0,72},{1,73},{2,74},{3,75},{4,76},{5,77},{6,78},{7,79},{8,80},{9,... | collective-permute-start | bytes 417800 | tf_op jit(solution)/shard_map/ppermute | solution.py:35
  40.9 83.8 %collective-permute-start.11 = (bf16[1,2048,1536]{2,1,0:T(8,128)(2,1)}, bf16[1,2048,1536]{2,1,0:T(8,128)(2,1)}, u32[]{:S(2)}, u32[]{:S(2)}) collective-permute-start(bf16[1,2048,1536]{2,1,0:T(8,128)(2,1)} %refs_5_), channel_id=1, source_target_pairs={{0,1},{1,0},{2,3},{3,2},{4,5},{5,4},{6,7},{7,6},{8,9},{9,8},{10,11... | collective-permute-start | bytes 18874376 | tf_op jit(solution)/shard_map/ppermute | solution.py:29
  42.9 81.9 %collective-permute-start.12 = (bf16[1,768,2048]{2,1,0:T(8,128)(2,1)}, bf16[1,768,2048]{2,1,0:T(8,128)(2,1)S(1)}, u32[]{:S(2)}, u32[]{:S(2)}) collective-permute-start(bf16[1,768,2048]{2,1,0:T(8,128)(2,1)} %refs_6_), channel_id=1, source_target_pairs={{0,1},{1,0},{2,3},{3,2},{4,5},{5,4},{6,7},{7,6},{8,9},{9,8},{10,11... | collective-permute-start | bytes 9437192 | tf_op jit(solution)/shard_map/ppermute | solution.py:29
  45.3 11.8 %collective-permute-start.3 = (bf16[32,2176]{1,0:T(8,128)(2,1)S(1)}, bf16[32,2176]{1,0:T(8,128)(2,1)S(1)}, u32[]{:S(2)}, u32[]{:S(2)}) collective-permute-start(bf16[32,2176]{1,0:T(8,128)(2,1)S(1)} %collective-permute-done.1.refs_0_), channel_id=1, source_target_pairs={{0,8},{1,9},{2,10},{3,11},{4,12},{5,13},{6,14},{7,15},{8,16},{9,17... | collective-permute-start | bytes 417800 | tf_op jit(solution)/shard_map/ppermute | solution.py:29
  47.2 0.7 copy-start.5
  47.9 13.7 %collective-permute-start.6 = (bf16[32,2176]{1,0:T(8,128)(2,1)S(1)}, bf16[32,2176]{1,0:T(8,128)(2,1)}, u32[]{:S(2)}, u32[]{:S(2)}) collective-permute-start(bf16[32,2176]{1,0:T(8,128)(2,1)S(1)} %collective-permute-done.2.refs_4_), channel_id=1, source_target_pairs={{0,56},{1,57},{2,58},{3,59},{4,60},{5,61},{6,62},{7,63},{8,0},{9,1... | collective-permute-start | bytes 417800 | tf_op jit(solution)/shard_map/ppermute | solution.py:29
  57.0 25.4 %collective-permute-start.4 = (bf16[32,2176]{1,0:T(8,128)(2,1)S(1)}, bf16[32,2176]{1,0:T(8,128)(2,1)}, u32[]{:S(2)}, u32[]{:S(2)}) collective-permute-start(bf16[32,2176]{1,0:T(8,128)(2,1)S(1)} %collective-permute-done.3.refs_1_), channel_id=1, source_target_pairs={{0,8},{1,9},{2,10},{3,11},{4,12},{5,13},{6,14},{7,15},{8,16},{9,17... | collective-permute-start | bytes 417800 | tf_op jit(solution)/shard_map/ppermute | solution.py:29
  59.0 0.6 copy-start.7
  59.6 25.1 %collective-permute-start = (bf16[32,2176]{1,0:T(8,128)(2,1)}, bf16[32,2176]{1,0:T(8,128)(2,1)S(1)}, u32[]{:S(2)}, u32[]{:S(2)}) collective-permute-start(bf16[32,2176]{1,0:T(8,128)(2,1)} %get-tuple-element.29), channel_id=1, source_target_pairs={{0,64},{1,65},{2,66},{3,67},{4,68},{5,69},{6,70},{7,71},{8,72},{9,... | collective-permute-start | bytes 417800 | tf_op jit(solution)/shard_map/ppermute | solution.py:35
  61.5 27.7 %collective-permute-start.7 = (bf16[32,2176]{1,0:T(8,128)(2,1)}, bf16[32,2176]{1,0:T(8,128)(2,1)}, u32[]{:S(2)}, u32[]{:S(2)}) collective-permute-start(bf16[32,2176]{1,0:T(8,128)(2,1)} %collective-permute-done.6.refs_5_), channel_id=1, source_target_pairs={{0,56},{1,57},{2,58},{3,59},{4,60},{5,61},{6,62},{7,63},{8,0},{9,1... | collective-permute-start | bytes 417800 | tf_op jit(solution)/shard_map/ppermute | solution.py:29
  82.4 14.4 %collective-permute-start.5 = (bf16[32,2176]{1,0:T(8,128)(2,1)}, bf16[32,2176]{1,0:T(8,128)(2,1)}, u32[]{:S(2)}, u32[]{:S(2)}) collective-permute-start(bf16[32,2176]{1,0:T(8,128)(2,1)} %collective-permute-done.4.refs_2_), channel_id=1, source_target_pairs={{0,8},{1,9},{2,10},{3,11},{4,12},{5,13},{6,14},{7,15},{8,16},{9,17... | collective-permute-start | bytes 417800 | tf_op jit(solution)/shard_map/ppermute | solution.py:29
  96.9 0.7 copy-start.4
  97.6 0.9 copy-start.6
  98.5 0.9 copy-start.8
  102.1 14.8 %collective-permute-start.8 = (bf16[96,2048]{1,0:T(8,128)(2,1)S(1)}, bf16[96,2048]{1,0:T(8,128)(2,1)S(1)}, u32[]{:S(2)}, u32[]{:S(2)}) collective-permute-start(bf16[96,2048]{1,0:T(8,128)(2,1)S(1)} %get-tuple-element.36), channel_id=1, source_target_pairs={{0,2},{1,3},{2,4},{3,5},{4,6},{5,7},{6,8},{7,9},{8,10},{9,11},{10,... | collective-permute-start | bytes 1179656 | tf_op jit(solution)/shard_map/ppermute | solution.py:29
  108.4 13.9 %collective-permute-start.9 = (bf16[96,2048]{1,0:T(8,128)(2,1)S(1)}, bf16[96,2048]{1,0:T(8,128)(2,1)S(1)}, u32[]{:S(2)}, u32[]{:S(2)}) collective-permute-start(bf16[96,2048]{1,0:T(8,128)(2,1)S(1)} %get-tuple-element.37), channel_id=1, source_target_pairs={{0,62},{1,63},{2,0},{3,1},{4,2},{5,3},{6,4},{7,5},{8,6},{9,7},{10,... | collective-permute-start | bytes 1179656 | tf_op jit(solution)/shard_map/ppermute | solution.py:29
  110.3 14.4 %collective-permute-start.10 = (bf16[96,2048]{1,0:T(8,128)(2,1)S(1)}, bf16[96,2048]{1,0:T(8,128)(2,1)S(1)}, u32[]{:S(2)}, u32[]{:S(2)}) collective-permute-start(bf16[96,2048]{1,0:T(8,128)(2,1)S(1)} %get-tuple-element.38), channel_id=1, source_target_pairs={{0,4},{1,61},{2,6},{3,63},{4,8},{5,1},{6,10},{7,3},{8,12},{9,5},{1... | collective-permute-start | bytes 1179656 | tf_op jit(solution)/shard_map/ppermute | solution.py:29
  124.8 2.8 %copy-start = (bf16[1,2048,1536]{2,1,0:T(8,128)(2,1)S(1)}, bf16[1,2048,1536]{2,1,0:T(8,128)(2,1)}, u32[]{:S(2)}) copy-start(bf16[1,2048,1536]{2,1,0:T(8,128)(2,1)} %refs_5_) | copy-start | bytes 18874372
  127.5 1.9 copy-start.1
  138.7 12.5 %collective-permute-start.13 = (bf16[96,2048]{1,0:T(8,128)(2,1)S(1)}, bf16[96,2048]{1,0:T(8,128)(2,1)S(1)}, u32[]{:S(2)}, u32[]{:S(2)}) collective-permute-start(bf16[96,2048]{1,0:T(8,128)(2,1)S(1)} %get-tuple-element.42), channel_id=1, source_target_pairs={{0,62},{1,63},{2,0},{3,1},{4,2},{5,3},{6,4},{7,5},{8,6},{9,7},{10,... | collective-permute-start | bytes 1179656 | tf_op jit(solution)/shard_map/ppermute | solution.py:29
  144.1 12.5 %collective-permute-start.14 = (bf16[96,2048]{1,0:T(8,128)(2,1)S(1)}, bf16[96,2048]{1,0:T(8,128)(2,1)S(1)}, u32[]{:S(2)}, u32[]{:S(2)}) collective-permute-start(bf16[96,2048]{1,0:T(8,128)(2,1)S(1)} %get-tuple-element.43), channel_id=1, source_target_pairs={{0,2},{1,3},{2,4},{3,5},{4,6},{5,7},{6,8},{7,9},{8,10},{9,11},{10,... | collective-permute-start | bytes 1179656 | tf_op jit(solution)/shard_map/ppermute | solution.py:29
  146.0 17.4 %collective-permute-start.15 = (bf16[96,2048]{1,0:T(8,128)(2,1)S(1)}, bf16[96,2048]{1,0:T(8,128)(2,1)S(1)}, u32[]{:S(2)}, u32[]{:S(2)}) collective-permute-start(bf16[96,2048]{1,0:T(8,128)(2,1)S(1)} %get-tuple-element.44), channel_id=1, source_target_pairs={{0,60},{1,5},{2,62},{3,7},{4,0},{5,9},{6,2},{7,11},{8,4},{9,13},{1... | collective-permute-start | bytes 1179656 | tf_op jit(solution)/shard_map/ppermute | solution.py:29
  164.7 17.0 %collective-permute-start.16 = (bf16[32,2048]{1,0:T(8,128)(2,1)S(1)}, bf16[32,2048]{1,0:T(8,128)(2,1)S(1)}, u32[]{:S(2)}, u32[]{:S(2)}) collective-permute-start(bf16[32,2048]{1,0:T(8,128)(2,1)S(1)} %get-tuple-element.49), channel_id=1, source_target_pairs={{0,56},{1,57},{2,58},{3,59},{4,60},{5,61},{6,62},{7,63},{8,0},{9,1... | collective-permute-start | bytes 393224 | tf_op jit(solution)/shard_map/ppermute | solution.py:29
  170.4 17.3 %collective-permute-start.20 = (bf16[32,2048]{1,0:T(8,128)(2,1)S(1)}, bf16[32,2048]{1,0:T(8,128)(2,1)S(1)}, u32[]{:S(2)}, u32[]{:S(2)}) collective-permute-start(bf16[32,2048]{1,0:T(8,128)(2,1)S(1)} %get-tuple-element.52), channel_id=1, source_target_pairs={{0,8},{1,9},{2,10},{3,11},{4,12},{5,13},{6,14},{7,15},{8,16},{9,17... | collective-permute-start | bytes 393224 | tf_op jit(solution)/shard_map/ppermute | solution.py:29
  181.8 19.8 %collective-permute-start.17 = (bf16[32,2048]{1,0:T(8,128)(2,1)S(1)}, bf16[32,2048]{1,0:T(8,128)(2,1)S(1)}, u32[]{:S(2)}, u32[]{:S(2)}) collective-permute-start(bf16[32,2048]{1,0:T(8,128)(2,1)S(1)} %add_convert_fusion.5), channel_id=1, source_target_pairs={{0,56},{1,57},{2,58},{3,59},{4,60},{5,61},{6,62},{7,63},{8,0},{9,1... | collective-permute-start | bytes 393224 | tf_op jit(solution)/shard_map/ppermute | solution.py:29
  187.7 15.8 %collective-permute-start.21 = (bf16[32,2048]{1,0:T(8,128)(2,1)S(1)}, bf16[32,2048]{1,0:T(8,128)(2,1)S(1)}, u32[]{:S(2)}, u32[]{:S(2)}) collective-permute-start(bf16[32,2048]{1,0:T(8,128)(2,1)S(1)} %add_convert_fusion.2), channel_id=1, source_target_pairs={{0,8},{1,9},{2,10},{3,11},{4,12},{5,13},{6,14},{7,15},{8,16},{9,17... | collective-permute-start | bytes 393224 | tf_op jit(solution)/shard_map/ppermute | solution.py:29
  201.6 18.4 %collective-permute-start.18 = (bf16[32,2048]{1,0:T(8,128)(2,1)S(1)}, bf16[32,2048]{1,0:T(8,128)(2,1)S(1)}, u32[]{:S(2)}, u32[]{:S(2)}) collective-permute-start(bf16[32,2048]{1,0:T(8,128)(2,1)S(1)} %add_convert_fusion.4), channel_id=1, source_target_pairs={{0,56},{1,57},{2,58},{3,59},{4,60},{5,61},{6,62},{7,63},{8,0},{9,1... | collective-permute-start | bytes 393224 | tf_op jit(solution)/shard_map/ppermute | solution.py:29
  203.6 18.4 %collective-permute-start.22 = (bf16[32,2048]{1,0:T(8,128)(2,1)S(1)}, bf16[32,2048]{1,0:T(8,128)(2,1)S(1)}, u32[]{:S(2)}, u32[]{:S(2)}) collective-permute-start(bf16[32,2048]{1,0:T(8,128)(2,1)S(1)} %add_convert_fusion.1), channel_id=1, source_target_pairs={{0,8},{1,9},{2,10},{3,11},{4,12},{5,13},{6,14},{7,15},{8,16},{9,17... | collective-permute-start | bytes 393224 | tf_op jit(solution)/shard_map/ppermute | solution.py:29
  220.0 10.8 %collective-permute-start.19 = (bf16[32,2048]{1,0:T(8,128)(2,1)S(1)}, bf16[32,2048]{1,0:T(8,128)(2,1)S(1)}, u32[]{:S(2)}, u32[]{:S(2)}) collective-permute-start(bf16[32,2048]{1,0:T(8,128)(2,1)S(1)} %add_convert_fusion.3), channel_id=1, source_target_pairs={{0,56},{1,57},{2,58},{3,59},{4,60},{5,61},{6,62},{7,63},{8,0},{9,1... | collective-permute-start | bytes 393224 | tf_op jit(solution)/shard_map/ppermute | solution.py:29

commit v3 on v2

v3 whole, which is shorter than its diff:
```python
import functools

import jax
import jax.numpy as jnp
from jax import lax
from jax.experimental import pallas as pl
from jax.experimental.pallas import tpu as pltpu
from jax.sharding import PartitionSpec as P

CAP = 6
ROWS = 32
INFO = 128
FAR = 4
NEAR = FAR // 2
BLOCKS = 8
SEG = BLOCKS * CAP
SLOTS = 8 * SEG
TILES = 3


def send(value, up, down, other=False, onward=0):
    count, sections = lax.axis_size("expert"), lax.axis_size("section")

    def place(i):
        core = 1 - i % 2 if other else i % 2
        return ((i // 2 + (down if i % 2 else up)) * 2) % count + core

    if not onward:
        return lax.ppermute(value, "expert", [(i, place(i)) for i in range(count)])
    pairs = [
        (s * count + i, (s + onward) % sections * count + place(i))
        for s in range(sections)
        for i in range(count)
    ]
    return lax.ppermute(value, ("section", "expert"), pairs)


def prepare_kernel(tokens, gain, ids, weights, ready):
    width = tokens.shape[2]
    values = tokens[0].astype(jnp.float32)
    scale = lax.rsqrt(jnp.mean(values * values, axis=1, keepdims=True) + 1e-06)
    share = weights[0] / jnp.sum(weights[0], axis=1, keepdims=True)
    hi = share.astype(jnp.bfloat16).astype(jnp.float32)
    lo = share - hi
    named = ids[0].astype(jnp.float32)
    lane = lax.broadcasted_iota(jnp.int32, (ROWS, INFO), 1)
    info = jnp.zeros((ROWS, INFO), jnp.float32)
    for k in range(8):
        info = jnp.where(lane == k, named[:, k : k + 1], info)
        info = jnp.where(lane == 8 + k, hi[:, k : k + 1], info)
        info = jnp.where(lane == 16 + k, lo[:, k : k + 1], info)
    info = info.astype(jnp.bfloat16)
    ready[:, :width] = (values * scale * gain[...]).astype(jnp.bfloat16)
    ready[:, width:] = info


def prepare(tokens, gain, ids, weights):
    shape = jax.ShapeDtypeStruct((ROWS, tokens.shape[2] + INFO), jnp.bfloat16)
    return pl.pallas_call(
        prepare_kernel,
        out_shape=shape,
        compiler_params=pltpu.CompilerParams(vmem_limit_bytes=56 * 2**20),
        name="prepare",
    )(tokens, gain.reshape(1, -1), ids, weights)


def dispatch_kernel(count, place, *refs):
    blocks = refs[:BLOCKS]
    *outs, hi_ref, lo_ref = refs[BLOCKS:]
    width = outs[0].shape[1]
    rows = BLOCKS * ROWS
    chip = place[0] >> 1
    info = jnp.concatenate([b[:, width:] for b in blocks], axis=0).astype(jnp.float32)
    group = lax.broadcasted_iota(jnp.int32, (1, SLOTS), 1) // SEG
    offset = jnp.where(group < 4, group, jnp.where(group < 6, group - 6, jnp.where(group == 6, 4, -3)))
    expert = 2 * chip + offset
    expert = jnp.where(expert < 0, expert + count, expert)
    expert = jnp.where(expert >= count, expert - count, expert).astype(jnp.float32)
    member = jnp.zeros((rows, SLOTS), jnp.float32)
    hi = jnp.zeros((rows, SLOTS), jnp.float32)
    lo = jnp.zeros((rows, SLOTS), jnp.float32)
    for k in range(8):
        same = info[:, k : k + 1] == expert
        member = jnp.where(same, 1.0, member)
        hi = jnp.where(same, info[:, 8 + k : 9 + k], hi)
        lo = jnp.where(same, info[:, 16 + k : 17 + k], lo)
    r = lax.broadcasted_iota(jnp.int32, (rows, rows), 0)
    c = lax.broadcasted_iota(jnp.int32, (rows, rows), 1)
    before = jnp.where((c < r) & (c // ROWS == r // ROWS), 1.0, 0.0).astype(jnp.bfloat16)
    rank = jnp.dot(before, member.astype(jnp.bfloat16), preferred_element_type=jnp.float32)
    row_block = lax.broadcasted_iota(jnp.int32, (rows, SLOTS), 0) // ROWS
    q = lax.broadcasted_iota(jnp.int32, (1, SLOTS), 1) % SEG
    taken = (member > 0.5) & (rank == (q % CAP).astype(jnp.float32)) & (q // CAP == row_block)
    hi_ref[...] = jnp.where(taken, hi, 0.0).astype(jnp.bfloat16)
    lo_ref[...] = jnp.where(taken, lo, 0.0).astype(jnp.bfloat16)
    pick = jnp.where(taken, 1.0, 0.0).astype(jnp.bfloat16)
    step = min(512, width)
    for at in range(0, width, step):
        cols = slice(at, at + step)
        x = jnp.concatenate([b[:, cols] for b in blocks], axis=0)
        y = lax.dot_general(pick, x, (((0,), (0,)), ((), ())), preferred_element_type=jnp.float32)
        y = y.astype(jnp.bfloat16)
        first = 0
        for out in outs:
            out[:, cols] = y[first : first + out.shape[0]]
            first += out.shape[0]


def dispatch(count, place, blocks):
    rows, width = BLOCKS * ROWS, blocks[0].shape[1] - INFO
    vmem = pl.BlockSpec(memory_space=pltpu.VMEM)
    shapes = [(n * SEG, width) for n in (2, 2, 2, 1, 1)] + [(rows, SLOTS)] * 2
    return pl.pallas_call(
        functools.partial(dispatch_kernel, count),
        in_specs=[pl.BlockSpec(memory_space=pltpu.SMEM)] + [vmem] * BLOCKS,
        out_shape=[jax.ShapeDtypeStruct(shape, jnp.bfloat16) for shape in shapes],
        compiler_params=pltpu.CompilerParams(vmem_limit_bytes=24 * 2**20),
        cost_estimate=pl.CostEstimate(
            flops=2 * rows * SLOTS * (width + rows), bytes_accessed=4 * 2**20, transcendentals=0
        ),
        name="dispatch",
    )(place, *blocks)


def expert_kernel(n, place, *refs):
    ins, (g0, u0, d0, g1, u1, d1) = refs[:n], refs[n : n + 6]
    outs, (x, acc) = refs[n + 6 : 2 * n + 6], refs[2 * n + 6 :]
    i = pl.program_id(0)
    turn, tile = i // TILES, i % TILES
    core = place[0] & 1
    which = jnp.where(turn == 0, core, 1 - core)

    def parts(pieces, e):
        found = [piece.at[e * SEG : (e + 1) * SEG] for piece in pieces if piece.shape[0] == 2 * SEG]
        single = [piece for piece in pieces if piece.shape[0] == SEG]
        return found + single[e : e + 1]

    for e in range(2):
        @pl.when((tile == 0) & (which == e))
        def _():
            for at, piece in enumerate(parts(ins, e)):
                x[at * SEG : (at + 1) * SEG] = piece[...]

    def work(g, u, d):
        gate = jnp.dot(x[...], g[0], preferred_element_type=jnp.float32)
        lift = jnp.dot(x[...], u[0], preferred_element_type=jnp.float32)
        hidden = (gate / (1.0 + jnp.exp(-gate)) * lift).astype(jnp.bfloat16)
        y = jnp.dot(hidden, d[0], preferred_element_type=jnp.float32)

        @pl.when(tile == 0)
        def _():
            acc[...] = y

        @pl.when(tile > 0)
        def _():
            acc[...] += y

    @pl.when(turn == 0)
    def _():
        work(g0, u0, d0)

    @pl.when(turn == 1)
    def _():
        work(g1, u1, d1)

    for e in range(2):
        @pl.when((tile == TILES - 1) & (which == e))
        def _():
            for at, piece in enumerate(parts(outs, e)):
                piece[...] = acc[at * SEG : (at + 1) * SEG].astype(jnp.bfloat16)


def experts(place, pieces, own_gu, own_d, other_gu, other_d):
    width, hid = own_gu.shape[1], own_d.shape[1]
    tile = hid // TILES
    rows = sum(p.shape[0] for p in pieces) // 2
    whole = [pl.BlockSpec(p.shape, lambda i, c: (0, 0)) for p in pieces]

    def early(i):
        return jnp.minimum(i, TILES - 1)

    def late(i):
        return jnp.maximum(i - TILES, 0)

    def weights(at):
        return [
            pl.BlockSpec((1, width, tile), lambda i, c: (0, 0, at(i))),
            pl.BlockSpec((1, width, tile), lambda i, c: (0, 0, at(i) + TILES)),
            pl.BlockSpec((1, tile, width), lambda i, c: (0, at(i), 0)),
        ]

    return pl.pallas_call(
        functools.partial(expert_kernel, len(pieces)),
        grid_spec=pltpu.PrefetchScalarGridSpec(
            num_scalar_prefetch=1,
            grid=(2 * TILES,),
            in_specs=whole + weights(early) + weights(late),
            out_specs=whole,
            scratch_shapes=[
                pltpu.VMEM((rows, width), jnp.bfloat16),
                pltpu.VMEM((rows, width), jnp.float32),
            ],
        ),
        out_shape=[jax.ShapeDtypeStruct(p.shape, jnp.bfloat16) for p in pieces],
        compiler_params=pltpu.CompilerParams(vmem_limit_bytes=32 * 2**20),
        cost_estimate=pl.CostEstimate(
            flops=2 * 2 * rows * 3 * width * hid,
            bytes_accessed=2 * 3 * 2 * width * hid,
            transcendentals=2 * rows * hid,
        ),
        name="experts",
    )(place, *pieces, own_gu, own_gu, own_d, other_gu, other_gu, other_d)


def combine_kernel(hi, lo, tokens, *refs):
    answers, outs = refs[:5], refs[5:]
    width = outs[0].shape[1]
    step = min(512, width)
    for at in range(0, width, step):
        cols = slice(at, at + step)
        a = jnp.concatenate([r[:, cols] for r in answers], axis=0)
        y = jnp.dot(hi[...], a, preferred_element_type=jnp.float32)
        y = y + jnp.dot(lo[...], a, preferred_element_type=jnp.float32)
        outs[0][:, cols] = y[:ROWS] + tokens[0, :, cols].astype(jnp.float32)
        for b in range(1, BLOCKS):
            outs[b][:, cols] = y[b * ROWS : (b + 1) * ROWS].astype(jnp.bfloat16)


def combine(hi, lo, tokens, answers):
    width = tokens.shape[2]
    shapes = [jax.ShapeDtypeStruct((ROWS, width), jnp.float32)]
    shapes += [jax.ShapeDtypeStruct((ROWS, width), jnp.bfloat16)] * (BLOCKS - 1)
    return pl.pallas_call(
        combine_kernel,
        out_shape=shapes,
        compiler_params=pltpu.CompilerParams(vmem_limit_bytes=24 * 2**20),
        cost_estimate=pl.CostEstimate(
            flops=4 * BLOCKS * ROWS * SLOTS * width, bytes_accessed=4 * 2**20, transcendentals=0
        ),
        name="combine",
    )(hi, lo, tokens, *answers)


def add(a, b):
    return (a.astype(jnp.float32) + b.astype(jnp.float32)).astype(jnp.bfloat16)


def body(tokens, norm_gain, route_ids, route_weight, gate_up, down):
    count = lax.axis_size("expert")
    place = lax.axis_index("expert").reshape(1)

    p = [prepare(tokens, norm_gain, route_ids, route_weight)]
    p.append(send(p[0], FAR, -FAR))
    q = [send(p[0], -FAR, FAR, other=True)]
    for _ in range(2):
        p.append(send(p[-1], FAR, -FAR))
        q.append(send(q[-1], FAR, -FAR))
    gate_up, down, _, _ = lax.optimization_barrier((gate_up, down, p[2], q[1]))
    other_gu = send(gate_up, 0, 0, other=True)
    other_d = send(down, 0, 0, other=True)
    p.append(send(p[-1], FAR, -FAR))

    here, up1, low1, up2, low2, hi, lo = dispatch(count, place, p + q)
    up2 = send(up2, 2, 2)
    up1 = send(up1, 1, 1)
    low1 = send(low1, -1, -1)
    low2 = send(low2, -2, -2)
    weights = (gate_up, down, other_gu, other_d)
    [here] = experts(place, [here], *weights)
    here, up1, low1, up2, low2 = lax.optimization_barrier((here, up1, low1, up2, low2))
    up1, low1, up2, low2 = experts(place, [up1, low1, up2, low2], *weights)
    up1 = send(up1, -1, -1)
    low1 = send(low1, 1, 1)
    up2 = send(up2, -2, -2)
    low2 = send(low2, 2, 2)
    base, p1, p2, p3, p4, q1, q2, q3 = combine(hi, lo, tokens, [here, up1, low1, up2, low2])
    base = send(base, 0, 0, onward=1)
    x = add(p3, send(p4, -FAR, FAR))
    y = add(q2, send(q3, -FAR, FAR))
    x = add(p2, send(x, -FAR, FAR))
    y = add(q1, send(y, -FAR, FAR))
    x = add(p1, send(x, -FAR, FAR))
    y = send(y, -FAR, FAR, other=True, onward=1)
    x = send(x, -FAR, FAR, onward=1)
    out = base + x.astype(jnp.float32) + y.astype(jnp.float32)
    return out.astype(jnp.bfloat16)[None]


def solution(mesh):
    placed = (
        P("section", "expert", None),
        P(),
        P("section", "expert", None),
        P("section", "expert", None),
        P("expert", None, None),
        P("expert", None, None),
    )
    return jax.shard_map(
        body, mesh=mesh, in_specs=placed, out_specs=P("section", "expert", None), check_vma=False
    )
```

time: 233 us -> 214 us (0.918)
  the two profiles are of different devices: /device:TPU:6 before, /device:TPU:1 now
where the time goes in v3:
time: 214 us; the launch traced here: 212 us
  starting transfers between devices  122 us (57%)
  waiting for transfers between devices  57.3 us (27%)
  Pallas kernels  22 us (10%)
  local copies, waits for them, and re-layouts  9.87 us (5%)
    ppermute x22, starting transfers between devices, send(): return lax.ppermute(value, 'expert', [(i, place(i)) for i in range(count)])  101 us
    ppermute x22, waiting for transfers between devices, send(): return lax.ppermute(value, 'expert', [(i, place(i)) for i in range(count)])  43.6 us
    ppermute x3, starting transfers between devices, send(): return lax.ppermute(value, ('section', 'expert'), pairs)  21.2 us
    pallas_call x2, Pallas kernels, experts(): pl.pallas_call(functools.partial(expert_kernel, len(pieces)), grid_spec=p...  16.2 us
    ppermute x3, waiting for transfers between devices, send(): return lax.ppermute(value, ('section', 'expert'), pairs)  13.7 us
    unnamed x14, local copies, waits for them, and re-layouts  9.87 us
  transfers between devices with their start and end apart: 25, of which 11 were waited for; matrix products, arithmetic and copies ran while one was open for 0% of the time, Pallas kernels for 5%

profile of v3, /device:TPU:1, one launch (start us, length us, event | category | flops | bytes accessed | tf_op | source)
XLA Modules:
  0.0 212.4 jit_solution(8379633651028197076)
XLA Ops:
  4.5 20.5 %collective-permute-start = (bf16[32,2176]{1,0:T(8,128)(2,1)}, bf16[32,2176]{1,0:T(8,128)(2,1)S(1)}, u32[]{:S(2)}, u32[]{:S(2)}) collective-permute-start(bf16[32,2176]{1,0:T(8,128)(2,1)} %prepare.1.refs_0_), channel_id=1, source_target_pairs={{0,8},{1,57},{2,10},{3,59},{4,12},{5,61},{6,14},{7,63},{8,16},{9,1... | collective-permute-start | bytes 417800 | tf_op jit(solution)/shard_map/ppermute | solution.py:29
  27.0 4.9 %collective-permute-done.refs_1_ = bf16[32,2176]{1,0:T(8,128)(2,1)S(1)} collective-permute-done((bf16[32,2176]{1,0:T(8,128)(2,1)}, bf16[32,2176]{1,0:T(8,128)(2,1)S(1)}, u32[]{:S(2)}, u32[]{:S(2)}) %collective-permute-start) | collective-permute-done | bytes 139296 | tf_op jit(solution)/shard_map/ppermute | solution.py:29
  31.9 8.0 %collective-permute-start.1 = (bf16[32,2176]{1,0:T(8,128)(2,1)S(1)}, bf16[32,2176]{1,0:T(8,128)(2,1)S(1)}, u32[]{:S(2)}, u32[]{:S(2)}) collective-permute-start(bf16[32,2176]{1,0:T(8,128)(2,1)S(1)} %collective-permute-done.refs_1_), channel_id=1, source_target_pairs={{0,8},{1,57},{2,10},{3,59},{4,12},{5,61},{6,14},{7,63},{8,16},{9,1... | collective-permute-start | bytes 417800 | tf_op jit(solution)/shard_map/ppermute | solution.py:29
  39.9 5.6 %collective-permute-done.4.refs_5_ = bf16[32,2176]{1,0:T(8,128)(2,1)S(1)} collective-permute-done((bf16[32,2176]{1,0:T(8,128)(2,1)}, bf16[32,2176]{1,0:T(8,128)(2,1)S(1)}, u32[]{:S(2)}, u32[]{:S(2)}) %collective-permute-start.4) | collective-permute-done | bytes 139296 | tf_op jit(solution)/shard_map/ppermute | solution.py:29
  45.5 2.9 %collective-permute-start.5 = (bf16[32,2176]{1,0:T(8,128)(2,1)S(1)}, bf16[32,2176]{1,0:T(8,128)(2,1)}, u32[]{:S(2)}, u32[]{:S(2)}) collective-permute-start(bf16[32,2176]{1,0:T(8,128)(2,1)S(1)} %collective-permute-done.4.refs_5_), channel_id=1, source_target_pairs={{0,8},{1,57},{2,10},{3,59},{4,12},{5,61},{6,14},{7,63},{8,16},{9,1... | collective-permute-start | bytes 417800 | tf_op jit(solution)/shard_map/ppermute | solution.py:29
  48.4 7.9 %collective-permute-done.5.refs_6_ = bf16[32,2176]{1,0:T(8,128)(2,1)} collective-permute-done((bf16[32,2176]{1,0:T(8,128)(2,1)S(1)}, bf16[32,2176]{1,0:T(8,128)(2,1)}, u32[]{:S(2)}, u32[]{:S(2)}) %collective-permute-start.5) | collective-permute-done | bytes 139296 | tf_op jit(solution)/shard_map/ppermute | solution.py:29
  56.3 5.9 %collective-permute-start.7 = (bf16[1,2048,1536]{2,1,0:T(8,128)(2,1)}, bf16[1,2048,1536]{2,1,0:T(8,128)(2,1)}, u32[]{:S(2)}, u32[]{:S(2)}) collective-permute-start(bf16[1,2048,1536]{2,1,0:T(8,128)(2,1)} %refs_5_), channel_id=1, source_target_pairs={{0,1},{1,0},{2,3},{3,2},{4,5},{5,4},{6,7},{7,6},{8,9},{9,8},{10,11... | collective-permute-start | bytes 18874376 | tf_op jit(solution)/shard_map/ppermute | solution.py:29
  66.7 2.6 %collective-permute-start.6 = (bf16[32,2176]{1,0:T(8,128)(2,1)}, bf16[32,2176]{1,0:T(8,128)(2,1)}, u32[]{:S(2)}, u32[]{:S(2)}) collective-permute-start(bf16[32,2176]{1,0:T(8,128)(2,1)} %collective-permute-done.5.refs_6_), channel_id=1, source_target_pairs={{0,8},{1,57},{2,10},{3,59},{4,12},{5,61},{6,14},{7,63},{8,16},{9,1... | collective-permute-start | bytes 417800 | tf_op jit(solution)/shard_map/ppermute | solution.py:29
  69.4 5.5 %collective-permute-done.2.refs_3_ = bf16[32,2176]{1,0:T(8,128)(2,1)} collective-permute-done((bf16[32,2176]{1,0:T(8,128)(2,1)S(1)}, bf16[32,2176]{1,0:T(8,128)(2,1)}, u32[]{:S(2)}, u32[]{:S(2)}) %collective-permute-start.2) | collective-permute-done | bytes 139296 | tf_op jit(solution)/shard_map/ppermute | solution.py:29
  76.8 2.9 %collective-permute-done.6.refs_7_ = bf16[32,2176]{1,0:T(8,128)(2,1)} collective-permute-done((bf16[32,2176]{1,0:T(8,128)(2,1)}, bf16[32,2176]{1,0:T(8,128)(2,1)}, u32[]{:S(2)}, u32[]{:S(2)}) %collective-permute-start.6) | collective-permute-done | bytes 139296 | tf_op jit(solution)/shard_map/ppermute | solution.py:29
  79.7 6.7 %collective-permute-done.3.refs_4_ = bf16[32,2176]{1,0:T(8,128)(2,1)} collective-permute-done((bf16[32,2176]{1,0:T(8,128)(2,1)}, bf16[32,2176]{1,0:T(8,128)(2,1)}, u32[]{:S(2)}, u32[]{:S(2)}) %collective-permute-start.3) | collective-permute-done | bytes 139296 | tf_op jit(solution)/shard_map/ppermute | solution.py:29
  88.2 2.7 %dispatch.1 = (bf16[96,2048]{1,0:T(8,128)(2,1)S(1)}, bf16[96,2048]{1,0:T(8,128)(2,1)S(1)}, bf16[96,2048]{1,0:T(8,128)(2,1)S(1)}, bf16[48,2048]{1,0:T(8,128)(2,1)...) custom-call(s32[1]{0:T(128)} %bitcast.place, ...), custom_call_target="tpu_custom_call" | custom-call | flops 452984832 | bytes 4194304 | tf_op jit(solution)/shard_map/dispatch/pallas_call | solution.py:113
  90.9 6.2 %collective-permute-start.9 = (bf16[96,2048]{1,0:T(8,128)(2,1)S(1)}, bf16[96,2048]{1,0:T(8,128)(2,1)S(1)}, u32[]{:S(2)}, u32[]{:S(2)}) collective-permute-start(bf16[96,2048]{1,0:T(8,128)(2,1)S(1)} %get-tuple-element.36), channel_id=1, source_target_pairs={{0,2},{1,3},{2,4},{3,5},{4,6},{5,7},{6,8},{7,9},{8,10},{9,11},{10,... | collective-permute-start | bytes 1179656 | tf_op jit(solution)/shard_map/ppermute | solution.py:29
  99.0 3.1 %collective-permute-start.11 = (bf16[48,2048]{1,0:T(8,128)(2,1)S(1)}, bf16[48,2048]{1,0:T(8,128)(2,1)S(1)}, u32[]{:S(2)}, u32[]{:S(2)}) collective-permute-start(bf16[48,2048]{1,0:T(8,128)(2,1)S(1)} %get-tuple-element.38), channel_id=1, source_target_pairs={{0,4},{1,5},{2,6},{3,7},{4,8},{5,9},{6,10},{7,11},{8,12},{9,13},{1... | collective-permute-start | bytes 589832 | tf_op jit(solution)/shard_map/ppermute | solution.py:29
  102.1 4.3 %collective-permute-start.12 = (bf16[48,2048]{1,0:T(8,128)(2,1)S(1)}, bf16[48,2048]{1,0:T(8,128)(2,1)S(1)}, u32[]{:S(2)}, u32[]{:S(2)}) collective-permute-start(bf16[48,2048]{1,0:T(8,128)(2,1)S(1)} %get-tuple-element.39), channel_id=1, source_target_pairs={{0,60},{1,61},{2,62},{3,63},{4,0},{5,1},{6,2},{7,3},{8,4},{9,5},{1... | collective-permute-start | bytes 589832 | tf_op jit(solution)/shard_map/ppermute | solution.py:29
  106.4 2.8 %copy-done = bf16[1,2048,1536]{2,1,0:T(8,128)(2,1)S(1)} copy-done((bf16[1,2048,1536]{2,1,0:T(8,128)(2,1)S(1)}, bf16[1,2048,1536]{2,1,0:T(8,128)(2,1)}, u32[]{:S(2)}) %copy-start) | copy-done | bytes 6291480
  111.1 7.8 %experts.2.refs_0_ = bf16[96,2048]{1,0:T(8,128)(2,1)S(1)} custom-call(s32[1]{0:T(128)} %bitcast.place, bf16[96,2048]{1,0:T(8,128)(2,1)S(1)} %get-tuple-element.33.refs_0_, bf16[1,2048,1536]{2,1,0:T(8,128)(2,1)S(1)} %copy-done, bf16[1,2048,1536]{2,1,0:T(8,128)(2,1)S(1)} %copy-done, bf16[1,768,2048]{2,1,0:T(8,128)(2,1)S(1)} %copy-done.1, ...), custom_call_target="tpu_custom_call" | custom-call | flops 905969664 | bytes 18874368 | tf_op jit(solution)/shard_map/experts/pallas_call | solution.py:192
  119.0 8.4 %experts.3 = (bf16[96,2048]{1,0:T(8,128)(2,1)S(1)}, bf16[96,2048]{1,0:T(8,128)(2,1)S(1)}, bf16[48,2048]{1,0:T(8,128)(2,1)S(1)}, bf16[48,2048]{1,0:T(8,128)(2,1)S(1)}) custom-call(s32[1]{0:T(128)} %bitcast.place, bf16[96,2048]{1,0:T(8,128)(2,1)S(1)} %collective-permute-done.9.refs_0_, bf16[96,2048]{1,0:T(8,128)(2,1)S(1)} %collective-permute-done.10.refs_1_, ...), custom_call_target="tpu_custom_call" | custom-call | flops 2717908992 | bytes 18874368 | tf_op jit(solution)/shard_map/experts/pallas_call | solution.py:192
  127.3 2.2 %collective-permute-start.13 = (bf16[96,2048]{1,0:T(8,128)(2,1)S(1)}, bf16[96,2048]{1,0:T(8,128)(2,1)S(1)}, u32[]{:S(2)}, u32[]{:S(2)}) collective-permute-start(bf16[96,2048]{1,0:T(8,128)(2,1)S(1)} %get-tuple-element.45), channel_id=1, source_target_pairs={{0,62},{1,63},{2,0},{3,1},{4,2},{5,3},{6,4},{7,5},{8,6},{9,7},{10,... | collective-permute-start | bytes 1179656 | tf_op jit(solution)/shard_map/ppermute | solution.py:29
  129.5 3.1 %collective-permute-start.14 = (bf16[96,2048]{1,0:T(8,128)(2,1)S(1)}, bf16[96,2048]{1,0:T(8,128)(2,1)S(1)}, u32[]{:S(2)}, u32[]{:S(2)}) collective-permute-start(bf16[96,2048]{1,0:T(8,128)(2,1)S(1)} %get-tuple-element.46), channel_id=1, source_target_pairs={{0,2},{1,3},{2,4},{3,5},{4,6},{5,7},{6,8},{7,9},{8,10},{9,11},{10,... | collective-permute-start | bytes 1179656 | tf_op jit(solution)/shard_map/ppermute | solution.py:29
  132.6 2.2 %collective-permute-start.15 = (bf16[48,2048]{1,0:T(8,128)(2,1)S(1)}, bf16[48,2048]{1,0:T(8,128)(2,1)S(1)}, u32[]{:S(2)}, u32[]{:S(2)}) collective-permute-start(bf16[48,2048]{1,0:T(8,128)(2,1)S(1)} %get-tuple-element.47), channel_id=1, source_target_pairs={{0,60},{1,61},{2,62},{3,63},{4,0},{5,1},{6,2},{7,3},{8,4},{9,5},{1... | collective-permute-start | bytes 589832 | tf_op jit(solution)/shard_map/ppermute | solution.py:29
  134.8 4.0 %collective-permute-start.16 = (bf16[48,2048]{1,0:T(8,128)(2,1)S(1)}, bf16[48,2048]{1,0:T(8,128)(2,1)S(1)}, u32[]{:S(2)}, u32[]{:S(2)}) collective-permute-start(bf16[48,2048]{1,0:T(8,128)(2,1)S(1)} %get-tuple-element.48), channel_id=1, source_target_pairs={{0,4},{1,5},{2,6},{3,7},{4,8},{5,9},{6,10},{7,11},{8,12},{9,13},{1... | collective-permute-start | bytes 589832 | tf_op jit(solution)/shard_map/ppermute | solution.py:29
  138.8 4.5 %collective-permute-done.15.refs_3_ = bf16[48,2048]{1,0:T(8,128)(2,1)S(1)} collective-permute-done((bf16[48,2048]{1,0:T(8,128)(2,1)S(1)}, bf16[48,2048]{1,0:T(8,128)(2,1)S(1)}, u32[]{:S(2)}, u32[]{:S(2)}) %collective-permute-start.15) | collective-permute-done | bytes 196640 | tf_op jit(solution)/shard_map/ppermute | solution.py:29
  143.4 4.1 %collective-permute-done.16.refs_4_ = bf16[48,2048]{1,0:T(8,128)(2,1)S(1)} collective-permute-done((bf16[48,2048]{1,0:T(8,128)(2,1)S(1)}, bf16[48,2048]{1,0:T(8,128)(2,1)S(1)}, u32[]{:S(2)}, u32[]{:S(2)}) %collective-permute-start.16) | collective-permute-done | bytes 196640 | tf_op jit(solution)/shard_map/ppermute | solution.py:29
  148.7 6.5 %collective-permute-start.18 = (bf16[32,2048]{1,0:T(8,128)(2,1)S(1)}, bf16[32,2048]{1,0:T(8,128)(2,1)S(1)}, u32[]{:S(2)}, u32[]{:S(2)}) collective-permute-start(bf16[32,2048]{1,0:T(8,128)(2,1)S(1)} %get-tuple-element.53), channel_id=1, source_target_pairs={{0,56},{1,9},{2,58},{3,11},{4,60},{5,13},{6,62},{7,15},{8,0},{9,17... | collective-permute-start | bytes 393224 | tf_op jit(solution)/shard_map/ppermute | solution.py:29
  155.2 4.7 %collective-permute-start.22 = (bf16[32,2048]{1,0:T(8,128)(2,1)S(1)}, bf16[32,2048]{1,0:T(8,128)(2,1)S(1)}, u32[]{:S(2)}, u32[]{:S(2)}) collective-permute-start(bf16[32,2048]{1,0:T(8,128)(2,1)S(1)} %get-tuple-element.56), channel_id=1, source_target_pairs={{0,56},{1,9},{2,58},{3,11},{4,60},{5,13},{6,62},{7,15},{8,0},{9,17... | collective-permute-start | bytes 393224 | tf_op jit(solution)/shard_map/ppermute | solution.py:29
  161.9 5.6 %collective-permute-start.19 = (bf16[32,2048]{1,0:T(8,128)(2,1)S(1)}, bf16[32,2048]{1,0:T(8,128)(2,1)S(1)}, u32[]{:S(2)}, u32[]{:S(2)}) collective-permute-start(bf16[32,2048]{1,0:T(8,128)(2,1)S(1)} %add_convert_fusion.5), channel_id=1, source_target_pairs={{0,56},{1,9},{2,58},{3,11},{4,60},{5,13},{6,62},{7,15},{8,0},{9,17... | collective-permute-start | bytes 393224 | tf_op jit(solution)/shard_map/ppermute | solution.py:29
  167.6 4.3 %collective-permute-start.23 = (bf16[32,2048]{1,0:T(8,128)(2,1)S(1)}, bf16[32,2048]{1,0:T(8,128)(2,1)S(1)}, u32[]{:S(2)}, u32[]{:S(2)}) collective-permute-start(bf16[32,2048]{1,0:T(8,128)(2,1)S(1)} %add_convert_fusion.2), channel_id=1, source_target_pairs={{0,56},{1,9},{2,58},{3,11},{4,60},{5,13},{6,62},{7,15},{8,0},{9,17... | collective-permute-start | bytes 393224 | tf_op jit(solution)/shard_map/ppermute | solution.py:29
  173.5 5.1 %collective-permute-start.20 = (bf16[32,2048]{1,0:T(8,128)(2,1)S(1)}, bf16[32,2048]{1,0:T(8,128)(2,1)S(1)}, u32[]{:S(2)}, u32[]{:S(2)}) collective-permute-start(bf16[32,2048]{1,0:T(8,128)(2,1)S(1)} %add_convert_fusion.4), channel_id=1, source_target_pairs={{0,56},{1,9},{2,58},{3,11},{4,60},{5,13},{6,62},{7,15},{8,0},{9,17... | collective-permute-start | bytes 393224 | tf_op jit(solution)/shard_map/ppermute | solution.py:29
  178.6 15.5 %collective-permute-start.24 = (bf16[32,2048]{1,0:T(8,128)(2,1)S(1)}, bf16[32,2048]{1,0:T(8,128)(2,1)S(1)}, u32[]{:S(2)}, u32[]{:S(2)}) collective-permute-start(bf16[32,2048]{1,0:T(8,128)(2,1)S(1)} %add_convert_fusion.1), channel_id=1, source_target_pairs={{0,121},{1,72},{2,123},{3,74},{4,125},{5,76},{6,127},{7,78},{8,65}... | collective-permute-start | bytes 393224 | tf_op jit(solution)/shard_map/ppermute | solution.py:35
  194.1 3.8 %collective-permute-start.21 = (bf16[32,2048]{1,0:T(8,128)(2,1)S(1)}, bf16[32,2048]{1,0:T(8,128)(2,1)S(1)}, u32[]{:S(2)}, u32[]{:S(2)}) collective-permute-start(bf16[32,2048]{1,0:T(8,128)(2,1)S(1)} %add_convert_fusion.3), channel_id=1, source_target_pairs={{0,120},{1,73},{2,122},{3,75},{4,124},{5,77},{6,126},{7,79},{8,64}... | collective-permute-start | bytes 393224 | tf_op jit(solution)/shard_map/ppermute | solution.py:35
  199.6 12.1 %collective-permute-done.21 = bf16[32,2048]{1,0:T(8,128)(2,1)S(1)} collective-permute-done((bf16[32,2048]{1,0:T(8,128)(2,1)S(1)}, bf16[32,2048]{1,0:T(8,128)(2,1)S(1)}, u32[]{:S(2)}, u32[]{:S(2)}) %collective-permute-start.21) | collective-permute-done | bytes 131104 | tf_op jit(solution)/shard_map/ppermute | solution.py:35
  (43 shorter events, 25.8 us)
Async XLA Ops:
  4.5 27.4 %collective-permute-start = (bf16[32,2176]{1,0:T(8,128)(2,1)}, bf16[32,2176]{1,0:T(8,128)(2,1)S(1)}, u32[]{:S(2)}, u32[]{:S(2)}) collective-permute-start(bf16[32,2176]{1,0:T(8,128)(2,1)} %prepare.1.refs_0_), channel_id=1, source_target_pairs={{0,8},{1,57},{2,10},{3,59},{4,12},{5,61},{6,14},{7,63},{8,16},{9,1... | collective-permute-start | bytes 417800 | tf_op jit(solution)/shard_map/ppermute | solution.py:29
  25.1 20.4 %collective-permute-start.4 = (bf16[32,2176]{1,0:T(8,128)(2,1)}, bf16[32,2176]{1,0:T(8,128)(2,1)S(1)}, u32[]{:S(2)}, u32[]{:S(2)}) collective-permute-start(bf16[32,2176]{1,0:T(8,128)(2,1)} %prepare.1.refs_0_), channel_id=1, source_target_pairs={{0,57},{1,8},{2,59},{3,10},{4,61},{5,12},{6,63},{7,14},{8,1},{9,16... | collective-permute-start | bytes 417800 | tf_op jit(solution)/shard_map/ppermute | solution.py:29
  31.9 16.5 %collective-permute-start.1 = (bf16[32,2176]{1,0:T(8,128)(2,1)S(1)}, bf16[32,2176]{1,0:T(8,128)(2,1)S(1)}, u32[]{:S(2)}, u32[]{:S(2)}) collective-permute-start(bf16[32,2176]{1,0:T(8,128)(2,1)S(1)} %collective-permute-done.refs_1_), channel_id=1, source_target_pairs={{0,8},{1,57},{2,10},{3,59},{4,12},{5,61},{6,14},{7,63},{8,16},{9,1... | collective-permute-start | bytes 417800 | tf_op jit(solution)/shard_map/ppermute | solution.py:29
  45.5 10.8 %collective-permute-start.5 = (bf16[32,2176]{1,0:T(8,128)(2,1)S(1)}, bf16[32,2176]{1,0:T(8,128)(2,1)}, u32[]{:S(2)}, u32[]{:S(2)}) collective-permute-start(bf16[32,2176]{1,0:T(8,128)(2,1)S(1)} %collective-permute-done.4.refs_5_), channel_id=1, source_target_pairs={{0,8},{1,57},{2,10},{3,59},{4,12},{5,61},{6,14},{7,63},{8,16},{9,1... | collective-permute-start | bytes 417800 | tf_op jit(solution)/shard_map/ppermute | solution.py:29
  56.3 50.1 %collective-permute-start.7 = (bf16[1,2048,1536]{2,1,0:T(8,128)(2,1)}, bf16[1,2048,1536]{2,1,0:T(8,128)(2,1)}, u32[]{:S(2)}, u32[]{:S(2)}) collective-permute-start(bf16[1,2048,1536]{2,1,0:T(8,128)(2,1)} %refs_5_), channel_id=1, source_target_pairs={{0,1},{1,0},{2,3},{3,2},{4,5},{5,4},{6,7},{7,6},{8,9},{9,8},{10,11... | collective-permute-start | bytes 18874376 | tf_op jit(solution)/shard_map/ppermute | solution.py:29
  62.2 39.9 %collective-permute-start.8 = (bf16[1,768,2048]{2,1,0:T(8,128)(2,1)}, bf16[1,768,2048]{2,1,0:T(8,128)(2,1)S(1)}, u32[]{:S(2)}, u32[]{:S(2)}) collective-permute-start(bf16[1,768,2048]{2,1,0:T(8,128)(2,1)} %refs_6_), channel_id=1, source_target_pairs={{0,1},{1,0},{2,3},{3,2},{4,5},{5,4},{6,7},{7,6},{8,9},{9,8},{10,11... | collective-permute-start | bytes 9437192 | tf_op jit(solution)/shard_map/ppermute | solution.py:29
  64.1 10.8 %collective-permute-start.2 = (bf16[32,2176]{1,0:T(8,128)(2,1)S(1)}, bf16[32,2176]{1,0:T(8,128)(2,1)}, u32[]{:S(2)}, u32[]{:S(2)}) collective-permute-start(bf16[32,2176]{1,0:T(8,128)(2,1)S(1)} %collective-permute-done.1.refs_2_), channel_id=1, source_target_pairs={{0,8},{1,57},{2,10},{3,59},{4,12},{5,61},{6,14},{7,63},{8,16},{9,1... | collective-permute-start | bytes 417800 | tf_op jit(solution)/shard_map/ppermute | solution.py:29
  66.0 0.7 copy-start.4
  66.7 13.0 %collective-permute-start.6 = (bf16[32,2176]{1,0:T(8,128)(2,1)}, bf16[32,2176]{1,0:T(8,128)(2,1)}, u32[]{:S(2)}, u32[]{:S(2)}) collective-permute-start(bf16[32,2176]{1,0:T(8,128)(2,1)} %collective-permute-done.5.refs_6_), channel_id=1, source_target_pairs={{0,8},{1,57},{2,10},{3,59},{4,12},{5,61},{6,14},{7,63},{8,16},{9,1... | collective-permute-start | bytes 417800 | tf_op jit(solution)/shard_map/ppermute | solution.py:29
  74.9 11.5 %collective-permute-start.3 = (bf16[32,2176]{1,0:T(8,128)(2,1)}, bf16[32,2176]{1,0:T(8,128)(2,1)}, u32[]{:S(2)}, u32[]{:S(2)}) collective-permute-start(bf16[32,2176]{1,0:T(8,128)(2,1)} %collective-permute-done.2.refs_3_), channel_id=1, source_target_pairs={{0,8},{1,57},{2,10},{3,59},{4,12},{5,61},{6,14},{7,63},{8,16},{9,1... | collective-permute-start | bytes 417800 | tf_op jit(solution)/shard_map/ppermute | solution.py:29
  86.3 0.9 copy-start.2
  87.3 0.9 copy-start.5
  90.9 28.0 %collective-permute-start.9 = (bf16[96,2048]{1,0:T(8,128)(2,1)S(1)}, bf16[96,2048]{1,0:T(8,128)(2,1)S(1)}, u32[]{:S(2)}, u32[]{:S(2)}) collective-permute-start(bf16[96,2048]{1,0:T(8,128)(2,1)S(1)} %get-tuple-element.36), channel_id=1, source_target_pairs={{0,2},{1,3},{2,4},{3,5},{4,6},{5,7},{6,8},{7,9},{8,10},{9,11},{10,... | collective-permute-start | bytes 1179656 | tf_op jit(solution)/shard_map/ppermute | solution.py:29
  97.1 21.9 %collective-permute-start.10 = (bf16[96,2048]{1,0:T(8,128)(2,1)S(1)}, bf16[96,2048]{1,0:T(8,128)(2,1)S(1)}, u32[]{:S(2)}, u32[]{:S(2)}) collective-permute-start(bf16[96,2048]{1,0:T(8,128)(2,1)S(1)} %get-tuple-element.37), channel_id=1, source_target_pairs={{0,62},{1,63},{2,0},{3,1},{4,2},{5,3},{6,4},{7,5},{8,6},{9,7},{10,... | collective-permute-start | bytes 1179656 | tf_op jit(solution)/shard_map/ppermute | solution.py:29
  99.0 19.9 %collective-permute-start.11 = (bf16[48,2048]{1,0:T(8,128)(2,1)S(1)}, bf16[48,2048]{1,0:T(8,128)(2,1)S(1)}, u32[]{:S(2)}, u32[]{:S(2)}) collective-permute-start(bf16[48,2048]{1,0:T(8,128)(2,1)S(1)} %get-tuple-element.38), channel_id=1, source_target_pairs={{0,4},{1,5},{2,6},{3,7},{4,8},{5,9},{6,10},{7,11},{8,12},{9,13},{1... | collective-permute-start | bytes 589832 | tf_op jit(solution)/shard_map/ppermute | solution.py:29
  102.1 16.8 %collective-permute-start.12 = (bf16[48,2048]{1,0:T(8,128)(2,1)S(1)}, bf16[48,2048]{1,0:T(8,128)(2,1)S(1)}, u32[]{:S(2)}, u32[]{:S(2)}) collective-permute-start(bf16[48,2048]{1,0:T(8,128)(2,1)S(1)} %get-tuple-element.39), channel_id=1, source_target_pairs={{0,60},{1,61},{2,62},{3,63},{4,0},{5,1},{6,2},{7,3},{8,4},{9,5},{1... | collective-permute-start | bytes 589832 | tf_op jit(solution)/shard_map/ppermute | solution.py:29
  106.4 2.8 %copy-start = (bf16[1,2048,1536]{2,1,0:T(8,128)(2,1)S(1)}, bf16[1,2048,1536]{2,1,0:T(8,128)(2,1)}, u32[]{:S(2)}) copy-start(bf16[1,2048,1536]{2,1,0:T(8,128)(2,1)} %refs_5_) | copy-start | bytes 18874372
  109.2 1.9 copy-start.1
  118.9 28.5 %copy-start.3 = (bf16[1,32,2048]{2,1,0:T(8,128)(2,1)S(1)}, bf16[1,32,2048]{2,1,0:T(8,128)(2,1)}, u32[]{:S(2)}) copy-start(bf16[1,32,2048]{2,1,0:T(8,128)(2,1)} %tokens.3) | copy-start | bytes 393220
  127.3 20.1 %collective-permute-start.13 = (bf16[96,2048]{1,0:T(8,128)(2,1)S(1)}, bf16[96,2048]{1,0:T(8,128)(2,1)S(1)}, u32[]{:S(2)}, u32[]{:S(2)}) collective-permute-start(bf16[96,2048]{1,0:T(8,128)(2,1)S(1)} %get-tuple-element.45), channel_id=1, source_target_pairs={{0,62},{1,63},{2,0},{3,1},{4,2},{5,3},{6,4},{7,5},{8,6},{9,7},{10,... | collective-permute-start | bytes 1179656 | tf_op jit(solution)/shard_map/ppermute | solution.py:29
  129.5 17.9 %collective-permute-start.14 = (bf16[96,2048]{1,0:T(8,128)(2,1)S(1)}, bf16[96,2048]{1,0:T(8,128)(2,1)S(1)}, u32[]{:S(2)}, u32[]{:S(2)}) collective-permute-start(bf16[96,2048]{1,0:T(8,128)(2,1)S(1)} %get-tuple-element.46), channel_id=1, source_target_pairs={{0,2},{1,3},{2,4},{3,5},{4,6},{5,7},{6,8},{7,9},{8,10},{9,11},{10,... | collective-permute-start | bytes 1179656 | tf_op jit(solution)/shard_map/ppermute | solution.py:29
  132.6 10.7 %collective-permute-start.15 = (bf16[48,2048]{1,0:T(8,128)(2,1)S(1)}, bf16[48,2048]{1,0:T(8,128)(2,1)S(1)}, u32[]{:S(2)}, u32[]{:S(2)}) collective-permute-start(bf16[48,2048]{1,0:T(8,128)(2,1)S(1)} %get-tuple-element.47), channel_id=1, source_target_pairs={{0,60},{1,61},{2,62},{3,63},{4,0},{5,1},{6,2},{7,3},{8,4},{9,5},{1... | collective-permute-start | bytes 589832 | tf_op jit(solution)/shard_map/ppermute | solution.py:29
  134.8 12.6 %collective-permute-start.16 = (bf16[48,2048]{1,0:T(8,128)(2,1)S(1)}, bf16[48,2048]{1,0:T(8,128)(2,1)S(1)}, u32[]{:S(2)}, u32[]{:S(2)}) collective-permute-start(bf16[48,2048]{1,0:T(8,128)(2,1)S(1)} %get-tuple-element.48), channel_id=1, source_target_pairs={{0,4},{1,5},{2,6},{3,7},{4,8},{5,9},{6,10},{7,11},{8,12},{9,13},{1... | collective-permute-start | bytes 589832 | tf_op jit(solution)/shard_map/ppermute | solution.py:29
  148.7 13.2 %collective-permute-start.18 = (bf16[32,2048]{1,0:T(8,128)(2,1)S(1)}, bf16[32,2048]{1,0:T(8,128)(2,1)S(1)}, u32[]{:S(2)}, u32[]{:S(2)}) collective-permute-start(bf16[32,2048]{1,0:T(8,128)(2,1)S(1)} %get-tuple-element.53), channel_id=1, source_target_pairs={{0,56},{1,9},{2,58},{3,11},{4,60},{5,13},{6,62},{7,15},{8,0},{9,17... | collective-permute-start | bytes 393224 | tf_op jit(solution)/shard_map/ppermute | solution.py:29
  155.2 12.3 %collective-permute-start.22 = (bf16[32,2048]{1,0:T(8,128)(2,1)S(1)}, bf16[32,2048]{1,0:T(8,128)(2,1)S(1)}, u32[]{:S(2)}, u32[]{:S(2)}) collective-permute-start(bf16[32,2048]{1,0:T(8,128)(2,1)S(1)} %get-tuple-element.56), channel_id=1, source_target_pairs={{0,56},{1,9},{2,58},{3,11},{4,60},{5,13},{6,62},{7,15},{8,0},{9,17... | collective-permute-start | bytes 393224 | tf_op jit(solution)/shard_map/ppermute | solution.py:29
  159.9 38.0 %collective-permute-start.17 = (f32[32,2048]{1,0:T(8,128)S(1)}, f32[32,2048]{1,0:T(8,128)S(1)}, u32[]{:S(2)}, u32[]{:S(2)}) collective-permute-start(f32[32,2048]{1,0:T(8,128)S(1)} %get-tuple-element.49), channel_id=1, source_target_pairs={{0,64},{1,65},{2,66},{3,67},{4,68},{5,69},{6,70},{7,71},{8,72},{9,... | collective-permute-start | bytes 786440 | tf_op jit(solution)/shard_map/ppermute | solution.py:35
  161.9 11.6 %collective-permute-start.19 = (bf16[32,2048]{1,0:T(8,128)(2,1)S(1)}, bf16[32,2048]{1,0:T(8,128)(2,1)S(1)}, u32[]{:S(2)}, u32[]{:S(2)}) collective-permute-start(bf16[32,2048]{1,0:T(8,128)(2,1)S(1)} %add_convert_fusion.5), channel_id=1, source_target_pairs={{0,56},{1,9},{2,58},{3,11},{4,60},{5,13},{6,62},{7,15},{8,0},{9,17... | collective-permute-start | bytes 393224 | tf_op jit(solution)/shard_map/ppermute | solution.py:29
  167.6 11.0 %collective-permute-start.23 = (bf16[32,2048]{1,0:T(8,128)(2,1)S(1)}, bf16[32,2048]{1,0:T(8,128)(2,1)S(1)}, u32[]{:S(2)}, u32[]{:S(2)}) collective-permute-start(bf16[32,2048]{1,0:T(8,128)(2,1)S(1)} %add_convert_fusion.2), channel_id=1, source_target_pairs={{0,56},{1,9},{2,58},{3,11},{4,60},{5,13},{6,62},{7,15},{8,0},{9,17... | collective-permute-start | bytes 393224 | tf_op jit(solution)/shard_map/ppermute | solution.py:29
  173.5 20.6 %collective-permute-start.20 = (bf16[32,2048]{1,0:T(8,128)(2,1)S(1)}, bf16[32,2048]{1,0:T(8,128)(2,1)S(1)}, u32[]{:S(2)}, u32[]{:S(2)}) collective-permute-start(bf16[32,2048]{1,0:T(8,128)(2,1)S(1)} %add_convert_fusion.4), channel_id=1, source_target_pairs={{0,56},{1,9},{2,58},{3,11},{4,60},{5,13},{6,62},{7,15},{8,0},{9,17... | collective-permute-start | bytes 393224 | tf_op jit(solution)/shard_map/ppermute | solution.py:29
  178.6 21.0 %collective-permute-start.24 = (bf16[32,2048]{1,0:T(8,128)(2,1)S(1)}, bf16[32,2048]{1,0:T(8,128)(2,1)S(1)}, u32[]{:S(2)}, u32[]{:S(2)}) collective-permute-start(bf16[32,2048]{1,0:T(8,128)(2,1)S(1)} %add_convert_fusion.1), channel_id=1, source_target_pairs={{0,121},{1,72},{2,123},{3,74},{4,125},{5,76},{6,127},{7,78},{8,65}... | collective-permute-start | bytes 393224 | tf_op jit(solution)/shard_map/ppermute | solution.py:35
  194.1 17.5 %collective-permute-start.21 = (bf16[32,2048]{1,0:T(8,128)(2,1)S(1)}, bf16[32,2048]{1,0:T(8,128)(2,1)S(1)}, u32[]{:S(2)}, u32[]{:S(2)}) collective-permute-start(bf16[32,2048]{1,0:T(8,128)(2,1)S(1)} %add_convert_fusion.3), channel_id=1, source_target_pairs={{0,120},{1,73},{2,122},{3,75},{4,124},{5,77},{6,126},{7,79},{8,64}... | collective-permute-start | bytes 393224 | tf_op jit(solution)/shard_map/ppermute | solution.py:35

commit v4 on v3

--- a/solution.py
+++ b/solution.py
@@ -39,17 +39,16 @@
     width = tokens.shape[2]
     values = tokens[0].astype(jnp.float32)
     scale = lax.rsqrt(jnp.mean(values * values, axis=1, keepdims=True) + 1e-06)
-    share = weights[0] / jnp.sum(weights[0], axis=1, keepdims=True)
+    share = weights[0] / jnp.sum(weights[0], axis=0, keepdims=True)
     hi = share.astype(jnp.bfloat16).astype(jnp.float32)
-    lo = share - hi
-    named = ids[0].astype(jnp.float32)
-    lane = lax.broadcasted_iota(jnp.int32, (ROWS, INFO), 1)
-    info = jnp.zeros((ROWS, INFO), jnp.float32)
-    for k in range(8):
-        info = jnp.where(lane == k, named[:, k : k + 1], info)
-        info = jnp.where(lane == 8 + k, hi[:, k : k + 1], info)
-        info = jnp.where(lane == 16 + k, lo[:, k : k + 1], info)
-    info = info.astype(jnp.bfloat16)
+    unused = jnp.zeros((INFO - 24, ROWS), jnp.float32)
+    columns = jnp.concatenate([ids[0].astype(jnp.float32), hi, share - hi, unused], axis=0)
+    r = lax.broadcasted_iota(jnp.int32, (INFO, INFO), 0)
+    c = lax.broadcasted_iota(jnp.int32, (INFO, INFO), 1)
+    same = jnp.where(r == c, 1.0, 0.0).astype(jnp.bfloat16)
+    info = lax.dot_general(
+        columns.astype(jnp.bfloat16), same, (((0,), (0,)), ((), ())), preferred_element_type=jnp.float32
+    ).astype(jnp.bfloat16)
     ready[:, :width] = (values * scale * gain[...]).astype(jnp.bfloat16)
     ready[:, width:] = info
 
@@ -61,7 +60,7 @@
         out_shape=shape,
         compiler_params=pltpu.CompilerParams(vmem_limit_bytes=56 * 2**20),
         name="prepare",
-    )(tokens, gain.reshape(1, -1), ids, weights)
+    )(tokens, gain.reshape(1, -1), ids.transpose(0, 2, 1), weights.transpose(0, 2, 1))
 
 
 def dispatch_kernel(count, place, *refs):
@@ -202,7 +201,7 @@
             ],
         ),
         out_shape=[jax.ShapeDtypeStruct(p.shape, jnp.bfloat16) for p in pieces],
-        compiler_params=pltpu.CompilerParams(vmem_limit_bytes=32 * 2**20),
+        compiler_params=pltpu.CompilerParams(vmem_limit_bytes=56 * 2**20),
         cost_estimate=pl.CostEstimate(
             flops=2 * 2 * rows * 3 * width * hid,
             bytes_accessed=2 * 3 * 2 * width * hid,
@@ -250,17 +249,15 @@
     place = lax.axis_index("expert").reshape(1)
 
     p = [prepare(tokens, norm_gain, route_ids, route_weight)]
+    q = [send(p[0], 0, 0, other=True)]
     p.append(send(p[0], FAR, -FAR))
-    q = [send(p[0], -FAR, FAR, other=True)]
-    for _ in range(2):
-        p.append(send(p[-1], FAR, -FAR))
-        q.append(send(q[-1], FAR, -FAR))
-    gate_up, down, _, _ = lax.optimization_barrier((gate_up, down, p[2], q[1]))
     other_gu = send(gate_up, 0, 0, other=True)
     other_d = send(down, 0, 0, other=True)
-    p.append(send(p[-1], FAR, -FAR))
-
-    here, up1, low1, up2, low2, hi, lo = dispatch(count, place, p + q)
+    for _ in range(3):
+        q.append(send(q[-1], FAR, -FAR))
+        p.append(send(p[-1], FAR, -FAR))
+
+    here, up1, low1, up2, low2, hi, lo = dispatch(count, place, p + q[1:])
     up2 = send(up2, 2, 2)
     up1 = send(up1, 1, 1)
     low1 = send(low1, -1, -1)

time: 214 us -> 213 us (level)
  the two profiles are of different devices: /device:TPU:1 before, /device:TPU:6 now
where the time goes in v4:
time: 213 us; the launch traced here: 212 us
  starting transfers between devices  136 us (64%)
  waiting for transfers between devices  43 us (20%)
  Pallas kernels  28.4 us (13%)
  local copies, waits for them, and re-layouts  3.3 us (2%)
    ppermute x23, starting transfers between devices, send(): return lax.ppermute(value, 'expert', [(i, place(i)) for i in range(count)])  123 us
    ppermute x23, waiting for transfers between devices, send(): return lax.ppermute(value, 'expert', [(i, place(i)) for i in range(count)])  32.8 us
    pallas_call x2, Pallas kernels, experts(): pl.pallas_call(functools.partial(expert_kernel, len(pieces)), grid_spec=p...  23.8 us
    ppermute x3, starting transfers between devices, send(): return lax.ppermute(value, ('section', 'expert'), pairs)  13 us
    ppermute x3, waiting for transfers between devices, send(): return lax.ppermute(value, ('section', 'expert'), pairs)  10.2 us
  transfers between devices with their start and end apart: 26, of which 10 were waited for; matrix products, arithmetic and copies ran while one was open for 0% of the time, Pallas kernels for 7%

profile of v4, /device:TPU:6, one launch (start us, length us, event | category | flops | bytes accessed | tf_op | source)
XLA Modules:
  0.0 211.9 jit_solution(9629524653164331786)
XLA Ops:
  0.0 1.9 collective-permute-start.8
  1.9 2.4 %collective-permute-start.9 = (bf16[1,768,2048]{2,1,0:T(8,128)(2,1)}, bf16[1,768,2048]{2,1,0:T(8,128)(2,1)}, u32[]{:S(2)}, u32[]{:S(2)}) collective-permute-start(bf16[1,768,2048]{2,1,0:T(8,128)(2,1)} %refs_6_.1), channel_id=1, source_target_pairs={{0,1},{1,0},{2,3},{3,2},{4,5},{5,4},{6,7},{7,6},{8,9},{9,8},{10,11... | collective-permute-start | bytes 9437192 | tf_op jit(solution)/shard_map/ppermute | solution.py:29
  6.1 9.1 %collective-permute-start = (bf16[32,2176]{1,0:T(8,128)(2,1)}, bf16[32,2176]{1,0:T(8,128)(2,1)S(1)}, u32[]{:S(2)}, u32[]{:S(2)}) collective-permute-start(bf16[32,2176]{1,0:T(8,128)(2,1)} %prepare.1.refs_0_), channel_id=1, source_target_pairs={{0,8},{1,57},{2,10},{3,59},{4,12},{5,61},{6,14},{7,63},{8,16},{9,1... | collective-permute-start | bytes 417800 | tf_op jit(solution)/shard_map/ppermute | solution.py:29
  15.2 12.6 %collective-permute-start.4 = (bf16[32,2176]{1,0:T(8,128)(2,1)}, bf16[32,2176]{1,0:T(8,128)(2,1)S(1)}, u32[]{:S(2)}, u32[]{:S(2)}) collective-permute-start(bf16[32,2176]{1,0:T(8,128)(2,1)} %prepare.1.refs_0_), channel_id=1, source_target_pairs={{0,1},{1,0},{2,3},{3,2},{4,5},{5,4},{6,7},{7,6},{8,9},{9,8},{10,11... | collective-permute-start | bytes 417800 | tf_op jit(solution)/shard_map/ppermute | solution.py:29
  31.6 8.2 %collective-permute-start.5 = (bf16[32,2176]{1,0:T(8,128)(2,1)S(1)}, bf16[32,2176]{1,0:T(8,128)(2,1)S(1)}, u32[]{:S(2)}, u32[]{:S(2)}) collective-permute-start(bf16[32,2176]{1,0:T(8,128)(2,1)S(1)} %collective-permute-done.4), channel_id=1, source_target_pairs={{0,8},{1,57},{2,10},{3,59},{4,12},{5,61},{6,14},{7,63},{8,16},{9,1... | collective-permute-start | bytes 417800 | tf_op jit(solution)/shard_map/ppermute | solution.py:29
  40.5 7.4 %collective-permute-start.2 = (bf16[32,2176]{1,0:T(8,128)(2,1)S(1)}, bf16[32,2176]{1,0:T(8,128)(2,1)S(1)}, u32[]{:S(2)}, u32[]{:S(2)}) collective-permute-start(bf16[32,2176]{1,0:T(8,128)(2,1)S(1)} %collective-permute-done.1.refs_2_), channel_id=1, source_target_pairs={{0,8},{1,57},{2,10},{3,59},{4,12},{5,61},{6,14},{7,63},{8,16},{9,1... | collective-permute-start | bytes 417800 | tf_op jit(solution)/shard_map/ppermute | solution.py:29
  47.9 3.3 %collective-permute-done.5.refs_5_ = bf16[32,2176]{1,0:T(8,128)(2,1)S(1)} collective-permute-done((bf16[32,2176]{1,0:T(8,128)(2,1)S(1)}, bf16[32,2176]{1,0:T(8,128)(2,1)S(1)}, u32[]{:S(2)}, u32[]{:S(2)}) %collective-permute-start.5) | collective-permute-done | bytes 139296 | tf_op jit(solution)/shard_map/ppermute | solution.py:29
  51.2 8.4 %collective-permute-start.6 = (bf16[32,2176]{1,0:T(8,128)(2,1)S(1)}, bf16[32,2176]{1,0:T(8,128)(2,1)S(1)}, u32[]{:S(2)}, u32[]{:S(2)}) collective-permute-start(bf16[32,2176]{1,0:T(8,128)(2,1)S(1)} %collective-permute-done.5.refs_5_), channel_id=1, source_target_pairs={{0,8},{1,57},{2,10},{3,59},{4,12},{5,61},{6,14},{7,63},{8,16},{9,1... | collective-permute-start | bytes 417800 | tf_op jit(solution)/shard_map/ppermute | solution.py:29
  59.6 2.5 %collective-permute-start.3 = (bf16[32,2176]{1,0:T(8,128)(2,1)S(1)}, bf16[32,2176]{1,0:T(8,128)(2,1)S(1)}, u32[]{:S(2)}, u32[]{:S(2)}) collective-permute-start(bf16[32,2176]{1,0:T(8,128)(2,1)S(1)} %collective-permute-done.2.refs_3_), channel_id=1, source_target_pairs={{0,8},{1,57},{2,10},{3,59},{4,12},{5,61},{6,14},{7,63},{8,16},{9,1... | collective-permute-start | bytes 417800 | tf_op jit(solution)/shard_map/ppermute | solution.py:29
  62.2 6.5 %collective-permute-done.6.refs_6_ = bf16[32,2176]{1,0:T(8,128)(2,1)S(1)} collective-permute-done((bf16[32,2176]{1,0:T(8,128)(2,1)S(1)}, bf16[32,2176]{1,0:T(8,128)(2,1)S(1)}, u32[]{:S(2)}, u32[]{:S(2)}) %collective-permute-start.6) | collective-permute-done | bytes 139296 | tf_op jit(solution)/shard_map/ppermute | solution.py:29
  68.7 8.4 %collective-permute-start.7 = (bf16[32,2176]{1,0:T(8,128)(2,1)S(1)}, bf16[32,2176]{1,0:T(8,128)(2,1)S(1)}, u32[]{:S(2)}, u32[]{:S(2)}) collective-permute-start(bf16[32,2176]{1,0:T(8,128)(2,1)S(1)} %collective-permute-done.6.refs_6_), channel_id=1, source_target_pairs={{0,8},{1,57},{2,10},{3,59},{4,12},{5,61},{6,14},{7,63},{8,16},{9,1... | collective-permute-start | bytes 417800 | tf_op jit(solution)/shard_map/ppermute | solution.py:29
  77.1 6.6 %collective-permute-done.7.refs_7_ = bf16[32,2176]{1,0:T(8,128)(2,1)S(1)} collective-permute-done((bf16[32,2176]{1,0:T(8,128)(2,1)S(1)}, bf16[32,2176]{1,0:T(8,128)(2,1)S(1)}, u32[]{:S(2)}, u32[]{:S(2)}) %collective-permute-start.7) | collective-permute-done | bytes 139296 | tf_op jit(solution)/shard_map/ppermute | solution.py:29
  88.9 5.8 %collective-permute-start.11 = (bf16[96,2048]{1,0:T(8,128)(2,1)S(1)}, bf16[96,2048]{1,0:T(8,128)(2,1)S(1)}, u32[]{:S(2)}, u32[]{:S(2)}) collective-permute-start(bf16[96,2048]{1,0:T(8,128)(2,1)S(1)} %get-tuple-element.33), channel_id=1, source_target_pairs={{0,62},{1,63},{2,0},{3,1},{4,2},{5,3},{6,4},{7,5},{8,6},{9,7},{10,... | collective-permute-start | bytes 1179656 | tf_op jit(solution)/shard_map/ppermute | solution.py:29
  94.7 1.9 collective-permute-start.12
  96.7 6.0 %collective-permute-start.13 = (bf16[48,2048]{1,0:T(8,128)(2,1)S(1)}, bf16[48,2048]{1,0:T(8,128)(2,1)S(1)}, u32[]{:S(2)}, u32[]{:S(2)}) collective-permute-start(bf16[48,2048]{1,0:T(8,128)(2,1)S(1)} %get-tuple-element.35), channel_id=1, source_target_pairs={{0,60},{1,61},{2,62},{3,63},{4,0},{5,1},{6,2},{7,3},{8,4},{9,5},{1... | collective-permute-start | bytes 589832 | tf_op jit(solution)/shard_map/ppermute | solution.py:29
  102.7 11.5 %experts.2.refs_0_ = bf16[96,2048]{1,0:T(8,128)(2,1)} custom-call(s32[1]{0:T(128)} %bitcast.place, bf16[96,2048]{1,0:T(8,128)(2,1)} %copy-done.1, bf16[1,2048,1536]{2,1,0:T(8,128)(2,1)} %refs_5_.1, bf16[1,2048,1536]{2,1,0:T(8,128)(2,1)} %refs_5_.1, bf16[1,768,2048]{2,1,0:T(8,128)(2,1)} %refs_6_.1, ...), custom_call_target="tpu_custom_call" | custom-call | flops 905969664 | bytes 18874368 | tf_op jit(solution)/shard_map/experts/pallas_call | solution.py:191
  115.9 12.3 %experts.3 = (bf16[96,2048]{1,0:T(8,128)(2,1)}, bf16[96,2048]{1,0:T(8,128)(2,1)}, bf16[48,2048]{1,0:T(8,128)(2,1)}, bf16[48,2048]{1,0:T(8,128)(2,1)}) custom-call(s32[1]{0:T(128)} %bitcast.place, bf16[96,2048]{1,0:T(8,128)(2,1)} %copy-done.4, bf16[96,2048]{1,0:T(8,128)(2,1)} %copy-done.5, bf16[48,2048]{1,0:T(8,128)(2,1)} %copy-done.6, ...), custom_call_target="tpu_custom_call" | custom-call | flops 2717908992 | bytes 18874368 | tf_op jit(solution)/shard_map/experts/pallas_call | solution.py:191
  128.2 2.7 %collective-permute-start.14 = (bf16[96,2048]{1,0:T(8,128)(2,1)}, bf16[96,2048]{1,0:T(8,128)(2,1)S(1)}, u32[]{:S(2)}, u32[]{:S(2)}) collective-permute-start(bf16[96,2048]{1,0:T(8,128)(2,1)} %get-tuple-element.41), channel_id=1, source_target_pairs={{0,62},{1,63},{2,0},{3,1},{4,2},{5,3},{6,4},{7,5},{8,6},{9,7},{10,... | collective-permute-start | bytes 1179656 | tf_op jit(solution)/shard_map/ppermute | solution.py:29
  130.9 3.1 %collective-permute-start.15 = (bf16[96,2048]{1,0:T(8,128)(2,1)}, bf16[96,2048]{1,0:T(8,128)(2,1)S(1)}, u32[]{:S(2)}, u32[]{:S(2)}) collective-permute-start(bf16[96,2048]{1,0:T(8,128)(2,1)} %get-tuple-element.42), channel_id=1, source_target_pairs={{0,2},{1,3},{2,4},{3,5},{4,6},{5,7},{6,8},{7,9},{8,10},{9,11},{10,... | collective-permute-start | bytes 1179656 | tf_op jit(solution)/shard_map/ppermute | solution.py:29
  134.0 2.1 %collective-permute-start.16 = (bf16[48,2048]{1,0:T(8,128)(2,1)}, bf16[48,2048]{1,0:T(8,128)(2,1)S(1)}, u32[]{:S(2)}, u32[]{:S(2)}) collective-permute-start(bf16[48,2048]{1,0:T(8,128)(2,1)} %get-tuple-element.43), channel_id=1, source_target_pairs={{0,60},{1,61},{2,62},{3,63},{4,0},{5,1},{6,2},{7,3},{8,4},{9,5},{1... | collective-permute-start | bytes 589832 | tf_op jit(solution)/shard_map/ppermute | solution.py:29
  136.2 4.6 %collective-permute-start.17 = (bf16[48,2048]{1,0:T(8,128)(2,1)}, bf16[48,2048]{1,0:T(8,128)(2,1)S(1)}, u32[]{:S(2)}, u32[]{:S(2)}) collective-permute-start(bf16[48,2048]{1,0:T(8,128)(2,1)} %get-tuple-element.44), channel_id=1, source_target_pairs={{0,4},{1,5},{2,6},{3,7},{4,8},{5,9},{6,10},{7,11},{8,12},{9,13},{1... | collective-permute-start | bytes 589832 | tf_op jit(solution)/shard_map/ppermute | solution.py:29
  140.8 4.7 %collective-permute-done.16.refs_3_ = bf16[48,2048]{1,0:T(8,128)(2,1)S(1)} collective-permute-done((bf16[48,2048]{1,0:T(8,128)(2,1)}, bf16[48,2048]{1,0:T(8,128)(2,1)S(1)}, u32[]{:S(2)}, u32[]{:S(2)}) %collective-permute-start.16) | collective-permute-done | bytes 196640 | tf_op jit(solution)/shard_map/ppermute | solution.py:29
  149.2 4.2 %collective-permute-start.19 = (bf16[32,2048]{1,0:T(8,128)(2,1)S(1)}, bf16[32,2048]{1,0:T(8,128)(2,1)S(1)}, u32[]{:S(2)}, u32[]{:S(2)}) collective-permute-start(bf16[32,2048]{1,0:T(8,128)(2,1)S(1)} %get-tuple-element.49), channel_id=1, source_target_pairs={{0,56},{1,9},{2,58},{3,11},{4,60},{5,13},{6,62},{7,15},{8,0},{9,17... | collective-permute-start | bytes 393224 | tf_op jit(solution)/shard_map/ppermute | solution.py:29
  153.4 7.8 %collective-permute-start.23 = (bf16[32,2048]{1,0:T(8,128)(2,1)S(1)}, bf16[32,2048]{1,0:T(8,128)(2,1)S(1)}, u32[]{:S(2)}, u32[]{:S(2)}) collective-permute-start(bf16[32,2048]{1,0:T(8,128)(2,1)S(1)} %get-tuple-element.52), channel_id=1, source_target_pairs={{0,56},{1,9},{2,58},{3,11},{4,60},{5,13},{6,62},{7,15},{8,0},{9,17... | collective-permute-start | bytes 393224 | tf_op jit(solution)/shard_map/ppermute | solution.py:29
  161.3 3.5 %collective-permute-start.18 = (f32[32,2048]{1,0:T(8,128)S(1)}, f32[32,2048]{1,0:T(8,128)S(1)}, u32[]{:S(2)}, u32[]{:S(2)}) collective-permute-start(f32[32,2048]{1,0:T(8,128)S(1)} %get-tuple-element.45), channel_id=1, source_target_pairs={{0,64},{1,65},{2,66},{3,67},{4,68},{5,69},{6,70},{7,71},{8,72},{9,... | collective-permute-start | bytes 786440 | tf_op jit(solution)/shard_map/ppermute | solution.py:35
  164.8 6.3 %collective-permute-start.20 = (bf16[32,2048]{1,0:T(8,128)(2,1)S(1)}, bf16[32,2048]{1,0:T(8,128)(2,1)S(1)}, u32[]{:S(2)}, u32[]{:S(2)}) collective-permute-start(bf16[32,2048]{1,0:T(8,128)(2,1)S(1)} %add_convert_fusion.5), channel_id=1, source_target_pairs={{0,56},{1,9},{2,58},{3,11},{4,60},{5,13},{6,62},{7,15},{8,0},{9,17... | collective-permute-start | bytes 393224 | tf_op jit(solution)/shard_map/ppermute | solution.py:29
  171.2 6.2 %collective-permute-start.24 = (bf16[32,2048]{1,0:T(8,128)(2,1)S(1)}, bf16[32,2048]{1,0:T(8,128)(2,1)S(1)}, u32[]{:S(2)}, u32[]{:S(2)}) collective-permute-start(bf16[32,2048]{1,0:T(8,128)(2,1)S(1)} %add_convert_fusion.2), channel_id=1, source_target_pairs={{0,56},{1,9},{2,58},{3,11},{4,60},{5,13},{6,62},{7,15},{8,0},{9,17... | collective-permute-start | bytes 393224 | tf_op jit(solution)/shard_map/ppermute | solution.py:29
  177.5 7.2 %collective-permute-start.21 = (bf16[32,2048]{1,0:T(8,128)(2,1)S(1)}, bf16[32,2048]{1,0:T(8,128)(2,1)S(1)}, u32[]{:S(2)}, u32[]{:S(2)}) collective-permute-start(bf16[32,2048]{1,0:T(8,128)(2,1)S(1)} %add_convert_fusion.4), channel_id=1, source_target_pairs={{0,56},{1,9},{2,58},{3,11},{4,60},{5,13},{6,62},{7,15},{8,0},{9,17... | collective-permute-start | bytes 393224 | tf_op jit(solution)/shard_map/ppermute | solution.py:29
  184.8 1.9 collective-permute-start.25
  186.7 6.6 %collective-permute-done.21 = bf16[32,2048]{1,0:T(8,128)(2,1)S(1)} collective-permute-done((bf16[32,2048]{1,0:T(8,128)(2,1)S(1)}, bf16[32,2048]{1,0:T(8,128)(2,1)S(1)}, u32[]{:S(2)}, u32[]{:S(2)}) %collective-permute-start.21) | collective-permute-done | bytes 131104 | tf_op jit(solution)/shard_map/ppermute | solution.py:29
  193.3 7.6 %collective-permute-start.22 = (bf16[32,2048]{1,0:T(8,128)(2,1)S(1)}, bf16[32,2048]{1,0:T(8,128)(2,1)S(1)}, u32[]{:S(2)}, u32[]{:S(2)}) collective-permute-start(bf16[32,2048]{1,0:T(8,128)(2,1)S(1)} %add_convert_fusion.3), channel_id=1, source_target_pairs={{0,120},{1,73},{2,122},{3,75},{4,124},{5,77},{6,126},{7,79},{8,64}... | collective-permute-start | bytes 393224 | tf_op jit(solution)/shard_map/ppermute | solution.py:35
  201.0 10.2 %collective-permute-done.22 = bf16[32,2048]{1,0:T(8,128)(2,1)S(1)} collective-permute-done((bf16[32,2048]{1,0:T(8,128)(2,1)S(1)}, bf16[32,2048]{1,0:T(8,128)(2,1)S(1)}, u32[]{:S(2)}, u32[]{:S(2)}) %collective-permute-start.22) | collective-permute-done | bytes 131104 | tf_op jit(solution)/shard_map/ppermute | solution.py:35
  (47 shorter events, 17.7 us)
Async XLA Ops:
  0.0 102.7 %collective-permute-start.8 = (bf16[1,2048,1536]{2,1,0:T(8,128)(2,1)}, bf16[1,2048,1536]{2,1,0:T(8,128)(2,1)}, u32[]{:S(2)}, u32[]{:S(2)}) collective-permute-start(bf16[1,2048,1536]{2,1,0:T(8,128)(2,1)} %refs_5_.1), channel_id=1, source_target_pairs={{0,1},{1,0},{2,3},{3,2},{4,5},{5,4},{6,7},{7,6},{8,9},{9,8},{10,11... | collective-permute-start | bytes 18874376 | tf_op jit(solution)/shard_map/ppermute | solution.py:29
  1.9 94.8 %collective-permute-start.9 = (bf16[1,768,2048]{2,1,0:T(8,128)(2,1)}, bf16[1,768,2048]{2,1,0:T(8,128)(2,1)}, u32[]{:S(2)}, u32[]{:S(2)}) collective-permute-start(bf16[1,768,2048]{2,1,0:T(8,128)(2,1)} %refs_6_.1), channel_id=1, source_target_pairs={{0,1},{1,0},{2,3},{3,2},{4,5},{5,4},{6,7},{7,6},{8,9},{9,8},{10,11... | collective-permute-start | bytes 9437192 | tf_op jit(solution)/shard_map/ppermute | solution.py:29
  6.1 23.5 %collective-permute-start = (bf16[32,2176]{1,0:T(8,128)(2,1)}, bf16[32,2176]{1,0:T(8,128)(2,1)S(1)}, u32[]{:S(2)}, u32[]{:S(2)}) collective-permute-start(bf16[32,2176]{1,0:T(8,128)(2,1)} %prepare.1.refs_0_), channel_id=1, source_target_pairs={{0,8},{1,57},{2,10},{3,59},{4,12},{5,61},{6,14},{7,63},{8,16},{9,1... | collective-permute-start | bytes 417800 | tf_op jit(solution)/shard_map/ppermute | solution.py:29
  15.2 16.4 %collective-permute-start.4 = (bf16[32,2176]{1,0:T(8,128)(2,1)}, bf16[32,2176]{1,0:T(8,128)(2,1)S(1)}, u32[]{:S(2)}, u32[]{:S(2)}) collective-permute-start(bf16[32,2176]{1,0:T(8,128)(2,1)} %prepare.1.refs_0_), channel_id=1, source_target_pairs={{0,1},{1,0},{2,3},{3,2},{4,5},{5,4},{6,7},{7,6},{8,9},{9,8},{10,11... | collective-permute-start | bytes 417800 | tf_op jit(solution)/shard_map/ppermute | solution.py:29
  29.6 10.8 %collective-permute-start.1 = (bf16[32,2176]{1,0:T(8,128)(2,1)S(1)}, bf16[32,2176]{1,0:T(8,128)(2,1)S(1)}, u32[]{:S(2)}, u32[]{:S(2)}) collective-permute-start(bf16[32,2176]{1,0:T(8,128)(2,1)S(1)} %collective-permute-done.refs_1_), channel_id=1, source_target_pairs={{0,8},{1,57},{2,10},{3,59},{4,12},{5,61},{6,14},{7,63},{8,16},{9,1... | collective-permute-start | bytes 417800 | tf_op jit(solution)/shard_map/ppermute | solution.py:29
  31.6 19.6 %collective-permute-start.5 = (bf16[32,2176]{1,0:T(8,128)(2,1)S(1)}, bf16[32,2176]{1,0:T(8,128)(2,1)S(1)}, u32[]{:S(2)}, u32[]{:S(2)}) collective-permute-start(bf16[32,2176]{1,0:T(8,128)(2,1)S(1)} %collective-permute-done.4), channel_id=1, source_target_pairs={{0,8},{1,57},{2,10},{3,59},{4,12},{5,61},{6,14},{7,63},{8,16},{9,1... | collective-permute-start | bytes 417800 | tf_op jit(solution)/shard_map/ppermute | solution.py:29
  40.5 19.1 %collective-permute-start.2 = (bf16[32,2176]{1,0:T(8,128)(2,1)S(1)}, bf16[32,2176]{1,0:T(8,128)(2,1)S(1)}, u32[]{:S(2)}, u32[]{:S(2)}) collective-permute-start(bf16[32,2176]{1,0:T(8,128)(2,1)S(1)} %collective-permute-done.1.refs_2_), channel_id=1, source_target_pairs={{0,8},{1,57},{2,10},{3,59},{4,12},{5,61},{6,14},{7,63},{8,16},{9,1... | collective-permute-start | bytes 417800 | tf_op jit(solution)/shard_map/ppermute | solution.py:29
  51.2 17.5 %collective-permute-start.6 = (bf16[32,2176]{1,0:T(8,128)(2,1)S(1)}, bf16[32,2176]{1,0:T(8,128)(2,1)S(1)}, u32[]{:S(2)}, u32[]{:S(2)}) collective-permute-start(bf16[32,2176]{1,0:T(8,128)(2,1)S(1)} %collective-permute-done.5.refs_5_), channel_id=1, source_target_pairs={{0,8},{1,57},{2,10},{3,59},{4,12},{5,61},{6,14},{7,63},{8,16},{9,1... | collective-permute-start | bytes 417800 | tf_op jit(solution)/shard_map/ppermute | solution.py:29
  59.6 17.4 %collective-permute-start.3 = (bf16[32,2176]{1,0:T(8,128)(2,1)S(1)}, bf16[32,2176]{1,0:T(8,128)(2,1)S(1)}, u32[]{:S(2)}, u32[]{:S(2)}) collective-permute-start(bf16[32,2176]{1,0:T(8,128)(2,1)S(1)} %collective-permute-done.2.refs_3_), channel_id=1, source_target_pairs={{0,8},{1,57},{2,10},{3,59},{4,12},{5,61},{6,14},{7,63},{8,16},{9,1... | collective-permute-start | bytes 417800 | tf_op jit(solution)/shard_map/ppermute | solution.py:29
  68.7 15.0 %collective-permute-start.7 = (bf16[32,2176]{1,0:T(8,128)(2,1)S(1)}, bf16[32,2176]{1,0:T(8,128)(2,1)S(1)}, u32[]{:S(2)}, u32[]{:S(2)}) collective-permute-start(bf16[32,2176]{1,0:T(8,128)(2,1)S(1)} %collective-permute-done.6.refs_6_), channel_id=1, source_target_pairs={{0,8},{1,57},{2,10},{3,59},{4,12},{5,61},{6,14},{7,63},{8,16},{9,1... | collective-permute-start | bytes 417800 | tf_op jit(solution)/shard_map/ppermute | solution.py:29
  83.7 0.9 copy-start.2
  86.2 0.8 copy-start.1
  87.0 27.3 %collective-permute-start.10 = (bf16[96,2048]{1,0:T(8,128)(2,1)S(1)}, bf16[96,2048]{1,0:T(8,128)(2,1)S(1)}, u32[]{:S(2)}, u32[]{:S(2)}) collective-permute-start(bf16[96,2048]{1,0:T(8,128)(2,1)S(1)} %get-tuple-element.32), channel_id=1, source_target_pairs={{0,2},{1,3},{2,4},{3,5},{4,6},{5,7},{6,8},{7,9},{8,10},{9,11},{10,... | collective-permute-start | bytes 1179656 | tf_op jit(solution)/shard_map/ppermute | solution.py:29
  88.9 25.4 %collective-permute-start.11 = (bf16[96,2048]{1,0:T(8,128)(2,1)S(1)}, bf16[96,2048]{1,0:T(8,128)(2,1)S(1)}, u32[]{:S(2)}, u32[]{:S(2)}) collective-permute-start(bf16[96,2048]{1,0:T(8,128)(2,1)S(1)} %get-tuple-element.33), channel_id=1, source_target_pairs={{0,62},{1,63},{2,0},{3,1},{4,2},{5,3},{6,4},{7,5},{8,6},{9,7},{10,... | collective-permute-start | bytes 1179656 | tf_op jit(solution)/shard_map/ppermute | solution.py:29
  94.7 19.5 %collective-permute-start.12 = (bf16[48,2048]{1,0:T(8,128)(2,1)S(1)}, bf16[48,2048]{1,0:T(8,128)(2,1)S(1)}, u32[]{:S(2)}, u32[]{:S(2)}) collective-permute-start(bf16[48,2048]{1,0:T(8,128)(2,1)S(1)} %get-tuple-element.34), channel_id=1, source_target_pairs={{0,4},{1,5},{2,6},{3,7},{4,8},{5,9},{6,10},{7,11},{8,12},{9,13},{1... | collective-permute-start | bytes 589832 | tf_op jit(solution)/shard_map/ppermute | solution.py:29
  96.7 17.5 %collective-permute-start.13 = (bf16[48,2048]{1,0:T(8,128)(2,1)S(1)}, bf16[48,2048]{1,0:T(8,128)(2,1)S(1)}, u32[]{:S(2)}, u32[]{:S(2)}) collective-permute-start(bf16[48,2048]{1,0:T(8,128)(2,1)S(1)} %get-tuple-element.35), channel_id=1, source_target_pairs={{0,60},{1,61},{2,62},{3,63},{4,0},{5,1},{6,2},{7,3},{8,4},{9,5},{1... | collective-permute-start | bytes 589832 | tf_op jit(solution)/shard_map/ppermute | solution.py:29
  114.2 33.8 %copy-start = (bf16[96,2048]{1,0:T(8,128)(2,1)S(1)}, bf16[96,2048]{1,0:T(8,128)(2,1)}, u32[]{:S(2)}) copy-start(bf16[96,2048]{1,0:T(8,128)(2,1)} %experts.2.refs_0_) | copy-start | bytes 1179652
  114.2 33.8 %copy-start.3 = (bf16[1,32,2048]{2,1,0:T(8,128)(2,1)S(1)}, bf16[1,32,2048]{2,1,0:T(8,128)(2,1)}, u32[]{:S(2)}) copy-start(bf16[1,32,2048]{2,1,0:T(8,128)(2,1)} %tokens.3) | copy-start | bytes 393220
  114.3 0.9 copy-start.4
  115.1 0.8 copy-start.5
  128.2 19.1 %collective-permute-start.14 = (bf16[96,2048]{1,0:T(8,128)(2,1)}, bf16[96,2048]{1,0:T(8,128)(2,1)S(1)}, u32[]{:S(2)}, u32[]{:S(2)}) collective-permute-start(bf16[96,2048]{1,0:T(8,128)(2,1)} %get-tuple-element.41), channel_id=1, source_target_pairs={{0,62},{1,63},{2,0},{3,1},{4,2},{5,3},{6,4},{7,5},{8,6},{9,7},{10,... | collective-permute-start | bytes 1179656 | tf_op jit(solution)/shard_map/ppermute | solution.py:29
  130.9 17.1 %collective-permute-start.15 = (bf16[96,2048]{1,0:T(8,128)(2,1)}, bf16[96,2048]{1,0:T(8,128)(2,1)S(1)}, u32[]{:S(2)}, u32[]{:S(2)}) collective-permute-start(bf16[96,2048]{1,0:T(8,128)(2,1)} %get-tuple-element.42), channel_id=1, source_target_pairs={{0,2},{1,3},{2,4},{3,5},{4,6},{5,7},{6,8},{7,9},{8,10},{9,11},{10,... | collective-permute-start | bytes 1179656 | tf_op jit(solution)/shard_map/ppermute | solution.py:29
  134.0 11.4 %collective-permute-start.16 = (bf16[48,2048]{1,0:T(8,128)(2,1)}, bf16[48,2048]{1,0:T(8,128)(2,1)S(1)}, u32[]{:S(2)}, u32[]{:S(2)}) collective-permute-start(bf16[48,2048]{1,0:T(8,128)(2,1)} %get-tuple-element.43), channel_id=1, source_target_pairs={{0,60},{1,61},{2,62},{3,63},{4,0},{5,1},{6,2},{7,3},{8,4},{9,5},{1... | collective-permute-start | bytes 589832 | tf_op jit(solution)/shard_map/ppermute | solution.py:29
  136.2 11.1 %collective-permute-start.17 = (bf16[48,2048]{1,0:T(8,128)(2,1)}, bf16[48,2048]{1,0:T(8,128)(2,1)S(1)}, u32[]{:S(2)}, u32[]{:S(2)}) collective-permute-start(bf16[48,2048]{1,0:T(8,128)(2,1)} %get-tuple-element.44), channel_id=1, source_target_pairs={{0,4},{1,5},{2,6},{3,7},{4,8},{5,9},{6,10},{7,11},{8,12},{9,13},{1... | collective-permute-start | bytes 589832 | tf_op jit(solution)/shard_map/ppermute | solution.py:29
  149.2 15.5 %collective-permute-start.19 = (bf16[32,2048]{1,0:T(8,128)(2,1)S(1)}, bf16[32,2048]{1,0:T(8,128)(2,1)S(1)}, u32[]{:S(2)}, u32[]{:S(2)}) collective-permute-start(bf16[32,2048]{1,0:T(8,128)(2,1)S(1)} %get-tuple-element.49), channel_id=1, source_target_pairs={{0,56},{1,9},{2,58},{3,11},{4,60},{5,13},{6,62},{7,15},{8,0},{9,17... | collective-permute-start | bytes 393224 | tf_op jit(solution)/shard_map/ppermute | solution.py:29
  153.4 17.7 %collective-permute-start.23 = (bf16[32,2048]{1,0:T(8,128)(2,1)S(1)}, bf16[32,2048]{1,0:T(8,128)(2,1)S(1)}, u32[]{:S(2)}, u32[]{:S(2)}) collective-permute-start(bf16[32,2048]{1,0:T(8,128)(2,1)S(1)} %get-tuple-element.52), channel_id=1, source_target_pairs={{0,56},{1,9},{2,58},{3,11},{4,60},{5,13},{6,62},{7,15},{8,0},{9,17... | collective-permute-start | bytes 393224 | tf_op jit(solution)/shard_map/ppermute | solution.py:29
  161.3 39.7 %collective-permute-start.18 = (f32[32,2048]{1,0:T(8,128)S(1)}, f32[32,2048]{1,0:T(8,128)S(1)}, u32[]{:S(2)}, u32[]{:S(2)}) collective-permute-start(f32[32,2048]{1,0:T(8,128)S(1)} %get-tuple-element.45), channel_id=1, source_target_pairs={{0,64},{1,65},{2,66},{3,67},{4,68},{5,69},{6,70},{7,71},{8,72},{9,... | collective-permute-start | bytes 786440 | tf_op jit(solution)/shard_map/ppermute | solution.py:35
  164.8 12.6 %collective-permute-start.20 = (bf16[32,2048]{1,0:T(8,128)(2,1)S(1)}, bf16[32,2048]{1,0:T(8,128)(2,1)S(1)}, u32[]{:S(2)}, u32[]{:S(2)}) collective-permute-start(bf16[32,2048]{1,0:T(8,128)(2,1)S(1)} %add_convert_fusion.5), channel_id=1, source_target_pairs={{0,56},{1,9},{2,58},{3,11},{4,60},{5,13},{6,62},{7,15},{8,0},{9,17... | collective-permute-start | bytes 393224 | tf_op jit(solution)/shard_map/ppermute | solution.py:29
  171.2 13.5 %collective-permute-start.24 = (bf16[32,2048]{1,0:T(8,128)(2,1)S(1)}, bf16[32,2048]{1,0:T(8,128)(2,1)S(1)}, u32[]{:S(2)}, u32[]{:S(2)}) collective-permute-start(bf16[32,2048]{1,0:T(8,128)(2,1)S(1)} %add_convert_fusion.2), channel_id=1, source_target_pairs={{0,56},{1,9},{2,58},{3,11},{4,60},{5,13},{6,62},{7,15},{8,0},{9,17... | collective-permute-start | bytes 393224 | tf_op jit(solution)/shard_map/ppermute | solution.py:29
  177.5 15.8 %collective-permute-start.21 = (bf16[32,2048]{1,0:T(8,128)(2,1)S(1)}, bf16[32,2048]{1,0:T(8,128)(2,1)S(1)}, u32[]{:S(2)}, u32[]{:S(2)}) collective-permute-start(bf16[32,2048]{1,0:T(8,128)(2,1)S(1)} %add_convert_fusion.4), channel_id=1, source_target_pairs={{0,56},{1,9},{2,58},{3,11},{4,60},{5,13},{6,62},{7,15},{8,0},{9,17... | collective-permute-start | bytes 393224 | tf_op jit(solution)/shard_map/ppermute | solution.py:29
  184.8 16.2 %collective-permute-start.25 = (bf16[32,2048]{1,0:T(8,128)(2,1)S(1)}, bf16[32,2048]{1,0:T(8,128)(2,1)S(1)}, u32[]{:S(2)}, u32[]{:S(2)}) collective-permute-start(bf16[32,2048]{1,0:T(8,128)(2,1)S(1)} %add_convert_fusion.1), channel_id=1, source_target_pairs={{0,121},{1,72},{2,123},{3,74},{4,125},{5,76},{6,127},{7,78},{8,65}... | collective-permute-start | bytes 393224 | tf_op jit(solution)/shard_map/ppermute | solution.py:35
  193.3 17.8 %collective-permute-start.22 = (bf16[32,2048]{1,0:T(8,128)(2,1)S(1)}, bf16[32,2048]{1,0:T(8,128)(2,1)S(1)}, u32[]{:S(2)}, u32[]{:S(2)}) collective-permute-start(bf16[32,2048]{1,0:T(8,128)(2,1)S(1)} %add_convert_fusion.3), channel_id=1, source_target_pairs={{0,120},{1,73},{2,122},{3,75},{4,124},{5,77},{6,126},{7,79},{8,64}... | collective-permute-start | bytes 393224 | tf_op jit(solution)/shard_map/ppermute | solution.py:35
  (2 other events, 1.4 us)

commit v5 on v4

--- a/solution.py
+++ b/solution.py
@@ -15,7 +15,7 @@
 BLOCKS = 8
 SEG = BLOCKS * CAP
 SLOTS = 8 * SEG
-TILES = 3
+UP, TILES = 4, 3
 
 
 def send(value, up, down, other=False, onward=0):
@@ -122,85 +122,76 @@
 
 
 def expert_kernel(n, place, *refs):
-    ins, (g0, u0, d0, g1, u1, d1) = refs[:n], refs[n : n + 6]
-    outs, (x, acc) = refs[n + 6 : 2 * n + 6], refs[2 * n + 6 :]
-    i = pl.program_id(0)
-    turn, tile = i // TILES, i % TILES
+    ins, sources, outs = refs[:n], refs[n : n + 4], refs[n + 4 : 2 * n + 4]
+    x, wide, deep, acc, sems = refs[2 * n + 4 :]
     core = place[0] & 1
-    which = jnp.where(turn == 0, core, 1 - core)
+    hid, width = deep.shape[1], deep.shape[2]
+
+    def fetch(turn, tile):
+        to, at = (wide, tile) if tile < UP else (deep, tile - UP)
+        step = to.shape[1] // (UP if tile < UP else TILES)
+        rows = slice(at * step, (at + 1) * step)
+        source = sources[2 * turn + (tile >= UP)]
+        return pltpu.make_async_copy(source.at[0, rows], to.at[turn, rows], sems.at[turn, tile])
+
+    for turn in range(2):
+        for tile in range(UP + TILES):
+            fetch(turn, tile).start()
 
     def parts(pieces, e):
         found = [piece.at[e * SEG : (e + 1) * SEG] for piece in pieces if piece.shape[0] == 2 * SEG]
         single = [piece for piece in pieces if piece.shape[0] == SEG]
         return found + single[e : e + 1]
 
-    for e in range(2):
-        @pl.when((tile == 0) & (which == e))
-        def _():
-            for at, piece in enumerate(parts(ins, e)):
-                x[at * SEG : (at + 1) * SEG] = piece[...]
-
-    def work(g, u, d):
-        gate = jnp.dot(x[...], g[0], preferred_element_type=jnp.float32)
-        lift = jnp.dot(x[...], u[0], preferred_element_type=jnp.float32)
-        hidden = (gate / (1.0 + jnp.exp(-gate)) * lift).astype(jnp.bfloat16)
-        y = jnp.dot(hidden, d[0], preferred_element_type=jnp.float32)
-
-        @pl.when(tile == 0)
-        def _():
-            acc[...] = y
-
-        @pl.when(tile > 0)
-        def _():
-            acc[...] += y
-
-    @pl.when(turn == 0)
-    def _():
-        work(g0, u0, d0)
-
-    @pl.when(turn == 1)
-    def _():
-        work(g1, u1, d1)
-
-    for e in range(2):
-        @pl.when((tile == TILES - 1) & (which == e))
-        def _():
-            for at, piece in enumerate(parts(outs, e)):
-                piece[...] = acc[at * SEG : (at + 1) * SEG].astype(jnp.bfloat16)
+    for turn in range(2):
+        which = core if turn == 0 else 1 - core
+        for e in range(2):
+            @pl.when(which == e)
+            def _():
+                for at, piece in enumerate(parts(ins, e)):
+                    x[at * SEG : (at + 1) * SEG] = piece[...]
+
+        step = width // UP
+        gated = None
+        for tile in range(UP):
+            fetch(turn, tile).wait()
+            rows = slice(tile * step, (tile + 1) * step)
+            y = jnp.dot(x[:, rows], wide[turn, rows], preferred_element_type=jnp.float32)
+            gated = y if gated is None else gated + y
+        gate = gated[:, :hid]
+        hidden = (gate / (1.0 + jnp.exp(-gate)) * gated[:, hid:]).astype(jnp.bfloat16)
+        step = hid // TILES
+        for tile in range(TILES):
+            fetch(turn, UP + tile).wait()
+            rows = slice(tile * step, (tile + 1) * step)
+            y = jnp.dot(hidden[:, rows], deep[turn, rows], preferred_element_type=jnp.float32)
+            if tile == 0:
+                acc[...] = y
+            else:
+                acc[...] += y
+        for e in range(2):
+            @pl.when(which == e)
+            def _():
+                for at, piece in enumerate(parts(outs, e)):
+                    piece[...] = acc[at * SEG : (at + 1) * SEG].astype(jnp.bfloat16)
 
 
 def experts(place, pieces, own_gu, own_d, other_gu, other_d):
     width, hid = own_gu.shape[1], own_d.shape[1]
-    tile = hid // TILES
     rows = sum(p.shape[0] for p in pieces) // 2
-    whole = [pl.BlockSpec(p.shape, lambda i, c: (0, 0)) for p in pieces]
-
-    def early(i):
-        return jnp.minimum(i, TILES - 1)
-
-    def late(i):
-        return jnp.maximum(i - TILES, 0)
-
-    def weights(at):
-        return [
-            pl.BlockSpec((1, width, tile), lambda i, c: (0, 0, at(i))),
-            pl.BlockSpec((1, width, tile), lambda i, c: (0, 0, at(i) + TILES)),
-            pl.BlockSpec((1, tile, width), lambda i, c: (0, at(i), 0)),
-        ]
-
+    vmem = [pl.BlockSpec(memory_space=pltpu.VMEM)] * len(pieces)
     return pl.pallas_call(
         functools.partial(expert_kernel, len(pieces)),
-        grid_spec=pltpu.PrefetchScalarGridSpec(
-            num_scalar_prefetch=1,
-            grid=(2 * TILES,),
-            in_specs=whole + weights(early) + weights(late),
-            out_specs=whole,
-            scratch_shapes=[
-                pltpu.VMEM((rows, width), jnp.bfloat16),
-                pltpu.VMEM((rows, width), jnp.float32),
-            ],
-        ),
+        in_specs=[pl.BlockSpec(memory_space=pltpu.SMEM)] + vmem + [pl.BlockSpec(memory_space=pl.ANY)] * 4,
+        out_specs=vmem,
         out_shape=[jax.ShapeDtypeStruct(p.shape, jnp.bfloat16) for p in pieces],
+        scratch_shapes=[
+            pltpu.VMEM((rows, width), jnp.bfloat16),
+            pltpu.VMEM((2, width, 2 * hid), jnp.bfloat16),
+            pltpu.VMEM((2, hid, width), jnp.bfloat16),
+            pltpu.VMEM((rows, width), jnp.float32),
+            pltpu.SemaphoreType.DMA((2, UP + TILES)),
+        ],
         compiler_params=pltpu.CompilerParams(vmem_limit_bytes=56 * 2**20),
         cost_estimate=pl.CostEstimate(
             flops=2 * 2 * rows * 3 * width * hid,
@@ -208,7 +199,7 @@
             transcendentals=2 * rows * hid,
         ),
         name="experts",
-    )(place, *pieces, own_gu, own_gu, own_d, other_gu, other_gu, other_d)
+    )(place, *pieces, own_gu, own_d, other_gu, other_d)
 
 
 def combine_kernel(hi, lo, tokens, *refs):

time: 213 us -> 208 us (0.977)
  waiting for transfers between devices: 43 us -> 53.9 us
  starting transfers between devices: 136 us -> 126 us
  Pallas kernels: 28.4 us -> 22.3 us
    ppermute x23, waiting for transfers between devices: 32.8 us -> 45 us  [send(): return lax.ppermute(value, 'expert', [(i, place(i)) for i in range(count)])]
    ppermute x23, starting transfers between devices: 123 us -> 116 us  [send(): return lax.ppermute(value, 'expert', [(i, place(i)) for i in range(count)])]
    pallas_call x2, Pallas kernels: 23.8 us -> 17.7 us  [experts(): pl.pallas_call(functools.partial(expert_kernel, len(pieces)), in_specs=[p...]
    ppermute x3, starting transfers between devices: 13 us -> 10.3 us  [send(): return lax.ppermute(value, ('section', 'expert'), pairs)]
  transfers between devices with their start and end apart: 26 -> 26, of which waited for: 10 -> 11; matrix products, arithmetic and copies ran while one was open for 0% -> 0% of each run, Pallas kernels for 7% -> 6%
where the time goes in v5:
time: 208 us; the launch traced here: 207 us
  starting transfers between devices  126 us (61%)
  waiting for transfers between devices  53.9 us (26%)
  Pallas kernels  22.3 us (11%)
  local copies, waits for them, and re-layouts  3.3 us (2%)
    ppermute x23, starting transfers between devices, send(): return lax.ppermute(value, 'expert', [(i, place(i)) for i in range(count)])  116 us
    ppermute x23, waiting for transfers between devices, send(): return lax.ppermute(value, 'expert', [(i, place(i)) for i in range(count)])  45 us
    pallas_call x2, Pallas kernels, experts(): pl.pallas_call(functools.partial(expert_kernel, len(pieces)), in_specs=[p...  17.7 us
    ppermute x3, starting transfers between devices, send(): return lax.ppermute(value, ('section', 'expert'), pairs)  10.3 us
    ppermute x3, waiting for transfers between devices, send(): return lax.ppermute(value, ('section', 'expert'), pairs)  8.94 us
  transfers between devices with their start and end apart: 26, of which 11 were waited for; matrix products, arithmetic and copies ran while one was open for 0% of the time, Pallas kernels for 6%

profile of v5, /device:TPU:6, one launch (start us, length us, event | category | flops | bytes accessed | tf_op | source)
XLA Modules:
  0.0 207.2 jit_solution(5702987168334415273)
XLA Ops:
  1.9 2.4 %collective-permute-start.9 = (bf16[1,768,2048]{2,1,0:T(8,128)(2,1)}, bf16[1,768,2048]{2,1,0:T(8,128)(2,1)}, u32[]{:S(2)}, u32[]{:S(2)}) collective-permute-start(bf16[1,768,2048]{2,1,0:T(8,128)(2,1)} %refs_5_.1), channel_id=1, source_target_pairs={{0,1},{1,0},{2,3},{3,2},{4,5},{5,4},{6,7},{7,6},{8,9},{9,8},{10,11... | collective-permute-start | bytes 9437192 | tf_op jit(solution)/shard_map/ppermute | solution.py:29
  6.1 9.1 %collective-permute-start = (bf16[32,2176]{1,0:T(8,128)(2,1)}, bf16[32,2176]{1,0:T(8,128)(2,1)S(1)}, u32[]{:S(2)}, u32[]{:S(2)}) collective-permute-start(bf16[32,2176]{1,0:T(8,128)(2,1)} %prepare.1.refs_0_), channel_id=1, source_target_pairs={{0,8},{1,57},{2,10},{3,59},{4,12},{5,61},{6,14},{7,63},{8,16},{9,1... | collective-permute-start | bytes 417800 | tf_op jit(solution)/shard_map/ppermute | solution.py:29
  15.2 12.6 %collective-permute-start.4 = (bf16[32,2176]{1,0:T(8,128)(2,1)}, bf16[32,2176]{1,0:T(8,128)(2,1)S(1)}, u32[]{:S(2)}, u32[]{:S(2)}) collective-permute-start(bf16[32,2176]{1,0:T(8,128)(2,1)} %prepare.1.refs_0_), channel_id=1, source_target_pairs={{0,1},{1,0},{2,3},{3,2},{4,5},{5,4},{6,7},{7,6},{8,9},{9,8},{10,11... | collective-permute-start | bytes 417800 | tf_op jit(solution)/shard_map/ppermute | solution.py:29
  31.6 8.2 %collective-permute-start.5 = (bf16[32,2176]{1,0:T(8,128)(2,1)S(1)}, bf16[32,2176]{1,0:T(8,128)(2,1)S(1)}, u32[]{:S(2)}, u32[]{:S(2)}) collective-permute-start(bf16[32,2176]{1,0:T(8,128)(2,1)S(1)} %collective-permute-done.4), channel_id=1, source_target_pairs={{0,8},{1,57},{2,10},{3,59},{4,12},{5,61},{6,14},{7,63},{8,16},{9,1... | collective-permute-start | bytes 417800 | tf_op jit(solution)/shard_map/ppermute | solution.py:29
  40.5 7.4 %collective-permute-start.2 = (bf16[32,2176]{1,0:T(8,128)(2,1)S(1)}, bf16[32,2176]{1,0:T(8,128)(2,1)S(1)}, u32[]{:S(2)}, u32[]{:S(2)}) collective-permute-start(bf16[32,2176]{1,0:T(8,128)(2,1)S(1)} %collective-permute-done.1.refs_2_), channel_id=1, source_target_pairs={{0,8},{1,57},{2,10},{3,59},{4,12},{5,61},{6,14},{7,63},{8,16},{9,1... | collective-permute-start | bytes 417800 | tf_op jit(solution)/shard_map/ppermute | solution.py:29
  47.9 3.3 %collective-permute-done.5.refs_5_ = bf16[32,2176]{1,0:T(8,128)(2,1)S(1)} collective-permute-done((bf16[32,2176]{1,0:T(8,128)(2,1)S(1)}, bf16[32,2176]{1,0:T(8,128)(2,1)S(1)}, u32[]{:S(2)}, u32[]{:S(2)}) %collective-permute-start.5) | collective-permute-done | bytes 139296 | tf_op jit(solution)/shard_map/ppermute | solution.py:29
  51.2 8.4 %collective-permute-start.6 = (bf16[32,2176]{1,0:T(8,128)(2,1)S(1)}, bf16[32,2176]{1,0:T(8,128)(2,1)S(1)}, u32[]{:S(2)}, u32[]{:S(2)}) collective-permute-start(bf16[32,2176]{1,0:T(8,128)(2,1)S(1)} %collective-permute-done.5.refs_5_), channel_id=1, source_target_pairs={{0,8},{1,57},{2,10},{3,59},{4,12},{5,61},{6,14},{7,63},{8,16},{9,1... | collective-permute-start | bytes 417800 | tf_op jit(solution)/shard_map/ppermute | solution.py:29
  59.6 2.5 %collective-permute-start.3 = (bf16[32,2176]{1,0:T(8,128)(2,1)S(1)}, bf16[32,2176]{1,0:T(8,128)(2,1)S(1)}, u32[]{:S(2)}, u32[]{:S(2)}) collective-permute-start(bf16[32,2176]{1,0:T(8,128)(2,1)S(1)} %collective-permute-done.2.refs_3_), channel_id=1, source_target_pairs={{0,8},{1,57},{2,10},{3,59},{4,12},{5,61},{6,14},{7,63},{8,16},{9,1... | collective-permute-start | bytes 417800 | tf_op jit(solution)/shard_map/ppermute | solution.py:29
  62.2 6.5 %collective-permute-done.6.refs_6_ = bf16[32,2176]{1,0:T(8,128)(2,1)S(1)} collective-permute-done((bf16[32,2176]{1,0:T(8,128)(2,1)S(1)}, bf16[32,2176]{1,0:T(8,128)(2,1)S(1)}, u32[]{:S(2)}, u32[]{:S(2)}) %collective-permute-start.6) | collective-permute-done | bytes 139296 | tf_op jit(solution)/shard_map/ppermute | solution.py:29
  68.7 8.4 %collective-permute-start.7 = (bf16[32,2176]{1,0:T(8,128)(2,1)S(1)}, bf16[32,2176]{1,0:T(8,128)(2,1)S(1)}, u32[]{:S(2)}, u32[]{:S(2)}) collective-permute-start(bf16[32,2176]{1,0:T(8,128)(2,1)S(1)} %collective-permute-done.6.refs_6_), channel_id=1, source_target_pairs={{0,8},{1,57},{2,10},{3,59},{4,12},{5,61},{6,14},{7,63},{8,16},{9,1... | collective-permute-start | bytes 417800 | tf_op jit(solution)/shard_map/ppermute | solution.py:29
  77.1 6.6 %collective-permute-done.7.refs_7_ = bf16[32,2176]{1,0:T(8,128)(2,1)S(1)} collective-permute-done((bf16[32,2176]{1,0:T(8,128)(2,1)S(1)}, bf16[32,2176]{1,0:T(8,128)(2,1)S(1)}, u32[]{:S(2)}, u32[]{:S(2)}) %collective-permute-start.7) | collective-permute-done | bytes 139296 | tf_op jit(solution)/shard_map/ppermute | solution.py:29
  88.9 5.8 %collective-permute-start.11 = (bf16[96,2048]{1,0:T(8,128)(2,1)S(1)}, bf16[96,2048]{1,0:T(8,128)(2,1)S(1)}, u32[]{:S(2)}, u32[]{:S(2)}) collective-permute-start(bf16[96,2048]{1,0:T(8,128)(2,1)S(1)} %get-tuple-element.33), channel_id=1, source_target_pairs={{0,62},{1,63},{2,0},{3,1},{4,2},{5,3},{6,4},{7,5},{8,6},{9,7},{10,... | collective-permute-start | bytes 1179656 | tf_op jit(solution)/shard_map/ppermute | solution.py:29
  96.7 6.0 %collective-permute-start.13 = (bf16[48,2048]{1,0:T(8,128)(2,1)S(1)}, bf16[48,2048]{1,0:T(8,128)(2,1)S(1)}, u32[]{:S(2)}, u32[]{:S(2)}) collective-permute-start(bf16[48,2048]{1,0:T(8,128)(2,1)S(1)} %get-tuple-element.35), channel_id=1, source_target_pairs={{0,60},{1,61},{2,62},{3,63},{4,0},{5,1},{6,2},{7,3},{8,4},{9,5},{1... | collective-permute-start | bytes 589832 | tf_op jit(solution)/shard_map/ppermute | solution.py:29
  102.7 8.6 %experts.2.refs_0_ = bf16[96,2048]{1,0:T(8,128)(2,1)} custom-call(s32[1]{0:T(128)} %bitcast.place, bf16[96,2048]{1,0:T(8,128)(2,1)} %copy-done.1, bf16[1,2048,1536]{2,1,0:T(8,128)(2,1)} %refs_4_.1, bf16[1,768,2048]{2,1,0:T(8,128)(2,1)} %refs_5_.1, bf16[1,2048,1536]{2,1,0:T(8,128)(2,1)} %collective-permute-done.8.refs_3_.refs_6_, ...), custom_call_target="tpu_custom_call" | custom-call | flops 905969664 | bytes 18874368 | tf_op jit(solution)/shard_map/experts/pallas_call | solution.py:183
  113.0 9.1 %experts.3 = (bf16[96,2048]{1,0:T(8,128)(2,1)}, bf16[96,2048]{1,0:T(8,128)(2,1)}, bf16[48,2048]{1,0:T(8,128)(2,1)}, bf16[48,2048]{1,0:T(8,128)(2,1)}) custom-call(s32[1]{0:T(128)} %bitcast.place, bf16[96,2048]{1,0:T(8,128)(2,1)} %copy-done.4, bf16[96,2048]{1,0:T(8,128)(2,1)} %copy-done.5, bf16[48,2048]{1,0:T(8,128)(2,1)} %copy-done.6, ...), custom_call_target="tpu_custom_call" | custom-call | flops 2717908992 | bytes 18874368 | tf_op jit(solution)/shard_map/experts/pallas_call | solution.py:183
  122.1 2.7 %collective-permute-start.14 = (bf16[96,2048]{1,0:T(8,128)(2,1)}, bf16[96,2048]{1,0:T(8,128)(2,1)S(1)}, u32[]{:S(2)}, u32[]{:S(2)}) collective-permute-start(bf16[96,2048]{1,0:T(8,128)(2,1)} %get-tuple-element.41), channel_id=1, source_target_pairs={{0,62},{1,63},{2,0},{3,1},{4,2},{5,3},{6,4},{7,5},{8,6},{9,7},{10,... | collective-permute-start | bytes 1179656 | tf_op jit(solution)/shard_map/ppermute | solution.py:29
  124.9 3.1 %collective-permute-start.15 = (bf16[96,2048]{1,0:T(8,128)(2,1)}, bf16[96,2048]{1,0:T(8,128)(2,1)S(1)}, u32[]{:S(2)}, u32[]{:S(2)}) collective-permute-start(bf16[96,2048]{1,0:T(8,128)(2,1)} %get-tuple-element.42), channel_id=1, source_target_pairs={{0,2},{1,3},{2,4},{3,5},{4,6},{5,7},{6,8},{7,9},{8,10},{9,11},{10,... | collective-permute-start | bytes 1179656 | tf_op jit(solution)/shard_map/ppermute | solution.py:29
  128.0 3.6 %collective-permute-start.16 = (bf16[48,2048]{1,0:T(8,128)(2,1)}, bf16[48,2048]{1,0:T(8,128)(2,1)S(1)}, u32[]{:S(2)}, u32[]{:S(2)}) collective-permute-start(bf16[48,2048]{1,0:T(8,128)(2,1)} %get-tuple-element.43), channel_id=1, source_target_pairs={{0,60},{1,61},{2,62},{3,63},{4,0},{5,1},{6,2},{7,3},{8,4},{9,5},{1... | collective-permute-start | bytes 589832 | tf_op jit(solution)/shard_map/ppermute | solution.py:29
  131.6 3.8 %collective-permute-start.17 = (bf16[48,2048]{1,0:T(8,128)(2,1)}, bf16[48,2048]{1,0:T(8,128)(2,1)S(1)}, u32[]{:S(2)}, u32[]{:S(2)}) collective-permute-start(bf16[48,2048]{1,0:T(8,128)(2,1)} %get-tuple-element.44), channel_id=1, source_target_pairs={{0,4},{1,5},{2,6},{3,7},{4,8},{5,9},{6,10},{7,11},{8,12},{9,13},{1... | collective-permute-start | bytes 589832 | tf_op jit(solution)/shard_map/ppermute | solution.py:29
  135.4 5.3 %collective-permute-done.16.refs_3_ = bf16[48,2048]{1,0:T(8,128)(2,1)S(1)} collective-permute-done((bf16[48,2048]{1,0:T(8,128)(2,1)}, bf16[48,2048]{1,0:T(8,128)(2,1)S(1)}, u32[]{:S(2)}, u32[]{:S(2)}) %collective-permute-start.16) | collective-permute-done | bytes 196640 | tf_op jit(solution)/shard_map/ppermute | solution.py:29
  140.6 3.5 %collective-permute-done.17.refs_4_ = bf16[48,2048]{1,0:T(8,128)(2,1)S(1)} collective-permute-done((bf16[48,2048]{1,0:T(8,128)(2,1)}, bf16[48,2048]{1,0:T(8,128)(2,1)S(1)}, u32[]{:S(2)}, u32[]{:S(2)}) %collective-permute-start.17) | collective-permute-done | bytes 196640 | tf_op jit(solution)/shard_map/ppermute | solution.py:29
  145.4 2.8 %collective-permute-start.19 = (bf16[32,2048]{1,0:T(8,128)(2,1)S(1)}, bf16[32,2048]{1,0:T(8,128)(2,1)S(1)}, u32[]{:S(2)}, u32[]{:S(2)}) collective-permute-start(bf16[32,2048]{1,0:T(8,128)(2,1)S(1)} %get-tuple-element.49), channel_id=1, source_target_pairs={{0,56},{1,9},{2,58},{3,11},{4,60},{5,13},{6,62},{7,15},{8,0},{9,17... | collective-permute-start | bytes 393224 | tf_op jit(solution)/shard_map/ppermute | solution.py:29
  148.2 7.1 %collective-permute-start.23 = (bf16[32,2048]{1,0:T(8,128)(2,1)S(1)}, bf16[32,2048]{1,0:T(8,128)(2,1)S(1)}, u32[]{:S(2)}, u32[]{:S(2)}) collective-permute-start(bf16[32,2048]{1,0:T(8,128)(2,1)S(1)} %get-tuple-element.52), channel_id=1, source_target_pairs={{0,56},{1,9},{2,58},{3,11},{4,60},{5,13},{6,62},{7,15},{8,0},{9,17... | collective-permute-start | bytes 393224 | tf_op jit(solution)/shard_map/ppermute | solution.py:29
  155.3 3.5 %collective-permute-start.18 = (f32[32,2048]{1,0:T(8,128)S(1)}, f32[32,2048]{1,0:T(8,128)S(1)}, u32[]{:S(2)}, u32[]{:S(2)}) collective-permute-start(f32[32,2048]{1,0:T(8,128)S(1)} %get-tuple-element.45), channel_id=1, source_target_pairs={{0,64},{1,65},{2,66},{3,67},{4,68},{5,69},{6,70},{7,71},{8,72},{9,... | collective-permute-start | bytes 786440 | tf_op jit(solution)/shard_map/ppermute | solution.py:35
  158.8 3.3 %collective-permute-done.19 = bf16[32,2048]{1,0:T(8,128)(2,1)S(1)} collective-permute-done((bf16[32,2048]{1,0:T(8,128)(2,1)S(1)}, bf16[32,2048]{1,0:T(8,128)(2,1)S(1)}, u32[]{:S(2)}, u32[]{:S(2)}) %collective-permute-start.19) | collective-permute-done | bytes 131104 | tf_op jit(solution)/shard_map/ppermute | solution.py:29
  162.1 5.8 %collective-permute-start.20 = (bf16[32,2048]{1,0:T(8,128)(2,1)S(1)}, bf16[32,2048]{1,0:T(8,128)(2,1)S(1)}, u32[]{:S(2)}, u32[]{:S(2)}) collective-permute-start(bf16[32,2048]{1,0:T(8,128)(2,1)S(1)} %add_convert_fusion.5), channel_id=1, source_target_pairs={{0,56},{1,9},{2,58},{3,11},{4,60},{5,13},{6,62},{7,15},{8,0},{9,17... | collective-permute-start | bytes 393224 | tf_op jit(solution)/shard_map/ppermute | solution.py:29
  168.0 6.2 %collective-permute-start.24 = (bf16[32,2048]{1,0:T(8,128)(2,1)S(1)}, bf16[32,2048]{1,0:T(8,128)(2,1)S(1)}, u32[]{:S(2)}, u32[]{:S(2)}) collective-permute-start(bf16[32,2048]{1,0:T(8,128)(2,1)S(1)} %add_convert_fusion.2), channel_id=1, source_target_pairs={{0,56},{1,9},{2,58},{3,11},{4,60},{5,13},{6,62},{7,15},{8,0},{9,17... | collective-permute-start | bytes 393224 | tf_op jit(solution)/shard_map/ppermute | solution.py:29
  174.2 4.9 %collective-permute-done.20 = bf16[32,2048]{1,0:T(8,128)(2,1)S(1)} collective-permute-done((bf16[32,2048]{1,0:T(8,128)(2,1)S(1)}, bf16[32,2048]{1,0:T(8,128)(2,1)S(1)}, u32[]{:S(2)}, u32[]{:S(2)}) %collective-permute-start.20) | collective-permute-done | bytes 131104 | tf_op jit(solution)/shard_map/ppermute | solution.py:29
  179.2 2.5 %collective-permute-start.21 = (bf16[32,2048]{1,0:T(8,128)(2,1)S(1)}, bf16[32,2048]{1,0:T(8,128)(2,1)S(1)}, u32[]{:S(2)}, u32[]{:S(2)}) collective-permute-start(bf16[32,2048]{1,0:T(8,128)(2,1)S(1)} %add_convert_fusion.4), channel_id=1, source_target_pairs={{0,56},{1,9},{2,58},{3,11},{4,60},{5,13},{6,62},{7,15},{8,0},{9,17... | collective-permute-start | bytes 393224 | tf_op jit(solution)/shard_map/ppermute | solution.py:29
  183.7 9.0 %collective-permute-done.21 = bf16[32,2048]{1,0:T(8,128)(2,1)S(1)} collective-permute-done((bf16[32,2048]{1,0:T(8,128)(2,1)S(1)}, bf16[32,2048]{1,0:T(8,128)(2,1)S(1)}, u32[]{:S(2)}, u32[]{:S(2)}) %collective-permute-start.21) | collective-permute-done | bytes 131104 | tf_op jit(solution)/shard_map/ppermute | solution.py:29
  192.7 4.9 %collective-permute-start.22 = (bf16[32,2048]{1,0:T(8,128)(2,1)S(1)}, bf16[32,2048]{1,0:T(8,128)(2,1)S(1)}, u32[]{:S(2)}, u32[]{:S(2)}) collective-permute-start(bf16[32,2048]{1,0:T(8,128)(2,1)S(1)} %add_convert_fusion.3), channel_id=1, source_target_pairs={{0,120},{1,73},{2,122},{3,75},{4,124},{5,77},{6,126},{7,79},{8,64}... | collective-permute-start | bytes 393224 | tf_op jit(solution)/shard_map/ppermute | solution.py:35
  197.6 8.9 %collective-permute-done.22 = bf16[32,2048]{1,0:T(8,128)(2,1)S(1)} collective-permute-done((bf16[32,2048]{1,0:T(8,128)(2,1)S(1)}, bf16[32,2048]{1,0:T(8,128)(2,1)S(1)}, u32[]{:S(2)}, u32[]{:S(2)}) %collective-permute-start.22) | collective-permute-done | bytes 131104 | tf_op jit(solution)/shard_map/ppermute | solution.py:35
  (47 shorter events, 21.0 us)
Async XLA Ops:
  0.0 102.7 %collective-permute-start.8 = (bf16[1,2048,1536]{2,1,0:T(8,128)(2,1)}, bf16[1,2048,1536]{2,1,0:T(8,128)(2,1)}, u32[]{:S(2)}, u32[]{:S(2)}) collective-permute-start(bf16[1,2048,1536]{2,1,0:T(8,128)(2,1)} %refs_4_.1), channel_id=1, source_target_pairs={{0,1},{1,0},{2,3},{3,2},{4,5},{5,4},{6,7},{7,6},{8,9},{9,8},{10,11... | collective-permute-start | bytes 18874376 | tf_op jit(solution)/shard_map/ppermute | solution.py:29
  1.9 94.8 %collective-permute-start.9 = (bf16[1,768,2048]{2,1,0:T(8,128)(2,1)}, bf16[1,768,2048]{2,1,0:T(8,128)(2,1)}, u32[]{:S(2)}, u32[]{:S(2)}) collective-permute-start(bf16[1,768,2048]{2,1,0:T(8,128)(2,1)} %refs_5_.1), channel_id=1, source_target_pairs={{0,1},{1,0},{2,3},{3,2},{4,5},{5,4},{6,7},{7,6},{8,9},{9,8},{10,11... | collective-permute-start | bytes 9437192 | tf_op jit(solution)/shard_map/ppermute | solution.py:29
  6.1 23.5 %collective-permute-start = (bf16[32,2176]{1,0:T(8,128)(2,1)}, bf16[32,2176]{1,0:T(8,128)(2,1)S(1)}, u32[]{:S(2)}, u32[]{:S(2)}) collective-permute-start(bf16[32,2176]{1,0:T(8,128)(2,1)} %prepare.1.refs_0_), channel_id=1, source_target_pairs={{0,8},{1,57},{2,10},{3,59},{4,12},{5,61},{6,14},{7,63},{8,16},{9,1... | collective-permute-start | bytes 417800 | tf_op jit(solution)/shard_map/ppermute | solution.py:29
  15.2 16.4 %collective-permute-start.4 = (bf16[32,2176]{1,0:T(8,128)(2,1)}, bf16[32,2176]{1,0:T(8,128)(2,1)S(1)}, u32[]{:S(2)}, u32[]{:S(2)}) collective-permute-start(bf16[32,2176]{1,0:T(8,128)(2,1)} %prepare.1.refs_0_), channel_id=1, source_target_pairs={{0,1},{1,0},{2,3},{3,2},{4,5},{5,4},{6,7},{7,6},{8,9},{9,8},{10,11... | collective-permute-start | bytes 417800 | tf_op jit(solution)/shard_map/ppermute | solution.py:29
  29.6 10.8 %collective-permute-start.1 = (bf16[32,2176]{1,0:T(8,128)(2,1)S(1)}, bf16[32,2176]{1,0:T(8,128)(2,1)S(1)}, u32[]{:S(2)}, u32[]{:S(2)}) collective-permute-start(bf16[32,2176]{1,0:T(8,128)(2,1)S(1)} %collective-permute-done.refs_1_), channel_id=1, source_target_pairs={{0,8},{1,57},{2,10},{3,59},{4,12},{5,61},{6,14},{7,63},{8,16},{9,1... | collective-permute-start | bytes 417800 | tf_op jit(solution)/shard_map/ppermute | solution.py:29
  31.6 19.6 %collective-permute-start.5 = (bf16[32,2176]{1,0:T(8,128)(2,1)S(1)}, bf16[32,2176]{1,0:T(8,128)(2,1)S(1)}, u32[]{:S(2)}, u32[]{:S(2)}) collective-permute-start(bf16[32,2176]{1,0:T(8,128)(2,1)S(1)} %collective-permute-done.4), channel_id=1, source_target_pairs={{0,8},{1,57},{2,10},{3,59},{4,12},{5,61},{6,14},{7,63},{8,16},{9,1... | collective-permute-start | bytes 417800 | tf_op jit(solution)/shard_map/ppermute | solution.py:29
  40.5 19.1 %collective-permute-start.2 = (bf16[32,2176]{1,0:T(8,128)(2,1)S(1)}, bf16[32,2176]{1,0:T(8,128)(2,1)S(1)}, u32[]{:S(2)}, u32[]{:S(2)}) collective-permute-start(bf16[32,2176]{1,0:T(8,128)(2,1)S(1)} %collective-permute-done.1.refs_2_), channel_id=1, source_target_pairs={{0,8},{1,57},{2,10},{3,59},{4,12},{5,61},{6,14},{7,63},{8,16},{9,1... | collective-permute-start | bytes 417800 | tf_op jit(solution)/shard_map/ppermute | solution.py:29
  51.2 17.5 %collective-permute-start.6 = (bf16[32,2176]{1,0:T(8,128)(2,1)S(1)}, bf16[32,2176]{1,0:T(8,128)(2,1)S(1)}, u32[]{:S(2)}, u32[]{:S(2)}) collective-permute-start(bf16[32,2176]{1,0:T(8,128)(2,1)S(1)} %collective-permute-done.5.refs_5_), channel_id=1, source_target_pairs={{0,8},{1,57},{2,10},{3,59},{4,12},{5,61},{6,14},{7,63},{8,16},{9,1... | collective-permute-start | bytes 417800 | tf_op jit(solution)/shard_map/ppermute | solution.py:29
  59.6 17.4 %collective-permute-start.3 = (bf16[32,2176]{1,0:T(8,128)(2,1)S(1)}, bf16[32,2176]{1,0:T(8,128)(2,1)S(1)}, u32[]{:S(2)}, u32[]{:S(2)}) collective-permute-start(bf16[32,2176]{1,0:T(8,128)(2,1)S(1)} %collective-permute-done.2.refs_3_), channel_id=1, source_target_pairs={{0,8},{1,57},{2,10},{3,59},{4,12},{5,61},{6,14},{7,63},{8,16},{9,1... | collective-permute-start | bytes 417800 | tf_op jit(solution)/shard_map/ppermute | solution.py:29
  68.7 15.0 %collective-permute-start.7 = (bf16[32,2176]{1,0:T(8,128)(2,1)S(1)}, bf16[32,2176]{1,0:T(8,128)(2,1)S(1)}, u32[]{:S(2)}, u32[]{:S(2)}) collective-permute-start(bf16[32,2176]{1,0:T(8,128)(2,1)S(1)} %collective-permute-done.6.refs_6_), channel_id=1, source_target_pairs={{0,8},{1,57},{2,10},{3,59},{4,12},{5,61},{6,14},{7,63},{8,16},{9,1... | collective-permute-start | bytes 417800 | tf_op jit(solution)/shard_map/ppermute | solution.py:29
  83.7 0.9 copy-start.2
  86.2 0.8 copy-start.1
  87.0 24.4 %collective-permute-start.10 = (bf16[96,2048]{1,0:T(8,128)(2,1)S(1)}, bf16[96,2048]{1,0:T(8,128)(2,1)S(1)}, u32[]{:S(2)}, u32[]{:S(2)}) collective-permute-start(bf16[96,2048]{1,0:T(8,128)(2,1)S(1)} %get-tuple-element.32), channel_id=1, source_target_pairs={{0,2},{1,3},{2,4},{3,5},{4,6},{5,7},{6,8},{7,9},{8,10},{9,11},{10,... | collective-permute-start | bytes 1179656 | tf_op jit(solution)/shard_map/ppermute | solution.py:29
  88.9 22.5 %collective-permute-start.11 = (bf16[96,2048]{1,0:T(8,128)(2,1)S(1)}, bf16[96,2048]{1,0:T(8,128)(2,1)S(1)}, u32[]{:S(2)}, u32[]{:S(2)}) collective-permute-start(bf16[96,2048]{1,0:T(8,128)(2,1)S(1)} %get-tuple-element.33), channel_id=1, source_target_pairs={{0,62},{1,63},{2,0},{3,1},{4,2},{5,3},{6,4},{7,5},{8,6},{9,7},{10,... | collective-permute-start | bytes 1179656 | tf_op jit(solution)/shard_map/ppermute | solution.py:29
  94.7 16.6 %collective-permute-start.12 = (bf16[48,2048]{1,0:T(8,128)(2,1)S(1)}, bf16[48,2048]{1,0:T(8,128)(2,1)S(1)}, u32[]{:S(2)}, u32[]{:S(2)}) collective-permute-start(bf16[48,2048]{1,0:T(8,128)(2,1)S(1)} %get-tuple-element.34), channel_id=1, source_target_pairs={{0,4},{1,5},{2,6},{3,7},{4,8},{5,9},{6,10},{7,11},{8,12},{9,13},{1... | collective-permute-start | bytes 589832 | tf_op jit(solution)/shard_map/ppermute | solution.py:29
  96.7 14.6 %collective-permute-start.13 = (bf16[48,2048]{1,0:T(8,128)(2,1)S(1)}, bf16[48,2048]{1,0:T(8,128)(2,1)S(1)}, u32[]{:S(2)}, u32[]{:S(2)}) collective-permute-start(bf16[48,2048]{1,0:T(8,128)(2,1)S(1)} %get-tuple-element.35), channel_id=1, source_target_pairs={{0,60},{1,61},{2,62},{3,63},{4,0},{5,1},{6,2},{7,3},{8,4},{9,5},{1... | collective-permute-start | bytes 589832 | tf_op jit(solution)/shard_map/ppermute | solution.py:29
  111.3 32.9 %copy-start = (bf16[96,2048]{1,0:T(8,128)(2,1)S(1)}, bf16[96,2048]{1,0:T(8,128)(2,1)}, u32[]{:S(2)}) copy-start(bf16[96,2048]{1,0:T(8,128)(2,1)} %experts.2.refs_0_) | copy-start | bytes 1179652
  111.3 32.9 %copy-start.3 = (bf16[1,32,2048]{2,1,0:T(8,128)(2,1)S(1)}, bf16[1,32,2048]{2,1,0:T(8,128)(2,1)}, u32[]{:S(2)}) copy-start(bf16[1,32,2048]{2,1,0:T(8,128)(2,1)} %tokens.3) | copy-start | bytes 393220
  111.4 0.9 copy-start.4
  112.2 0.8 copy-start.5
  122.1 22.0 %collective-permute-start.14 = (bf16[96,2048]{1,0:T(8,128)(2,1)}, bf16[96,2048]{1,0:T(8,128)(2,1)S(1)}, u32[]{:S(2)}, u32[]{:S(2)}) collective-permute-start(bf16[96,2048]{1,0:T(8,128)(2,1)} %get-tuple-element.41), channel_id=1, source_target_pairs={{0,62},{1,63},{2,0},{3,1},{4,2},{5,3},{6,4},{7,5},{8,6},{9,7},{10,... | collective-permute-start | bytes 1179656 | tf_op jit(solution)/shard_map/ppermute | solution.py:29
  124.9 19.3 %collective-permute-start.15 = (bf16[96,2048]{1,0:T(8,128)(2,1)}, bf16[96,2048]{1,0:T(8,128)(2,1)S(1)}, u32[]{:S(2)}, u32[]{:S(2)}) collective-permute-start(bf16[96,2048]{1,0:T(8,128)(2,1)} %get-tuple-element.42), channel_id=1, source_target_pairs={{0,2},{1,3},{2,4},{3,5},{4,6},{5,7},{6,8},{7,9},{8,10},{9,11},{10,... | collective-permute-start | bytes 1179656 | tf_op jit(solution)/shard_map/ppermute | solution.py:29
  128.0 12.6 %collective-permute-start.16 = (bf16[48,2048]{1,0:T(8,128)(2,1)}, bf16[48,2048]{1,0:T(8,128)(2,1)S(1)}, u32[]{:S(2)}, u32[]{:S(2)}) collective-permute-start(bf16[48,2048]{1,0:T(8,128)(2,1)} %get-tuple-element.43), channel_id=1, source_target_pairs={{0,60},{1,61},{2,62},{3,63},{4,0},{5,1},{6,2},{7,3},{8,4},{9,5},{1... | collective-permute-start | bytes 589832 | tf_op jit(solution)/shard_map/ppermute | solution.py:29
  131.6 12.6 %collective-permute-start.17 = (bf16[48,2048]{1,0:T(8,128)(2,1)}, bf16[48,2048]{1,0:T(8,128)(2,1)S(1)}, u32[]{:S(2)}, u32[]{:S(2)}) collective-permute-start(bf16[48,2048]{1,0:T(8,128)(2,1)} %get-tuple-element.44), channel_id=1, source_target_pairs={{0,4},{1,5},{2,6},{3,7},{4,8},{5,9},{6,10},{7,11},{8,12},{9,13},{1... | collective-permute-start | bytes 589832 | tf_op jit(solution)/shard_map/ppermute | solution.py:29
  145.4 16.7 %collective-permute-start.19 = (bf16[32,2048]{1,0:T(8,128)(2,1)S(1)}, bf16[32,2048]{1,0:T(8,128)(2,1)S(1)}, u32[]{:S(2)}, u32[]{:S(2)}) collective-permute-start(bf16[32,2048]{1,0:T(8,128)(2,1)S(1)} %get-tuple-element.49), channel_id=1, source_target_pairs={{0,56},{1,9},{2,58},{3,11},{4,60},{5,13},{6,62},{7,15},{8,0},{9,17... | collective-permute-start | bytes 393224 | tf_op jit(solution)/shard_map/ppermute | solution.py:29
  148.2 19.7 %collective-permute-start.23 = (bf16[32,2048]{1,0:T(8,128)(2,1)S(1)}, bf16[32,2048]{1,0:T(8,128)(2,1)S(1)}, u32[]{:S(2)}, u32[]{:S(2)}) collective-permute-start(bf16[32,2048]{1,0:T(8,128)(2,1)S(1)} %get-tuple-element.52), channel_id=1, source_target_pairs={{0,56},{1,9},{2,58},{3,11},{4,60},{5,13},{6,62},{7,15},{8,0},{9,17... | collective-permute-start | bytes 393224 | tf_op jit(solution)/shard_map/ppermute | solution.py:29
  155.3 42.3 %collective-permute-start.18 = (f32[32,2048]{1,0:T(8,128)S(1)}, f32[32,2048]{1,0:T(8,128)S(1)}, u32[]{:S(2)}, u32[]{:S(2)}) collective-permute-start(f32[32,2048]{1,0:T(8,128)S(1)} %get-tuple-element.45), channel_id=1, source_target_pairs={{0,64},{1,65},{2,66},{3,67},{4,68},{5,69},{6,70},{7,71},{8,72},{9,... | collective-permute-start | bytes 786440 | tf_op jit(solution)/shard_map/ppermute | solution.py:35
  162.1 17.0 %collective-permute-start.20 = (bf16[32,2048]{1,0:T(8,128)(2,1)S(1)}, bf16[32,2048]{1,0:T(8,128)(2,1)S(1)}, u32[]{:S(2)}, u32[]{:S(2)}) collective-permute-start(bf16[32,2048]{1,0:T(8,128)(2,1)S(1)} %add_convert_fusion.5), channel_id=1, source_target_pairs={{0,56},{1,9},{2,58},{3,11},{4,60},{5,13},{6,62},{7,15},{8,0},{9,17... | collective-permute-start | bytes 393224 | tf_op jit(solution)/shard_map/ppermute | solution.py:29
  168.0 13.7 %collective-permute-start.24 = (bf16[32,2048]{1,0:T(8,128)(2,1)S(1)}, bf16[32,2048]{1,0:T(8,128)(2,1)S(1)}, u32[]{:S(2)}, u32[]{:S(2)}) collective-permute-start(bf16[32,2048]{1,0:T(8,128)(2,1)S(1)} %add_convert_fusion.2), channel_id=1, source_target_pairs={{0,56},{1,9},{2,58},{3,11},{4,60},{5,13},{6,62},{7,15},{8,0},{9,17... | collective-permute-start | bytes 393224 | tf_op jit(solution)/shard_map/ppermute | solution.py:29
  179.2 13.5 %collective-permute-start.21 = (bf16[32,2048]{1,0:T(8,128)(2,1)S(1)}, bf16[32,2048]{1,0:T(8,128)(2,1)S(1)}, u32[]{:S(2)}, u32[]{:S(2)}) collective-permute-start(bf16[32,2048]{1,0:T(8,128)(2,1)S(1)} %add_convert_fusion.4), channel_id=1, source_target_pairs={{0,56},{1,9},{2,58},{3,11},{4,60},{5,13},{6,62},{7,15},{8,0},{9,17... | collective-permute-start | bytes 393224 | tf_op jit(solution)/shard_map/ppermute | solution.py:29
  181.7 15.9 %collective-permute-start.25 = (bf16[32,2048]{1,0:T(8,128)(2,1)S(1)}, bf16[32,2048]{1,0:T(8,128)(2,1)S(1)}, u32[]{:S(2)}, u32[]{:S(2)}) collective-permute-start(bf16[32,2048]{1,0:T(8,128)(2,1)S(1)} %add_convert_fusion.1), channel_id=1, source_target_pairs={{0,121},{1,72},{2,123},{3,74},{4,125},{5,76},{6,127},{7,78},{8,65}... | collective-permute-start | bytes 393224 | tf_op jit(solution)/shard_map/ppermute | solution.py:35
  192.7 13.8 %collective-permute-start.22 = (bf16[32,2048]{1,0:T(8,128)(2,1)S(1)}, bf16[32,2048]{1,0:T(8,128)(2,1)S(1)}, u32[]{:S(2)}, u32[]{:S(2)}) collective-permute-start(bf16[32,2048]{1,0:T(8,128)(2,1)S(1)} %add_convert_fusion.3), channel_id=1, source_target_pairs={{0,120},{1,73},{2,122},{3,75},{4,124},{5,77},{6,126},{7,79},{8,64}... | collective-permute-start | bytes 393224 | tf_op jit(solution)/shard_map/ppermute | solution.py:35
  (2 other events, 1.4 us)

commit v6 on v5

--- a/solution.py
+++ b/solution.py
@@ -192,7 +192,7 @@
             pltpu.VMEM((rows, width), jnp.float32),
             pltpu.SemaphoreType.DMA((2, UP + TILES)),
         ],
-        compiler_params=pltpu.CompilerParams(vmem_limit_bytes=56 * 2**20),
+        compiler_params=pltpu.CompilerParams(vmem_limit_bytes=50 * 2**20),
         cost_estimate=pl.CostEstimate(
             flops=2 * 2 * rows * 3 * width * hid,
             bytes_accessed=2 * 3 * 2 * width * hid,
@@ -255,7 +255,6 @@
     low2 = send(low2, -2, -2)
     weights = (gate_up, down, other_gu, other_d)
     [here] = experts(place, [here], *weights)
-    here, up1, low1, up2, low2 = lax.optimization_barrier((here, up1, low1, up2, low2))
     up1, low1, up2, low2 = experts(place, [up1, low1, up2, low2], *weights)
     up1 = send(up1, -1, -1)
     low1 = send(low1, 1, 1)

time: 208 us -> 203 us (0.976)
  the two profiles are of different devices: /device:TPU:6 before, /device:TPU:128 now
where the time goes in v6:
time: 203 us
  starting transfers between devices  122 us (60%)
  waiting for transfers between devices  61.1 us (30%)
  Pallas kernels  17.6 us (9%)
    ppermute x23, starting transfers between devices, send(): return lax.ppermute(value, 'expert', [(i, place(i)) for i in range(count)])  112 us
    ppermute x23, waiting for transfers between devices, send(): return lax.ppermute(value, 'expert', [(i, place(i)) for i in range(count)])  48.1 us
    ppermute x3, waiting for transfers between devices, send(): return lax.ppermute(value, ('section', 'expert'), pairs)  13.1 us
    pallas_call x2, Pallas kernels, experts(): pl.pallas_call(functools.partial(expert_kernel, len(pieces)), in_specs=[p...  13 us
    ppermute x3, starting transfers between devices, send(): return lax.ppermute(value, ('section', 'expert'), pairs)  9.34 us
  transfers between devices with their start and end apart: 26, of which 12 were waited for; matrix products, arithmetic and copies ran while one was open for 0% of the time, Pallas kernels for 5%

profile of v6, /device:TPU:128, one launch (start us, length us, event | category | flops | bytes accessed | tf_op | source)
XLA Modules:
  0.0 202.6 jit_solution(13671026682580449418)
XLA Ops:
  1.9 2.4 %collective-permute-start.9 = (bf16[1,768,2048]{2,1,0:T(8,128)(2,1)}, bf16[1,768,2048]{2,1,0:T(8,128)(2,1)}, u32[]{:S(2)}, u32[]{:S(2)}) collective-permute-start(bf16[1,768,2048]{2,1,0:T(8,128)(2,1)} %refs_5_.1), channel_id=1, source_target_pairs={{0,1},{1,0},{2,3},{3,2},{4,5},{5,4},{6,7},{7,6},{8,9},{9,8},{10,11... | collective-permute-start | bytes 9437192 | tf_op jit(solution)/shard_map/ppermute | solution.py:29
  8.0 9.1 %collective-permute-start = (bf16[32,2176]{1,0:T(8,128)(2,1)}, bf16[32,2176]{1,0:T(8,128)(2,1)S(1)}, u32[]{:S(2)}, u32[]{:S(2)}) collective-permute-start(bf16[32,2176]{1,0:T(8,128)(2,1)} %prepare.1.refs_0_), channel_id=1, source_target_pairs={{0,8},{1,57},{2,10},{3,59},{4,12},{5,61},{6,14},{7,63},{8,16},{9,1... | collective-permute-start | bytes 417800 | tf_op jit(solution)/shard_map/ppermute | solution.py:29
  17.1 9.1 %collective-permute-start.5 = (bf16[32,2176]{1,0:T(8,128)(2,1)S(1)}, bf16[32,2176]{1,0:T(8,128)(2,1)S(1)}, u32[]{:S(2)}, u32[]{:S(2)}) collective-permute-start(bf16[32,2176]{1,0:T(8,128)(2,1)S(1)} %collective-permute-done.4), channel_id=1, source_target_pairs={{0,8},{1,57},{2,10},{3,59},{4,12},{5,61},{6,14},{7,63},{8,16},{9,1... | collective-permute-start | bytes 417800 | tf_op jit(solution)/shard_map/ppermute | solution.py:29
  26.2 9.1 %collective-permute-start.1 = (bf16[32,2176]{1,0:T(8,128)(2,1)S(1)}, bf16[32,2176]{1,0:T(8,128)(2,1)S(1)}, u32[]{:S(2)}, u32[]{:S(2)}) collective-permute-start(bf16[32,2176]{1,0:T(8,128)(2,1)S(1)} %collective-permute-done.refs_1_), channel_id=1, source_target_pairs={{0,8},{1,57},{2,10},{3,59},{4,12},{5,61},{6,14},{7,63},{8,16},{9,1... | collective-permute-start | bytes 417800 | tf_op jit(solution)/shard_map/ppermute | solution.py:29
  35.4 6.6 %collective-permute-start.6 = (bf16[32,2176]{1,0:T(8,128)(2,1)S(1)}, bf16[32,2176]{1,0:T(8,128)(2,1)S(1)}, u32[]{:S(2)}, u32[]{:S(2)}) collective-permute-start(bf16[32,2176]{1,0:T(8,128)(2,1)S(1)} %collective-permute-done.5.refs_5_), channel_id=1, source_target_pairs={{0,8},{1,57},{2,10},{3,59},{4,12},{5,61},{6,14},{7,63},{8,16},{9,1... | collective-permute-start | bytes 417800 | tf_op jit(solution)/shard_map/ppermute | solution.py:29
  42.0 8.5 %collective-permute-start.2 = (bf16[32,2176]{1,0:T(8,128)(2,1)S(1)}, bf16[32,2176]{1,0:T(8,128)(2,1)S(1)}, u32[]{:S(2)}, u32[]{:S(2)}) collective-permute-start(bf16[32,2176]{1,0:T(8,128)(2,1)S(1)} %collective-permute-done.1.refs_2_), channel_id=1, source_target_pairs={{0,8},{1,57},{2,10},{3,59},{4,12},{5,61},{6,14},{7,63},{8,16},{9,1... | collective-permute-start | bytes 417800 | tf_op jit(solution)/shard_map/ppermute | solution.py:29
  50.5 4.5 %collective-permute-done.6.refs_6_ = bf16[32,2176]{1,0:T(8,128)(2,1)S(1)} collective-permute-done((bf16[32,2176]{1,0:T(8,128)(2,1)S(1)}, bf16[32,2176]{1,0:T(8,128)(2,1)S(1)}, u32[]{:S(2)}, u32[]{:S(2)}) %collective-permute-start.6) | collective-permute-done | bytes 139296 | tf_op jit(solution)/shard_map/ppermute | solution.py:29
  55.0 2.2 %collective-permute-start.7 = (bf16[32,2176]{1,0:T(8,128)(2,1)S(1)}, bf16[32,2176]{1,0:T(8,128)(2,1)S(1)}, u32[]{:S(2)}, u32[]{:S(2)}) collective-permute-start(bf16[32,2176]{1,0:T(8,128)(2,1)S(1)} %collective-permute-done.6.refs_6_), channel_id=1, source_target_pairs={{0,8},{1,57},{2,10},{3,59},{4,12},{5,61},{6,14},{7,63},{8,16},{9,1... | collective-permute-start | bytes 417800 | tf_op jit(solution)/shard_map/ppermute | solution.py:29
  57.3 7.7 %collective-permute-start.3 = (bf16[32,2176]{1,0:T(8,128)(2,1)S(1)}, bf16[32,2176]{1,0:T(8,128)(2,1)S(1)}, u32[]{:S(2)}, u32[]{:S(2)}) collective-permute-start(bf16[32,2176]{1,0:T(8,128)(2,1)S(1)} %collective-permute-done.2.refs_3_), channel_id=1, source_target_pairs={{0,8},{1,57},{2,10},{3,59},{4,12},{5,61},{6,14},{7,63},{8,16},{9,1... | collective-permute-start | bytes 417800 | tf_op jit(solution)/shard_map/ppermute | solution.py:29
  65.0 5.6 %collective-permute-done.7.refs_7_ = bf16[32,2176]{1,0:T(8,128)(2,1)S(1)} collective-permute-done((bf16[32,2176]{1,0:T(8,128)(2,1)S(1)}, bf16[32,2176]{1,0:T(8,128)(2,1)S(1)}, u32[]{:S(2)}, u32[]{:S(2)}) %collective-permute-start.7) | collective-permute-done | bytes 139296 | tf_op jit(solution)/shard_map/ppermute | solution.py:29
  74.7 7.1 %collective-permute-start.12 = (bf16[48,2048]{1,0:T(8,128)(2,1)S(1)}, bf16[48,2048]{1,0:T(8,128)(2,1)S(1)}, u32[]{:S(2)}, u32[]{:S(2)}) collective-permute-start(bf16[48,2048]{1,0:T(8,128)(2,1)S(1)} %get-tuple-element.29), channel_id=1, source_target_pairs={{0,4},{1,5},{2,6},{3,7},{4,8},{5,9},{6,10},{7,11},{8,12},{9,13},{1... | collective-permute-start | bytes 589832 | tf_op jit(solution)/shard_map/ppermute | solution.py:29
  81.9 4.8 %collective-permute-start.10 = (bf16[96,2048]{1,0:T(8,128)(2,1)S(1)}, bf16[96,2048]{1,0:T(8,128)(2,1)S(1)}, u32[]{:S(2)}, u32[]{:S(2)}) collective-permute-start(bf16[96,2048]{1,0:T(8,128)(2,1)S(1)} %get-tuple-element.27), channel_id=1, source_target_pairs={{0,2},{1,3},{2,4},{3,5},{4,6},{5,7},{6,8},{7,9},{8,10},{9,11},{10,... | collective-permute-start | bytes 1179656 | tf_op jit(solution)/shard_map/ppermute | solution.py:29
  86.7 2.3 %collective-permute-start.11 = (bf16[96,2048]{1,0:T(8,128)(2,1)S(1)}, bf16[96,2048]{1,0:T(8,128)(2,1)S(1)}, u32[]{:S(2)}, u32[]{:S(2)}) collective-permute-start(bf16[96,2048]{1,0:T(8,128)(2,1)S(1)} %get-tuple-element.28), channel_id=1, source_target_pairs={{0,62},{1,63},{2,0},{3,1},{4,2},{5,3},{6,4},{7,5},{8,6},{9,7},{10,... | collective-permute-start | bytes 1179656 | tf_op jit(solution)/shard_map/ppermute | solution.py:29
  88.9 2.1 %collective-permute-done.12.refs_2_ = bf16[48,2048]{1,0:T(8,128)(2,1)S(1)} collective-permute-done((bf16[48,2048]{1,0:T(8,128)(2,1)S(1)}, bf16[48,2048]{1,0:T(8,128)(2,1)S(1)}, u32[]{:S(2)}, u32[]{:S(2)}) %collective-permute-start.12) | collective-permute-done | bytes 196640 | tf_op jit(solution)/shard_map/ppermute | solution.py:29
  91.0 5.7 %collective-permute-start.13 = (bf16[48,2048]{1,0:T(8,128)(2,1)S(1)}, bf16[48,2048]{1,0:T(8,128)(2,1)S(1)}, u32[]{:S(2)}, u32[]{:S(2)}) collective-permute-start(bf16[48,2048]{1,0:T(8,128)(2,1)S(1)} %get-tuple-element.30), channel_id=1, source_target_pairs={{0,60},{1,61},{2,62},{3,63},{4,0},{5,1},{6,2},{7,3},{8,4},{9,5},{1... | collective-permute-start | bytes 589832 | tf_op jit(solution)/shard_map/ppermute | solution.py:29
  96.7 9.6 %collective-permute-done.13.refs_3_ = bf16[48,2048]{1,0:T(8,128)(2,1)S(1)} collective-permute-done((bf16[48,2048]{1,0:T(8,128)(2,1)S(1)}, bf16[48,2048]{1,0:T(8,128)(2,1)S(1)}, u32[]{:S(2)}, u32[]{:S(2)}) %collective-permute-start.13) | collective-permute-done | bytes 196640 | tf_op jit(solution)/shard_map/ppermute | solution.py:29
  106.3 6.9 %experts.3 = (bf16[96,2048]{1,0:T(8,128)(2,1)S(1)}, bf16[96,2048]{1,0:T(8,128)(2,1)S(1)}, bf16[48,2048]{1,0:T(8,128)(2,1)S(1)}, bf16[48,2048]{1,0:T(8,128)(2,1)S(1)}) custom-call(s32[1]{0:T(128)} %bitcast.place, bf16[96,2048]{1,0:T(8,128)(2,1)S(1)} %collective-permute-done.10.refs_0_, bf16[96,2048]{1,0:T(8,128)(2,1)S(1)} %collective-permute-done.11.refs_1_, ...), custom_call_target="tpu_custom_call" | custom-call | flops 2717908992 | bytes 18874368 | tf_op jit(solution)/shard_map/experts/pallas_call | solution.py:183
  113.2 1.9 collective-permute-start.14
  115.2 3.9 %collective-permute-start.15 = (bf16[96,2048]{1,0:T(8,128)(2,1)S(1)}, bf16[96,2048]{1,0:T(8,128)(2,1)S(1)}, u32[]{:S(2)}, u32[]{:S(2)}) collective-permute-start(bf16[96,2048]{1,0:T(8,128)(2,1)S(1)} %get-tuple-element.32), channel_id=1, source_target_pairs={{0,2},{1,3},{2,4},{3,5},{4,6},{5,7},{6,8},{7,9},{8,10},{9,11},{10,... | collective-permute-start | bytes 1179656 | tf_op jit(solution)/shard_map/ppermute | solution.py:29
  119.1 2.3 %collective-permute-start.16 = (bf16[48,2048]{1,0:T(8,128)(2,1)S(1)}, bf16[48,2048]{1,0:T(8,128)(2,1)S(1)}, u32[]{:S(2)}, u32[]{:S(2)}) collective-permute-start(bf16[48,2048]{1,0:T(8,128)(2,1)S(1)} %get-tuple-element.33), channel_id=1, source_target_pairs={{0,60},{1,61},{2,62},{3,63},{4,0},{5,1},{6,2},{7,3},{8,4},{9,5},{1... | collective-permute-start | bytes 589832 | tf_op jit(solution)/shard_map/ppermute | solution.py:29
  121.5 4.4 %collective-permute-start.17 = (bf16[48,2048]{1,0:T(8,128)(2,1)S(1)}, bf16[48,2048]{1,0:T(8,128)(2,1)S(1)}, u32[]{:S(2)}, u32[]{:S(2)}) collective-permute-start(bf16[48,2048]{1,0:T(8,128)(2,1)S(1)} %get-tuple-element.34), channel_id=1, source_target_pairs={{0,4},{1,5},{2,6},{3,7},{4,8},{5,9},{6,10},{7,11},{8,12},{9,13},{1... | collective-permute-start | bytes 589832 | tf_op jit(solution)/shard_map/ppermute | solution.py:29
  125.9 6.1 %experts.2.refs_0_ = bf16[96,2048]{1,0:T(8,128)(2,1)S(1)} custom-call(s32[1]{0:T(128)} %bitcast.place, bf16[96,2048]{1,0:T(8,128)(2,1)S(1)} %get-tuple-element.26.refs_0_, bf16[1,2048,1536]{2,1,0:T(8,128)(2,1)} %refs_4_.1, bf16[1,768,2048]{2,1,0:T(8,128)(2,1)S(1)} %copy-done, bf16[1,2048,1536]{2,1,0:T(8,128)(2,1)} %collective-permute-done.8.refs_3_.refs_6_, ...), custom_call_target="tpu_custom_call" | custom-call | flops 905969664 | bytes 18874368 | tf_op jit(solution)/shard_map/experts/pallas_call | solution.py:183
  134.2 6.0 %collective-permute-start.19 = (bf16[32,2048]{1,0:T(8,128)(2,1)S(1)}, bf16[32,2048]{1,0:T(8,128)(2,1)S(1)}, u32[]{:S(2)}, u32[]{:S(2)}) collective-permute-start(bf16[32,2048]{1,0:T(8,128)(2,1)S(1)} %get-tuple-element.39), channel_id=1, source_target_pairs={{0,56},{1,9},{2,58},{3,11},{4,60},{5,13},{6,62},{7,15},{8,0},{9,17... | collective-permute-start | bytes 393224 | tf_op jit(solution)/shard_map/ppermute | solution.py:29
  140.2 5.4 %collective-permute-start.23 = (bf16[32,2048]{1,0:T(8,128)(2,1)S(1)}, bf16[32,2048]{1,0:T(8,128)(2,1)S(1)}, u32[]{:S(2)}, u32[]{:S(2)}) collective-permute-start(bf16[32,2048]{1,0:T(8,128)(2,1)S(1)} %get-tuple-element.42), channel_id=1, source_target_pairs={{0,56},{1,9},{2,58},{3,11},{4,60},{5,13},{6,62},{7,15},{8,0},{9,17... | collective-permute-start | bytes 393224 | tf_op jit(solution)/shard_map/ppermute | solution.py:29
  145.6 5.5 %collective-permute-start.18 = (f32[32,2048]{1,0:T(8,128)S(1)}, f32[32,2048]{1,0:T(8,128)S(1)}, u32[]{:S(2)}, u32[]{:S(2)}) collective-permute-start(f32[32,2048]{1,0:T(8,128)S(1)} %get-tuple-element.35), channel_id=1, source_target_pairs={{0,64},{1,65},{2,66},{3,67},{4,68},{5,69},{6,70},{7,71},{8,72},{9,... | collective-permute-start | bytes 786440 | tf_op jit(solution)/shard_map/ppermute | solution.py:35
  151.1 5.0 %collective-permute-done.19 = bf16[32,2048]{1,0:T(8,128)(2,1)S(1)} collective-permute-done((bf16[32,2048]{1,0:T(8,128)(2,1)S(1)}, bf16[32,2048]{1,0:T(8,128)(2,1)S(1)}, u32[]{:S(2)}, u32[]{:S(2)}) %collective-permute-start.19) | collective-permute-done | bytes 131104 | tf_op jit(solution)/shard_map/ppermute | solution.py:29
  158.1 3.1 %collective-permute-start.24 = (bf16[32,2048]{1,0:T(8,128)(2,1)S(1)}, bf16[32,2048]{1,0:T(8,128)(2,1)S(1)}, u32[]{:S(2)}, u32[]{:S(2)}) collective-permute-start(bf16[32,2048]{1,0:T(8,128)(2,1)S(1)} %add_convert_fusion.2), channel_id=1, source_target_pairs={{0,56},{1,9},{2,58},{3,11},{4,60},{5,13},{6,62},{7,15},{8,0},{9,17... | collective-permute-start | bytes 393224 | tf_op jit(solution)/shard_map/ppermute | solution.py:29
  161.2 8.5 %collective-permute-done.20 = bf16[32,2048]{1,0:T(8,128)(2,1)S(1)} collective-permute-done((bf16[32,2048]{1,0:T(8,128)(2,1)S(1)}, bf16[32,2048]{1,0:T(8,128)(2,1)S(1)}, u32[]{:S(2)}, u32[]{:S(2)}) %collective-permute-start.20) | collective-permute-done | bytes 131104 | tf_op jit(solution)/shard_map/ppermute | solution.py:29
  169.8 5.0 %collective-permute-start.21 = (bf16[32,2048]{1,0:T(8,128)(2,1)S(1)}, bf16[32,2048]{1,0:T(8,128)(2,1)S(1)}, u32[]{:S(2)}, u32[]{:S(2)}) collective-permute-start(bf16[32,2048]{1,0:T(8,128)(2,1)S(1)} %add_convert_fusion.4), channel_id=1, source_target_pairs={{0,56},{1,9},{2,58},{3,11},{4,60},{5,13},{6,62},{7,15},{8,0},{9,17... | collective-permute-start | bytes 393224 | tf_op jit(solution)/shard_map/ppermute | solution.py:29
  176.8 10.2 %collective-permute-done.21 = bf16[32,2048]{1,0:T(8,128)(2,1)S(1)} collective-permute-done((bf16[32,2048]{1,0:T(8,128)(2,1)S(1)}, bf16[32,2048]{1,0:T(8,128)(2,1)S(1)}, u32[]{:S(2)}, u32[]{:S(2)}) %collective-permute-start.21) | collective-permute-done | bytes 131104 | tf_op jit(solution)/shard_map/ppermute | solution.py:29
  188.9 3.5 %collective-permute-done.25 = bf16[32,2048]{1,0:T(8,128)(2,1)S(1)} collective-permute-done((bf16[32,2048]{1,0:T(8,128)(2,1)S(1)}, bf16[32,2048]{1,0:T(8,128)(2,1)S(1)}, u32[]{:S(2)}, u32[]{:S(2)}) %collective-permute-start.25) | collective-permute-done | bytes 131104 | tf_op jit(solution)/shard_map/ppermute | solution.py:35
  192.4 9.6 %collective-permute-done.22 = bf16[32,2048]{1,0:T(8,128)(2,1)S(1)} collective-permute-done((bf16[32,2048]{1,0:T(8,128)(2,1)S(1)}, bf16[32,2048]{1,0:T(8,128)(2,1)S(1)}, u32[]{:S(2)}, u32[]{:S(2)}) %collective-permute-start.22) | collective-permute-done | bytes 131104 | tf_op jit(solution)/shard_map/ppermute | solution.py:35
  (37 shorter events, 18.6 us)
Async XLA Ops:
  0.0 106.3 %collective-permute-start.8 = (bf16[1,2048,1536]{2,1,0:T(8,128)(2,1)}, bf16[1,2048,1536]{2,1,0:T(8,128)(2,1)}, u32[]{:S(2)}, u32[]{:S(2)}) collective-permute-start(bf16[1,2048,1536]{2,1,0:T(8,128)(2,1)} %refs_4_.1), channel_id=1, source_target_pairs={{0,1},{1,0},{2,3},{3,2},{4,5},{5,4},{6,7},{7,6},{8,9},{9,8},{10,11... | collective-permute-start | bytes 18874376 | tf_op jit(solution)/shard_map/ppermute | solution.py:29
  1.9 104.4 %collective-permute-start.9 = (bf16[1,768,2048]{2,1,0:T(8,128)(2,1)}, bf16[1,768,2048]{2,1,0:T(8,128)(2,1)}, u32[]{:S(2)}, u32[]{:S(2)}) collective-permute-start(bf16[1,768,2048]{2,1,0:T(8,128)(2,1)} %refs_5_.1), channel_id=1, source_target_pairs={{0,1},{1,0},{2,3},{3,2},{4,5},{5,4},{6,7},{7,6},{8,9},{9,8},{10,11... | collective-permute-start | bytes 9437192 | tf_op jit(solution)/shard_map/ppermute | solution.py:29
  6.1 11.0 %collective-permute-start.4 = (bf16[32,2176]{1,0:T(8,128)(2,1)}, bf16[32,2176]{1,0:T(8,128)(2,1)S(1)}, u32[]{:S(2)}, u32[]{:S(2)}) collective-permute-start(bf16[32,2176]{1,0:T(8,128)(2,1)} %prepare.1.refs_0_), channel_id=1, source_target_pairs={{0,1},{1,0},{2,3},{3,2},{4,5},{5,4},{6,7},{7,6},{8,9},{9,8},{10,11... | collective-permute-start | bytes 417800 | tf_op jit(solution)/shard_map/ppermute | solution.py:29
  8.0 18.2 %collective-permute-start = (bf16[32,2176]{1,0:T(8,128)(2,1)}, bf16[32,2176]{1,0:T(8,128)(2,1)S(1)}, u32[]{:S(2)}, u32[]{:S(2)}) collective-permute-start(bf16[32,2176]{1,0:T(8,128)(2,1)} %prepare.1.refs_0_), channel_id=1, source_target_pairs={{0,8},{1,57},{2,10},{3,59},{4,12},{5,61},{6,14},{7,63},{8,16},{9,1... | collective-permute-start | bytes 417800 | tf_op jit(solution)/shard_map/ppermute | solution.py:29
  17.1 18.2 %collective-permute-start.5 = (bf16[32,2176]{1,0:T(8,128)(2,1)S(1)}, bf16[32,2176]{1,0:T(8,128)(2,1)S(1)}, u32[]{:S(2)}, u32[]{:S(2)}) collective-permute-start(bf16[32,2176]{1,0:T(8,128)(2,1)S(1)} %collective-permute-done.4), channel_id=1, source_target_pairs={{0,8},{1,57},{2,10},{3,59},{4,12},{5,61},{6,14},{7,63},{8,16},{9,1... | collective-permute-start | bytes 417800 | tf_op jit(solution)/shard_map/ppermute | solution.py:29
  26.2 15.7 %collective-permute-start.1 = (bf16[32,2176]{1,0:T(8,128)(2,1)S(1)}, bf16[32,2176]{1,0:T(8,128)(2,1)S(1)}, u32[]{:S(2)}, u32[]{:S(2)}) collective-permute-start(bf16[32,2176]{1,0:T(8,128)(2,1)S(1)} %collective-permute-done.refs_1_), channel_id=1, source_target_pairs={{0,8},{1,57},{2,10},{3,59},{4,12},{5,61},{6,14},{7,63},{8,16},{9,1... | collective-permute-start | bytes 417800 | tf_op jit(solution)/shard_map/ppermute | solution.py:29
  35.4 19.7 %collective-permute-start.6 = (bf16[32,2176]{1,0:T(8,128)(2,1)S(1)}, bf16[32,2176]{1,0:T(8,128)(2,1)S(1)}, u32[]{:S(2)}, u32[]{:S(2)}) collective-permute-start(bf16[32,2176]{1,0:T(8,128)(2,1)S(1)} %collective-permute-done.5.refs_5_), channel_id=1, source_target_pairs={{0,8},{1,57},{2,10},{3,59},{4,12},{5,61},{6,14},{7,63},{8,16},{9,1... | collective-permute-start | bytes 417800 | tf_op jit(solution)/shard_map/ppermute | solution.py:29
  42.0 15.3 %collective-permute-start.2 = (bf16[32,2176]{1,0:T(8,128)(2,1)S(1)}, bf16[32,2176]{1,0:T(8,128)(2,1)S(1)}, u32[]{:S(2)}, u32[]{:S(2)}) collective-permute-start(bf16[32,2176]{1,0:T(8,128)(2,1)S(1)} %collective-permute-done.1.refs_2_), channel_id=1, source_target_pairs={{0,8},{1,57},{2,10},{3,59},{4,12},{5,61},{6,14},{7,63},{8,16},{9,1... | collective-permute-start | bytes 417800 | tf_op jit(solution)/shard_map/ppermute | solution.py:29
  55.0 15.6 %collective-permute-start.7 = (bf16[32,2176]{1,0:T(8,128)(2,1)S(1)}, bf16[32,2176]{1,0:T(8,128)(2,1)S(1)}, u32[]{:S(2)}, u32[]{:S(2)}) collective-permute-start(bf16[32,2176]{1,0:T(8,128)(2,1)S(1)} %collective-permute-done.6.refs_6_), channel_id=1, source_target_pairs={{0,8},{1,57},{2,10},{3,59},{4,12},{5,61},{6,14},{7,63},{8,16},{9,1... | collective-permute-start | bytes 417800 | tf_op jit(solution)/shard_map/ppermute | solution.py:29
  57.3 14.9 %collective-permute-start.3 = (bf16[32,2176]{1,0:T(8,128)(2,1)S(1)}, bf16[32,2176]{1,0:T(8,128)(2,1)S(1)}, u32[]{:S(2)}, u32[]{:S(2)}) collective-permute-start(bf16[32,2176]{1,0:T(8,128)(2,1)S(1)} %collective-permute-done.2.refs_3_), channel_id=1, source_target_pairs={{0,8},{1,57},{2,10},{3,59},{4,12},{5,61},{6,14},{7,63},{8,16},{9,1... | collective-permute-start | bytes 417800 | tf_op jit(solution)/shard_map/ppermute | solution.py:29
  72.2 0.9 copy-start.1
  74.7 16.3 %collective-permute-start.12 = (bf16[48,2048]{1,0:T(8,128)(2,1)S(1)}, bf16[48,2048]{1,0:T(8,128)(2,1)S(1)}, u32[]{:S(2)}, u32[]{:S(2)}) collective-permute-start(bf16[48,2048]{1,0:T(8,128)(2,1)S(1)} %get-tuple-element.29), channel_id=1, source_target_pairs={{0,4},{1,5},{2,6},{3,7},{4,8},{5,9},{6,10},{7,11},{8,12},{9,13},{1... | collective-permute-start | bytes 589832 | tf_op jit(solution)/shard_map/ppermute | solution.py:29
  81.9 24.5 %collective-permute-start.10 = (bf16[96,2048]{1,0:T(8,128)(2,1)S(1)}, bf16[96,2048]{1,0:T(8,128)(2,1)S(1)}, u32[]{:S(2)}, u32[]{:S(2)}) collective-permute-start(bf16[96,2048]{1,0:T(8,128)(2,1)S(1)} %get-tuple-element.27), channel_id=1, source_target_pairs={{0,2},{1,3},{2,4},{3,5},{4,6},{5,7},{6,8},{7,9},{8,10},{9,11},{10,... | collective-permute-start | bytes 1179656 | tf_op jit(solution)/shard_map/ppermute | solution.py:29
  86.7 19.7 %collective-permute-start.11 = (bf16[96,2048]{1,0:T(8,128)(2,1)S(1)}, bf16[96,2048]{1,0:T(8,128)(2,1)S(1)}, u32[]{:S(2)}, u32[]{:S(2)}) collective-permute-start(bf16[96,2048]{1,0:T(8,128)(2,1)S(1)} %get-tuple-element.28), channel_id=1, source_target_pairs={{0,62},{1,63},{2,0},{3,1},{4,2},{5,3},{6,4},{7,5},{8,6},{9,7},{10,... | collective-permute-start | bytes 1179656 | tf_op jit(solution)/shard_map/ppermute | solution.py:29
  91.0 34.9 %copy-start = (bf16[1,768,2048]{2,1,0:T(8,128)(2,1)S(1)}, bf16[1,768,2048]{2,1,0:T(8,128)(2,1)}, u32[]{:S(2)}) copy-start(bf16[1,768,2048]{2,1,0:T(8,128)(2,1)} %refs_5_.1) | copy-start | bytes 9437188
  91.0 15.3 %collective-permute-start.13 = (bf16[48,2048]{1,0:T(8,128)(2,1)S(1)}, bf16[48,2048]{1,0:T(8,128)(2,1)S(1)}, u32[]{:S(2)}, u32[]{:S(2)}) collective-permute-start(bf16[48,2048]{1,0:T(8,128)(2,1)S(1)} %get-tuple-element.30), channel_id=1, source_target_pairs={{0,60},{1,61},{2,62},{3,63},{4,0},{5,1},{6,2},{7,3},{8,4},{9,5},{1... | collective-permute-start | bytes 589832 | tf_op jit(solution)/shard_map/ppermute | solution.py:29
  113.2 19.7 %collective-permute-start.14 = (bf16[96,2048]{1,0:T(8,128)(2,1)S(1)}, bf16[96,2048]{1,0:T(8,128)(2,1)S(1)}, u32[]{:S(2)}, u32[]{:S(2)}) collective-permute-start(bf16[96,2048]{1,0:T(8,128)(2,1)S(1)} %get-tuple-element.31), channel_id=1, source_target_pairs={{0,62},{1,63},{2,0},{3,1},{4,2},{5,3},{6,4},{7,5},{8,6},{9,7},{10,... | collective-permute-start | bytes 1179656 | tf_op jit(solution)/shard_map/ppermute | solution.py:29
  115.2 17.8 %collective-permute-start.15 = (bf16[96,2048]{1,0:T(8,128)(2,1)S(1)}, bf16[96,2048]{1,0:T(8,128)(2,1)S(1)}, u32[]{:S(2)}, u32[]{:S(2)}) collective-permute-start(bf16[96,2048]{1,0:T(8,128)(2,1)S(1)} %get-tuple-element.32), channel_id=1, source_target_pairs={{0,2},{1,3},{2,4},{3,5},{4,6},{5,7},{6,8},{7,9},{8,10},{9,11},{10,... | collective-permute-start | bytes 1179656 | tf_op jit(solution)/shard_map/ppermute | solution.py:29
  119.1 13.3 %collective-permute-start.16 = (bf16[48,2048]{1,0:T(8,128)(2,1)S(1)}, bf16[48,2048]{1,0:T(8,128)(2,1)S(1)}, u32[]{:S(2)}, u32[]{:S(2)}) collective-permute-start(bf16[48,2048]{1,0:T(8,128)(2,1)S(1)} %get-tuple-element.33), channel_id=1, source_target_pairs={{0,60},{1,61},{2,62},{3,63},{4,0},{5,1},{6,2},{7,3},{8,4},{9,5},{1... | collective-permute-start | bytes 589832 | tf_op jit(solution)/shard_map/ppermute | solution.py:29
  121.5 11.5 %collective-permute-start.17 = (bf16[48,2048]{1,0:T(8,128)(2,1)S(1)}, bf16[48,2048]{1,0:T(8,128)(2,1)S(1)}, u32[]{:S(2)}, u32[]{:S(2)}) collective-permute-start(bf16[48,2048]{1,0:T(8,128)(2,1)S(1)} %get-tuple-element.34), channel_id=1, source_target_pairs={{0,4},{1,5},{2,6},{3,7},{4,8},{5,9},{6,10},{7,11},{8,12},{9,13},{1... | collective-permute-start | bytes 589832 | tf_op jit(solution)/shard_map/ppermute | solution.py:29
  125.9 7.1 %copy-start.2 = (bf16[1,32,2048]{2,1,0:T(8,128)(2,1)S(1)}, bf16[1,32,2048]{2,1,0:T(8,128)(2,1)}, u32[]{:S(2)}) copy-start(bf16[1,32,2048]{2,1,0:T(8,128)(2,1)} %tokens.3) | copy-start | bytes 393220
  134.2 21.9 %collective-permute-start.19 = (bf16[32,2048]{1,0:T(8,128)(2,1)S(1)}, bf16[32,2048]{1,0:T(8,128)(2,1)S(1)}, u32[]{:S(2)}, u32[]{:S(2)}) collective-permute-start(bf16[32,2048]{1,0:T(8,128)(2,1)S(1)} %get-tuple-element.39), channel_id=1, source_target_pairs={{0,56},{1,9},{2,58},{3,11},{4,60},{5,13},{6,62},{7,15},{8,0},{9,17... | collective-permute-start | bytes 393224 | tf_op jit(solution)/shard_map/ppermute | solution.py:29
  140.2 17.9 %collective-permute-start.23 = (bf16[32,2048]{1,0:T(8,128)(2,1)S(1)}, bf16[32,2048]{1,0:T(8,128)(2,1)S(1)}, u32[]{:S(2)}, u32[]{:S(2)}) collective-permute-start(bf16[32,2048]{1,0:T(8,128)(2,1)S(1)} %get-tuple-element.42), channel_id=1, source_target_pairs={{0,56},{1,9},{2,58},{3,11},{4,60},{5,13},{6,62},{7,15},{8,0},{9,17... | collective-permute-start | bytes 393224 | tf_op jit(solution)/shard_map/ppermute | solution.py:29
  145.6 43.3 %collective-permute-start.18 = (f32[32,2048]{1,0:T(8,128)S(1)}, f32[32,2048]{1,0:T(8,128)S(1)}, u32[]{:S(2)}, u32[]{:S(2)}) collective-permute-start(f32[32,2048]{1,0:T(8,128)S(1)} %get-tuple-element.35), channel_id=1, source_target_pairs={{0,64},{1,65},{2,66},{3,67},{4,68},{5,69},{6,70},{7,71},{8,72},{9,... | collective-permute-start | bytes 786440 | tf_op jit(solution)/shard_map/ppermute | solution.py:35
  156.2 13.6 %collective-permute-start.20 = (bf16[32,2048]{1,0:T(8,128)(2,1)S(1)}, bf16[32,2048]{1,0:T(8,128)(2,1)S(1)}, u32[]{:S(2)}, u32[]{:S(2)}) collective-permute-start(bf16[32,2048]{1,0:T(8,128)(2,1)S(1)} %add_convert_fusion.5), channel_id=1, source_target_pairs={{0,56},{1,9},{2,58},{3,11},{4,60},{5,13},{6,62},{7,15},{8,0},{9,17... | collective-permute-start | bytes 393224 | tf_op jit(solution)/shard_map/ppermute | solution.py:29
  158.1 16.6 %collective-permute-start.24 = (bf16[32,2048]{1,0:T(8,128)(2,1)S(1)}, bf16[32,2048]{1,0:T(8,128)(2,1)S(1)}, u32[]{:S(2)}, u32[]{:S(2)}) collective-permute-start(bf16[32,2048]{1,0:T(8,128)(2,1)S(1)} %add_convert_fusion.2), channel_id=1, source_target_pairs={{0,56},{1,9},{2,58},{3,11},{4,60},{5,13},{6,62},{7,15},{8,0},{9,17... | collective-permute-start | bytes 393224 | tf_op jit(solution)/shard_map/ppermute | solution.py:29
  169.8 17.1 %collective-permute-start.21 = (bf16[32,2048]{1,0:T(8,128)(2,1)S(1)}, bf16[32,2048]{1,0:T(8,128)(2,1)S(1)}, u32[]{:S(2)}, u32[]{:S(2)}) collective-permute-start(bf16[32,2048]{1,0:T(8,128)(2,1)S(1)} %add_convert_fusion.4), channel_id=1, source_target_pairs={{0,56},{1,9},{2,58},{3,11},{4,60},{5,13},{6,62},{7,15},{8,0},{9,17... | collective-permute-start | bytes 393224 | tf_op jit(solution)/shard_map/ppermute | solution.py:29
  174.8 17.5 %collective-permute-start.25 = (bf16[32,2048]{1,0:T(8,128)(2,1)S(1)}, bf16[32,2048]{1,0:T(8,128)(2,1)S(1)}, u32[]{:S(2)}, u32[]{:S(2)}) collective-permute-start(bf16[32,2048]{1,0:T(8,128)(2,1)S(1)} %add_convert_fusion.1), channel_id=1, source_target_pairs={{0,121},{1,72},{2,123},{3,74},{4,125},{5,76},{6,127},{7,78},{8,65}... | collective-permute-start | bytes 393224 | tf_op jit(solution)/shard_map/ppermute | solution.py:35
  187.0 15.0 %collective-permute-start.22 = (bf16[32,2048]{1,0:T(8,128)(2,1)S(1)}, bf16[32,2048]{1,0:T(8,128)(2,1)S(1)}, u32[]{:S(2)}, u32[]{:S(2)}) collective-permute-start(bf16[32,2048]{1,0:T(8,128)(2,1)S(1)} %add_convert_fusion.3), channel_id=1, source_target_pairs={{0,120},{1,73},{2,122},{3,75},{4,124},{5,77},{6,126},{7,79},{8,64}... | collective-permute-start | bytes 393224 | tf_op jit(solution)/shard_map/ppermute | solution.py:35
